TPU v7x, 1024 devices: a whole 4x4x32 slice. The times are simulated.
1024 devices in a mesh: node: 2 (over x_hi), shard: 64 (over z, x_lo), rep: 8 (over y, core).
Axes of the slice: x: 4 (x_hi: 2, x_lo: 2; x = x_hi * 2 + x_lo), y: 4, z: 32, core: 2. Of those that a mesh axis runs over, the one named last changes fastest.
Arguments:
- activations: bfloat16 [262144, 4096], P(('node', 'shard', 'rep')), may hold values from -24 to 24
- weight_codes: bfloat16 [4096, 512], P(('node', 'shard')), may hold values from -127 to 127
- block_scales: bfloat16 [4096, 4], P(('node', 'shard')), may hold values from 9.9658966e-05 to 0.00039863586
- cotangent: bfloat16 [262144, 512], P(('node', 'shard', 'rep')), may hold values from -6 to 6
Outputs:
- projected: bfloat16 [262144, 512], P(('node', 'shard', 'rep'))
- weight_grads: float32 [4096, 512], P(('node', 'shard'))
All inputs are finite; a program needn't handle non-finite values.
Results may differ from a plain program's by a relative error of at most 0.015.
Values may be sent and summed in bfloat16 or wider, within the bound.
No kernel may reach another device: no remote copies, remote signals or barrier semaphores. Data moves between devices by JAX's collectives and lax.ppermute only.
A program may use at most 32 MiB of HBM per device.

v0:
```python
import jax
import jax.numpy as jnp
from jax import lax
from jax.sharding import PartitionSpec as P

BLOCK = 128


def body(activations, weight_codes, block_scales, cotangent):
    tok_rows = activations.shape[0]
    out_cols = weight_codes.shape[1]
    widened = jnp.repeat(block_scales.astype(jnp.float32), BLOCK, axis=1)
    local_weight = (weight_codes.astype(jnp.float32) * widened).astype(jnp.bfloat16)
    summed = jnp.dot(
        activations,
        lax.all_gather(local_weight, ("node", "shard"), axis=0, tiled=True),
        preferred_element_type=jnp.float32,
    )
    projected = summed.astype(jnp.bfloat16)
    device_count = lax.axis_size("node") * lax.axis_size("shard") * lax.axis_size("rep")
    factor = float(tok_rows * device_count) ** (-0.5)
    local = lax.dot_general(
        activations, cotangent, (((0,), (0,)), ((), ())), preferred_element_type=jnp.float32
    )
    partial_grad = (local * factor).astype(jnp.bfloat16)
    halves = lax.psum_scatter(
        partial_grad.astype(jnp.float32).astype(jnp.bfloat16),
        "node",
        scatter_dimension=0,
        tiled=True,
    )
    shard_count = lax.axis_size("shard")
    block_rows = halves.shape[0] // shard_count
    blocks = halves.reshape(shard_count, block_rows, out_cols)
    moved = lax.all_to_all(blocks, "shard", split_axis=0, concat_axis=0, tiled=True)
    owned = jnp.sum(moved.astype(jnp.float32), axis=0)
    weight_grads = lax.psum(owned.astype(jnp.bfloat16), "rep").astype(jnp.float32)
    return (projected, weight_grads)


def solution(mesh):
    placed = (
        P(("node", "shard", "rep"), None),
        P(("node", "shard"), None),
        P(("node", "shard"), None),
        P(("node", "shard", "rep"), None),
    )
    return jax.shard_map(
        body,
        mesh=mesh,
        in_specs=placed,
        out_specs=(P(("node", "shard", "rep"), None), P(("node", "shard"), None)),
        check_vma=False,
    )
```

profile of v0, /device:TPU:1, one launch (start us, length us, event | category | flops | bytes accessed | tf_op | source)
XLA Modules:
  0.0 777.1 jit_solution(2691604824341616364)
XLA Ops:
  8.0 0.0 copy-start
  8.0 0.0 reduce-scatter.2.cloned.1.call-start
  8.1 1.5 copy-done
  9.6 4.2 multiply_convert_fusion
  13.8 0.0 copy-start.2
  13.8 0.0 copy-start.1
  13.8 0.0 reduce-scatter.2.cloned.1.call-update
  13.8 84.7 %reduce-scatter.2.cloned.1.call-done = bf16[2048,512]{1,0:T(8,128)(2,1)} async-done(((bf16[4096,512]{1,0:T(8,128)(2,1)}), bf16[2048,512]{1,0:T(8,128)(2,1)}) %reduce-scatter.2.cloned.1.call-update) | async-done | bytes 2097168 | tf_op jit(solution)/shard_map/reduce_scatter | solution.py:26
  98.5 23.5 %all-to-all-start = ((bf16[64,32,512]{2,1,0:T(8,128)(2,1)}), bf16[64,32,512]{2,1,0:T(8,128)(2,1)}, u32[]{:S(2)}, u32[]{:S(2)}) async-start(bf16[64,32,512]{2,1,0:T(8,128)(2,1)} %bitcast.12), calls=%async_computation.1 | async-start | bytes 4194304 | tf_op jit(solution)/shard_map/all_to_all | solution.py:35
  122.1 0.0 all-gather.2.cloned.1.call-start
  122.1 0.0 copy-done.2
  122.1 0.1 copy.6
  122.2 0.1 broadcast_in_dim.3
  122.3 0.0 copy-done.1
  122.3 0.6 fusion.1
  122.9 0.0 all-gather.2.cloned.1.call-update
  123.0 543.4 %all-gather.2.cloned.1.call-done = bf16[4096,512]{1,0:T(8,128)(2,1)} async-done(((bf16[32,512]{1,0:T(8,128)(2,1)}), bf16[4096,512]{1,0:T(8,128)(2,1)}) %all-gather.2.cloned.1.call-update) | async-done | bytes 4194320 | tf_op jit(solution)/shard_map/all_gather | solution.py:16
  666.4 3.5 fusion
  669.9 0.8 copy.7
  670.7 0.0 all-to-all-done
  670.7 1.9 reduce_sum.12
  672.6 96.4 %psum.7 = bf16[32,512]{1,0:T(8,128)(2,1)S(1)} all-reduce(bf16[32,512]{1,0:T(8,128)(2,1)S(1)} %reduce_sum.12), channel_id=1, replica_groups=mesh['node'=2,'shard'=64,'rep'=8] {'rep'}, use_global_device_ids=true, to_apply=%region_2.0 | all-reduce | flops 16384 | bytes 65536 | tf_op jit(solution)/shard_map/psum | solution.py:37
  769.0 0.6 convert_element_type.31
Async XLA Ops:
  8.0 1.6 copy-start
  8.0 90.5 %reduce-scatter.2.cloned.1.call-start = ((), (), s32[]{:S(2)}) async-start(), calls=%async_computation.3 | async-start | bytes 6291456 | tf_op jit(solution)/shard_map/reduce_scatter | solution.py:26
  13.8 108.3 %copy-start.2 = (bf16[32,4]{0,1:T(4,128)(2,1)S(1)}, bf16[32,4]{0,1:T(4,128)(2,1)}, u32[]{:S(2)}) copy-start(bf16[32,4]{0,1:T(4,128)(2,1)} %param.6) | copy-start | bytes 772
  13.8 108.5 %copy-start.1 = (bf16[32,512]{1,0:T(8,128)(2,1)S(1)}, bf16[32,512]{1,0:T(8,128)(2,1)}, u32[]{:S(2)}) copy-start(bf16[32,512]{1,0:T(8,128)(2,1)} %param.5) | copy-start | bytes 98308
  98.5 572.2 %all-to-all-start = ((bf16[64,32,512]{2,1,0:T(8,128)(2,1)}), bf16[64,32,512]{2,1,0:T(8,128)(2,1)}, u32[]{:S(2)}, u32[]{:S(2)}) async-start(bf16[64,32,512]{2,1,0:T(8,128)(2,1)} %bitcast.12), calls=%async_computation.1 | async-start | bytes 4194304 | tf_op jit(solution)/shard_map/all_to_all | solution.py:35
  122.1 544.3 %all-gather.2.cloned.1.call-start = ((), (), s32[]{:S(2)}) async-start(), calls=%async_computation.2 | async-start | bytes 4227072 | tf_op jit(solution)/shard_map/all_gather | solution.py:16
Sparse Core Ops, SparseCore 0:
  13.9 84.5 reduce-scatter.1
Sparse Core Ops, SparseCore 1:
  125.8 540.6 all-gather.1
where the time goes:
time: 779 us; the launch traced here: 777 us
  waiting for transfers between devices  628 us (81%)
  blocking collectives  96.4 us (12%)
  starting transfers between devices  23.6 us (3%)
  between operations  15.5 us (2%)
    all_gather x1, waiting for transfers between devices, body(): lax.all_gather(local_weight, ('node', 'shard'), axis=0, tiled=True)  543 us
    psum x1, blocking collectives, body(): lax.psum(owned.astype(jnp.bfloat16), 'rep').astype(jnp.float32)  96.4 us
    reduce_scatter x1, waiting for transfers between devices, body(): lax.psum_scatter(partial_grad.astype(jnp.float32).astype(jnp.bfloat16), '...  84.7 us
    all_to_all x1, starting transfers between devices, body(): lax.all_to_all(blocks, 'shard', split_axis=0, concat_axis=0, tiled=True)  23.5 us
  transfers between devices with their start and end apart: 3, of which 2 were waited for; matrix products, arithmetic and copies ran while one was open for 1% of the time, Pallas kernels for 0%

commit v1 on v0

v1 whole, which is shorter than its diff:
```python
import jax
import jax.numpy as jnp
from jax import lax
from jax.sharding import Mesh, PartitionSpec as P

BLOCK = 128
ALL = ("xh", "z", "xl", "y", "c")
PLANE = ("xh", "xl", "y")
SWAP = [(0, 1), (1, 0)]


def body(activations, weight_codes, block_scales, cotangent):
    f32, bf16 = jnp.float32, jnp.bfloat16
    c = lax.axis_index("c")
    y = lax.axis_index("y")
    tok, d_in = activations.shape
    own, cols = weight_codes.shape
    half = cols // 2
    rows = own // 4
    n_z = lax.axis_size("z")
    tokens = tok * n_z * 32
    factor = float(tokens) ** (-0.5)

    other_act = lax.ppermute(activations, "c", SWAP)
    my_cot = lax.dynamic_slice(cotangent, (0, c * half), (tok, half))
    send_cot = lax.dynamic_slice(cotangent, (0, (1 - c) * half), (tok, half))
    other_cot = lax.ppermute(send_cot, "c", SWAP)

    dims = (((0,), (0,)), ((), ()))
    acts = jnp.concatenate([activations, other_act], axis=0)
    cots = jnp.concatenate([my_cot, other_cot], axis=0)
    grad = lax.dot_general(acts, cots, dims, preferred_element_type=f32)
    grad = (grad * factor).astype(bf16)
    grad = grad.reshape(2, n_z, 2, 4, rows, half)
    grad = grad.transpose(0, 2, 3, 1, 4, 5).reshape(16, n_z * rows, half)
    moved = lax.all_to_all(grad, PLANE, split_axis=0, concat_axis=0, tiled=True)
    plane = jnp.sum(moved.astype(f32), axis=0).astype(bf16)
    plane = plane.reshape(n_z, rows, half)
    moved_z = lax.all_to_all(plane, "z", split_axis=0, concat_axis=0, tiled=True)
    piece = jnp.sum(moved_z.astype(f32), axis=0)
    pieces = lax.all_gather(piece, ("y", "c"), axis=0, tiled=False)
    pieces = pieces.reshape(4, 2, rows, half)
    weight_grads = pieces.transpose(0, 2, 1, 3).reshape(own, cols)

    blocks = half // BLOCK
    codes = lax.dynamic_slice(weight_codes, (y * rows, c * half), (rows, half))
    scales = lax.dynamic_slice(block_scales, (y * rows, c * blocks), (rows, blocks))
    wide = jnp.repeat(scales.astype(f32), BLOCK, axis=1)
    mine = (codes.astype(f32) * wide).astype(bf16)
    spread = jnp.broadcast_to(mine[None], (n_z, rows, half))
    col = lax.all_to_all(spread, "z", split_axis=0, concat_axis=0, tiled=True)
    spread = jnp.broadcast_to(col.reshape(1, n_z * rows, half), (16, n_z * rows, half))
    whole = lax.all_to_all(spread, PLANE, split_axis=0, concat_axis=0, tiled=True)
    whole = whole.reshape(2, 2, 4, n_z, rows, half)
    weight = whole.transpose(0, 3, 1, 2, 4, 5).reshape(d_in, half)

    proj = jnp.dot(acts, weight, preferred_element_type=f32).astype(bf16)
    got = lax.ppermute(proj[tok:], "c", SWAP)
    kept = proj[:tok]
    left = jnp.where(c == 0, kept, got)
    right = jnp.where(c == 0, got, kept)
    projected = jnp.concatenate([left, right], axis=1)
    return (projected, weight_grads)


def solution(mesh):
    fine = Mesh(mesh.devices.reshape(2, 32, 2, 4, 2), ALL)
    placed = (
        P(ALL, None),
        P(("xh", "z", "xl"), None),
        P(("xh", "z", "xl"), None),
        P(ALL, None),
    )
    return jax.shard_map(
        body,
        mesh=fine,
        in_specs=placed,
        out_specs=(P(ALL, None), P(("xh", "z", "xl"), None)),
        check_vma=False,
    )
```

time: 779 us -> 179 us (0.23)
  waiting for transfers between devices: 628 us -> 59.8 us
  blocking collectives: 96.4 us -> 51.3 us
  starting transfers between devices: 23.6 us -> 50.4 us
  between operations: 15.5 us -> 0.8 us
    all_gather x1 -> x0, waiting for transfers between devices: 543 us -> none  [body(): lax.all_gather(local_weight, ('node', 'shard'), axis=0, tiled=True)]
    psum x1 -> x0, blocking collectives: 96.4 us -> none  [body(): lax.psum(owned.astype(jnp.bfloat16), 'rep').astype(jnp.float32)]
    reduce_scatter x1 -> x0, waiting for transfers between devices: 84.7 us -> none  [body(): lax.psum_scatter(partial_grad.astype(jnp.float32).astype(jnp.bfloat16), '...]
    all_to_all x1 -> x3, waiting for transfers between devices: 0.01 us -> 58.9 us  [the longest x1 23 us: body(): col = lax.all_to_all(spread, 'z', split_axis=0, concat_axis=0, tiled=True)]
    all_to_all x0 -> x1, blocking collectives: none -> 32.6 us  [body(): moved = lax.all_to_all(grad, PLANE, split_axis=0, concat_axis=0, tiled=True)]
    ppermute x0 -> x3, starting transfers between devices: none -> 25.6 us  [the longest x1 16.1 us: body(): other_act = lax.ppermute(activations, 'c', SWAP)]
    all_gather x0 -> x1, blocking collectives: none -> 18.7 us  [body(): pieces = lax.all_gather(piece, ('y', 'c'), axis=0, tiled=False)]
    all_to_all x1 -> x3, starting transfers between devices: 23.5 us -> 24.8 us  [the longest x1 15.8 us: body(): col = lax.all_to_all(spread, 'z', split_axis=0, concat_axis=0, tiled=True)]
  transfers between devices with their start and end apart: 3 -> 6, of which waited for: 2 -> 4; matrix products, arithmetic and copies ran while one was open for 1% -> 6% of each run, Pallas kernels for 0% -> 0%
where the time goes in v1:
time: 179 us
  waiting for transfers between devices  59.8 us (33%)
  blocking collectives  51.3 us (29%)
  starting transfers between devices  50.4 us (28%)
  local copies, waits for them, and re-layouts  9.52 us (5%)
  other arithmetic  4.14 us (2%)
  matrix products  2.6 us (1%)
    all_to_all x1, blocking collectives, body(): moved = lax.all_to_all(grad, PLANE, split_axis=0, concat_axis=0, tiled=True)  32.6 us
    all_to_all x1, waiting for transfers between devices, body(): col = lax.all_to_all(spread, 'z', split_axis=0, concat_axis=0, tiled=True)  23 us
    all_to_all x1, waiting for transfers between devices, body(): lax.all_to_all(spread, PLANE, split_axis=0, concat_axis=0, tiled=True)  22.6 us
    all_gather x1, blocking collectives, body(): pieces = lax.all_gather(piece, ('y', 'c'), axis=0, tiled=False)  18.7 us
    ppermute x1, starting transfers between devices, body(): other_act = lax.ppermute(activations, 'c', SWAP)  16.1 us
    all_to_all x1, starting transfers between devices, body(): col = lax.all_to_all(spread, 'z', split_axis=0, concat_axis=0, tiled=True)  15.8 us
    all_to_all x1, waiting for transfers between devices, body(): lax.all_to_all(plane, 'z', split_axis=0, concat_axis=0, tiled=True)  13.4 us
    ppermute x1, starting transfers between devices, body(): got = lax.ppermute(proj[tok:], 'c', SWAP)  7.33 us
  transfers between devices with their start and end apart: 6, of which 4 were waited for; matrix products, arithmetic and copies ran while one was open for 6% of the time, Pallas kernels for 0%

profile of v1, /device:TPU:1, one launch (start us, length us, event | category | flops | bytes accessed | tf_op | source)
XLA Modules:
  0.0 178.7 jit_solution(10214458360921215687)
XLA Ops:
  0.6 16.1 %collective-permute-start = (bf16[256,4096]{1,0:T(8,128)(2,1)}, bf16[256,4096]{1,0:T(8,128)(2,1)S(1)}, u32[]{:S(2)}, u32[]{:S(2)}) collective-permute-start(bf16[256,4096]{1,0:T(8,128)(2,1)} %param.4), channel_id=1, source_target_pairs={{0,1},{1,0},{2,3},{3,2},{4,5},{5,4},{6,7},{7,6},{8,9},{9,8},{10,11... | collective-permute-start | bytes 6291464 | tf_op jit(solution)/shard_map/ppermute | solution.py:24
  16.7 0.8 dynamic-slice_convert_fusion
  17.5 0.8 fusion.4
  18.2 0.7 broadcast_in_dim.17
  18.9 15.8 %all-to-all-start = ((bf16[32,8,256]{2,1,0:T(8,128)(2,1)}), bf16[32,8,256]{2,1,0:T(8,128)(2,1)S(1)}, u32[]{:S(2)}, u32[]{:S(2)}) async-start(bf16[32,8,256]{2,1,0:T(8,128)(2,1)} %broadcast_in_dim.17), calls=%async_computation | async-start | bytes 262144 | tf_op jit(solution)/shard_map/all_to_all | solution.py:51
  34.7 1.0 constant_dynamic-slice_fusion.1
  35.7 2.2 %collective-permute-start.2 = (bf16[256,256]{1,0:T(8,128)(2,1)S(1)}, bf16[256,256]{1,0:T(8,128)(2,1)S(1)}, u32[]{:S(2)}, u32[]{:S(2)}) collective-permute-start(bf16[256,256]{1,0:T(8,128)(2,1)S(1)} %get-tuple-element.13), channel_id=1, source_target_pairs={{0,1},{1,0},{2,3},{3,2},{4,5},{5,4},{6,7},{7,6},{8,9},{9,8},{10,11... | collective-permute-start | bytes 393224 | tf_op jit(solution)/shard_map/ppermute | solution.py:27
  37.9 1.7 constant_dynamic-update-slice_fusion.1
  39.6 0.0 collective-permute-done
  39.7 0.1 constant_dynamic-update-slice_fusion
  39.8 0.0 copy-start
  39.8 0.0 collective-permute-done.2
  39.8 1.3 fusion
  41.1 0.6 copy-done
  41.7 0.2 copy.13
  41.9 23.0 %all-to-all-done = bf16[32,8,256]{2,1,0:T(8,128)(2,1)S(1)} async-done(((bf16[32,8,256]{2,1,0:T(8,128)(2,1)}), bf16[32,8,256]{2,1,0:T(8,128)(2,1)S(1)}, u32[]{:S(2)}, u32[]{:S(2)}) %all-to-all-start) | async-done | bytes 131104 | tf_op jit(solution)/shard_map/all_to_all | solution.py:51
  64.9 32.6 %all_to_all.20 = bf16[16,256,256]{2,1,0:T(8,128)(2,1)} all-to-all(bf16[16,256,256]{2,1,0:T(8,128)(2,1)S(1)} %bitcast.23), channel_id=1, replica_groups=mesh['xh'=2,'z'=32,'xl'=2,'y'=4,'c'=2] {'xh','xl','y'}, dimensions={0} | all-to-all | bytes 4194304 | tf_op jit(solution)/shard_map/all_to_all | solution.py:36
  97.5 1.5 broadcast_in_dim.19
  99.0 3.7 %all-to-all-start.1 = ((bf16[16,256,256]{2,1,0:T(8,128)(2,1)}), bf16[16,256,256]{2,1,0:T(8,128)(2,1)S(1)}, u32[]{:S(2)}, u32[]{:S(2)}) async-start(bf16[16,256,256]{2,1,0:T(8,128)(2,1)} %broadcast_in_dim.19), calls=%async_computation.1 | async-start | bytes 4194304 | tf_op jit(solution)/shard_map/all_to_all | solution.py:53
  102.8 2.5 %reduce_sum.21 = bf16[256,256]{1,0:T(8,128)(2,1)} reduce(bf16[16,256,256]{2,1,0:T(8,128)(2,1)} %all_to_all.20, bf16[]{:T(256)} %constant.28.clone.1), dimensions={0}, to_apply=%region_0.0 | reduce | flops 983040 | bytes 2228226 | tf_op jit(solution)/shard_map/reduce_sum | solution.py:37
  105.3 22.6 %all-to-all-done.1 = bf16[16,256,256]{2,1,0:T(8,128)(2,1)S(1)} async-done(((bf16[16,256,256]{2,1,0:T(8,128)(2,1)}), bf16[16,256,256]{2,1,0:T(8,128)(2,1)S(1)}, u32[]{:S(2)}, u32[]{:S(2)}) %all-to-all-start.1) | async-done | bytes 2097184 | tf_op jit(solution)/shard_map/all_to_all | solution.py:53
  127.9 5.3 %all-to-all-start.3 = ((bf16[32,8,256]{2,1,0:T(8,128)(2,1)}), bf16[32,8,256]{2,1,0:T(8,128)(2,1)S(1)}, u32[]{:S(2)}, u32[]{:S(2)}) async-start(bf16[32,8,256]{2,1,0:T(8,128)(2,1)} %bitcast.8), calls=%async_computation.3 | async-start | bytes 262144 | tf_op jit(solution)/shard_map/all_to_all | solution.py:39
  133.2 0.0 copy-start.1
  133.2 0.3 copy.12
  133.5 1.9 %copy-done.1 = bf16[512,4096]{1,0:T(8,128)(2,1)S(1)} copy-done((bf16[512,4096]{1,0:T(8,128)(2,1)S(1)}, bf16[512,4096]{1,0:T(8,128)(2,1)}, u32[]{:S(2)}) %copy-start.1) | copy-done | bytes 4194328
  135.4 1.3 convolution_convert_fusion
  136.7 7.3 %collective-permute-start.1 = (bf16[256,256]{0,1:T(8,128)(2,1)S(1)}, bf16[256,256]{0,1:T(8,128)(2,1)S(1)}, u32[]{:S(2)}, u32[]{:S(2)}) collective-permute-start(bf16[256,256]{0,1:T(8,128)(2,1)S(1)} %slice.9), channel_id=1, source_target_pairs={{0,1},{1,0},{2,3},{3,2},{4,5},{5,4},{6,7},{7,6},{8,9},{9,8},{10,11... | collective-permute-start | bytes 393224 | tf_op jit(solution)/shard_map/ppermute | solution.py:58
  144.0 1.0 collective-permute-done.1
  145.0 0.8 copy.14
  145.9 13.4 %all-to-all-done.3 = bf16[32,8,256]{2,1,0:T(8,128)(2,1)S(1)} async-done(((bf16[32,8,256]{2,1,0:T(8,128)(2,1)}), bf16[32,8,256]{2,1,0:T(8,128)(2,1)S(1)}, u32[]{:S(2)}, u32[]{:S(2)}) %all-to-all-start.3) | async-done | bytes 131104 | tf_op jit(solution)/shard_map/all_to_all | solution.py:39
  159.3 18.7 %all-gather = f32[64,256]{1,0:T(8,128)S(1)} all-gather(f32[8,256]{1,0:T(8,128)S(1)} %convert_reduce_fusion), channel_id=2, replica_groups=mesh['xh'=2,'z'=32,'xl'=2,'y'=4,'c'=2] {'y','c'}, dimensions={0}, use_global_device_ids=true | all-gather | bytes 73728 | tf_op jit(solution)/shard_map/all_gather | solution.py:41
  178.0 0.6 copy.17
  (4 shorter events, 0.1 us)
Async XLA Ops:
  0.6 39.0 %collective-permute-start = (bf16[256,4096]{1,0:T(8,128)(2,1)}, bf16[256,4096]{1,0:T(8,128)(2,1)S(1)}, u32[]{:S(2)}, u32[]{:S(2)}) collective-permute-start(bf16[256,4096]{1,0:T(8,128)(2,1)} %param.4), channel_id=1, source_target_pairs={{0,1},{1,0},{2,3},{3,2},{4,5},{5,4},{6,7},{7,6},{8,9},{9,8},{10,11... | collective-permute-start | bytes 6291464 | tf_op jit(solution)/shard_map/ppermute | solution.py:24
  18.9 46.0 %all-to-all-start = ((bf16[32,8,256]{2,1,0:T(8,128)(2,1)}), bf16[32,8,256]{2,1,0:T(8,128)(2,1)S(1)}, u32[]{:S(2)}, u32[]{:S(2)}) async-start(bf16[32,8,256]{2,1,0:T(8,128)(2,1)} %broadcast_in_dim.17), calls=%async_computation | async-start | bytes 262144 | tf_op jit(solution)/shard_map/all_to_all | solution.py:51
  35.7 4.1 %collective-permute-start.2 = (bf16[256,256]{1,0:T(8,128)(2,1)S(1)}, bf16[256,256]{1,0:T(8,128)(2,1)S(1)}, u32[]{:S(2)}, u32[]{:S(2)}) collective-permute-start(bf16[256,256]{1,0:T(8,128)(2,1)S(1)} %get-tuple-element.13), channel_id=1, source_target_pairs={{0,1},{1,0},{2,3},{3,2},{4,5},{5,4},{6,7},{7,6},{8,9},{9,8},{10,11... | collective-permute-start | bytes 393224 | tf_op jit(solution)/shard_map/ppermute | solution.py:27
  39.8 1.9 %copy-start = (bf16[512,4096]{1,0:T(8,128)(2,1)}, bf16[512,4096]{1,0:T(8,128)(2,1)S(1)}, u32[]{:S(2)}) copy-start(bf16[512,4096]{1,0:T(8,128)(2,1)S(1)} %constant_dynamic-update-slice_fusion) | copy-start | bytes 12582916
  99.0 28.8 %all-to-all-start.1 = ((bf16[16,256,256]{2,1,0:T(8,128)(2,1)}), bf16[16,256,256]{2,1,0:T(8,128)(2,1)S(1)}, u32[]{:S(2)}, u32[]{:S(2)}) async-start(bf16[16,256,256]{2,1,0:T(8,128)(2,1)} %broadcast_in_dim.19), calls=%async_computation.1 | async-start | bytes 4194304 | tf_op jit(solution)/shard_map/all_to_all | solution.py:53
  127.9 31.4 %all-to-all-start.3 = ((bf16[32,8,256]{2,1,0:T(8,128)(2,1)}), bf16[32,8,256]{2,1,0:T(8,128)(2,1)S(1)}, u32[]{:S(2)}, u32[]{:S(2)}) async-start(bf16[32,8,256]{2,1,0:T(8,128)(2,1)} %bitcast.8), calls=%async_computation.3 | async-start | bytes 262144 | tf_op jit(solution)/shard_map/all_to_all | solution.py:39
  133.2 2.2 %copy-start.1 = (bf16[512,4096]{1,0:T(8,128)(2,1)S(1)}, bf16[512,4096]{1,0:T(8,128)(2,1)}, u32[]{:S(2)}) copy-start(bf16[512,4096]{1,0:T(8,128)(2,1)} %copy-done) | copy-start | bytes 12582916
  136.7 8.3 %collective-permute-start.1 = (bf16[256,256]{0,1:T(8,128)(2,1)S(1)}, bf16[256,256]{0,1:T(8,128)(2,1)S(1)}, u32[]{:S(2)}, u32[]{:S(2)}) collective-permute-start(bf16[256,256]{0,1:T(8,128)(2,1)S(1)} %slice.9), channel_id=1, source_target_pairs={{0,1},{1,0},{2,3},{3,2},{4,5},{5,4},{6,7},{7,6},{8,9},{9,8},{10,11... | collective-permute-start | bytes 393224 | tf_op jit(solution)/shard_map/ppermute | solution.py:58

commit v2 on v1

v2 whole, which is shorter than its diff:
```python
import jax
import jax.numpy as jnp
from jax import lax
from jax.sharding import Mesh, PartitionSpec as P

BLOCK = 128
ALL = ("xh", "z", "xl", "y", "c")
X = ("xh", "xl")
SWAP = [(0, 1), (1, 0)]


def around(value, shift):
    return lax.ppermute(value, X, [(i, (i + shift) % 4) for i in range(4)])


def pick(stack, index):
    return lax.dynamic_index_in_dim(stack, index, 0, keepdims=False)


def body(activations, weight_codes, block_scales, cotangent):
    f32, bf16 = jnp.float32, jnp.bfloat16
    c = lax.axis_index("c")
    y = lax.axis_index("y")
    x = lax.axis_index(X)
    tok, d_in = activations.shape
    own, cols = weight_codes.shape
    half = cols // 2
    rows = own // 4
    n_z = lax.axis_size("z")
    column = n_z * rows
    factor = float(tok * n_z * 32) ** (-0.5)

    other_act = lax.ppermute(activations, "c", SWAP)
    my_cot = lax.dynamic_slice(cotangent, (0, c * half), (tok, half))
    send_cot = lax.dynamic_slice(cotangent, (0, (1 - c) * half), (tok, half))
    other_cot = lax.ppermute(send_cot, "c", SWAP)

    blocks = half // BLOCK
    codes = lax.dynamic_slice(weight_codes, (y * rows, c * half), (rows, half))
    scales = lax.dynamic_slice(block_scales, (y * rows, c * blocks), (rows, blocks))
    wide = jnp.repeat(scales.astype(f32), BLOCK, axis=1)
    mine = (codes.astype(f32) * wide).astype(bf16)
    spread = jnp.broadcast_to(mine[None], (n_z, rows, half))
    col = lax.all_to_all(spread, "z", split_axis=0, concat_axis=0, tiled=True)

    dims = (((0,), (0,)), ((), ()))
    acts = jnp.concatenate([activations, other_act], axis=0)
    cots = jnp.concatenate([my_cot, other_cot], axis=0)
    grad = lax.dot_general(acts, cots, dims, preferred_element_type=f32)
    grad = (grad * factor).astype(bf16)
    grad = grad.reshape(2, n_z, 2, 4, rows, half)
    grad = grad.transpose(0, 2, 3, 1, 4, 5).reshape(4, 4, column, half)
    total = pick(grad, x).astype(f32)
    for shift in (1, 3, 2):
        total += around(pick(grad, (x + shift) % 4), shift).astype(f32)
    line = total.astype(bf16)

    both = jnp.concatenate(
        [line, jnp.broadcast_to(col.reshape(1, column, half), (4, column, half))], axis=1
    )
    both = lax.all_to_all(both, "y", split_axis=0, concat_axis=0, tiled=True)
    plane = jnp.sum(both[:, :column].astype(f32), axis=0).astype(bf16)
    moved = lax.all_to_all(
        plane.reshape(n_z, rows, half), "z", split_axis=0, concat_axis=0, tiled=True
    )
    piece = jnp.sum(moved.astype(f32), axis=0)
    pieces = jnp.broadcast_to(piece[None], (8, rows, half))
    pieces = lax.all_to_all(pieces, ("y", "c"), split_axis=0, concat_axis=0, tiled=True)
    pieces = pieces.reshape(4, 2, rows, half)
    weight_grads = pieces.transpose(0, 2, 1, 3).reshape(own, cols)

    slab = both[:, column:]
    held = {shift: around(slab, shift) for shift in (1, 3, 2)}
    stack = jnp.stack([slab, held[1], held[2], held[3]])
    whole = jnp.stack([pick(stack, (x - k) % 4) for k in range(4)])
    whole = whole.reshape(2, 2, 4, n_z, rows, half)
    weight = whole.transpose(0, 3, 1, 2, 4, 5).reshape(d_in, half)

    proj = jnp.dot(acts, weight, preferred_element_type=f32).astype(bf16)
    got = lax.ppermute(proj[tok:], "c", SWAP)
    kept = proj[:tok]
    left = jnp.where(c == 0, kept, got)
    right = jnp.where(c == 0, got, kept)
    projected = jnp.concatenate([left, right], axis=1)
    return (projected, weight_grads)


def solution(mesh):
    fine = Mesh(mesh.devices.reshape(2, 32, 2, 4, 2), ALL)
    placed = (
        P(ALL, None),
        P(("xh", "z", "xl"), None),
        P(("xh", "z", "xl"), None),
        P(ALL, None),
    )
    return jax.shard_map(
        body,
        mesh=fine,
        in_specs=placed,
        out_specs=(P(ALL, None), P(("xh", "z", "xl"), None)),
        check_vma=False,
    )
```

time: 179 us -> 166 us (0.927)
  starting transfers between devices: 50.4 us -> 87 us
  blocking collectives: 51.3 us -> 18.2 us
  waiting for transfers between devices: 59.8 us -> 41.8 us
    all_to_all x1, waiting for transfers between devices: 23 us -> 0.01 us  [body(): col = lax.all_to_all(spread, 'z', split_axis=0, concat_axis=0, tiled=True)]
    all_to_all x2, starting transfers between devices: 9.02 us -> 30.7 us  [the longest x1 21.5 us: body(): lax.all_to_all(plane.reshape(n_z, rows, half), 'z', split_axis=0, concat_...]
    ppermute x0 -> x6, waiting for transfers between devices: none -> 20.7 us  [around(): return lax.ppermute(value, X, [(i, (i + shift) % 4) for i in range(4)])]
    ppermute x0 -> x6, starting transfers between devices: none -> 19.1 us  [around(): return lax.ppermute(value, X, [(i, (i + shift) % 4) for i in range(4)])]
    all_gather x1 -> x0, blocking collectives: 18.7 us -> none  [body(): pieces = lax.all_gather(piece, ('y', 'c'), axis=0, tiled=False)]
    all_to_all x2, waiting for transfers between devices: 35.9 us -> 20.1 us  [the longest x1 16.1 us: body(): lax.all_to_all(plane.reshape(n_z, rows, half), 'z', split_axis=0, concat_...]
    all_to_all x1, blocking collectives: 32.6 us -> 18.2 us  [body(): both = lax.all_to_all(both, 'y', split_axis=0, concat_axis=0, tiled=True)]
    ppermute x1, starting transfers between devices: 7.33 us -> 3.08 us  [body(): got = lax.ppermute(proj[tok:], 'c', SWAP)]
  transfers between devices with their start and end apart: 6 -> 12, of which waited for: 4 -> 7; matrix products, arithmetic and copies ran while one was open for 6% -> 7% of each run, Pallas kernels for 0% -> 0%
where the time goes in v2:
time: 166 us; the launch traced here: 165 us
  starting transfers between devices  87 us (52%)
  waiting for transfers between devices  41.8 us (25%)
  blocking collectives  18.2 us (11%)
  local copies, waits for them, and re-layouts  9.8 us (6%)
  other arithmetic  4.58 us (3%)
  matrix products  2.61 us (2%)
    all_to_all x1, starting transfers between devices, body(): lax.all_to_all(plane.reshape(n_z, rows, half), 'z', split_axis=0, concat_...  21.5 us
    ppermute x6, waiting for transfers between devices, around(): return lax.ppermute(value, X, [(i, (i + shift) % 4) for i in range(4)])  20.7 us
    ppermute x6, starting transfers between devices, around(): return lax.ppermute(value, X, [(i, (i + shift) % 4) for i in range(4)])  19.1 us
    all_to_all x1, blocking collectives, body(): both = lax.all_to_all(both, 'y', split_axis=0, concat_axis=0, tiled=True)  18.2 us
    ppermute x1, starting transfers between devices, body(): other_act = lax.ppermute(activations, 'c', SWAP)  16.1 us
    all_to_all x1, waiting for transfers between devices, body(): lax.all_to_all(plane.reshape(n_z, rows, half), 'z', split_axis=0, concat_...  16.1 us
    all_to_all x1, starting transfers between devices, body(): col = lax.all_to_all(spread, 'z', split_axis=0, concat_axis=0, tiled=True)  15.8 us
    all_to_all x1, starting transfers between devices, body(): lax.all_to_all(pieces, ('y', 'c'), split_axis=0, concat_axis=0, tiled=True)  9.2 us
  transfers between devices with their start and end apart: 12, of which 7 were waited for; matrix products, arithmetic and copies ran while one was open for 7% of the time, Pallas kernels for 0%

profile of v2, /device:TPU:1, one launch (start us, length us, event | category | flops | bytes accessed | tf_op | source)
XLA Modules:
  0.0 165.0 jit_solution(12823218752082217888)
XLA Ops:
  0.6 16.1 %collective-permute-start = (bf16[256,4096]{1,0:T(8,128)(2,1)}, bf16[256,4096]{1,0:T(8,128)(2,1)S(1)}, u32[]{:S(2)}, u32[]{:S(2)}) collective-permute-start(bf16[256,4096]{1,0:T(8,128)(2,1)} %param.4), channel_id=1, source_target_pairs={{0,1},{1,0},{2,3},{3,2},{4,5},{5,4},{6,7},{7,6},{8,9},{9,8},{10,11... | collective-permute-start | bytes 6291464 | tf_op jit(solution)/shard_map/ppermute | solution.py:33
  16.7 0.8 dynamic-slice_convert_fusion
  17.5 0.8 fusion.7
  18.2 0.7 broadcast_in_dim.11
  18.9 15.8 %all-to-all-start = ((bf16[32,8,256]{2,1,0:T(8,128)(2,1)}), bf16[32,8,256]{2,1,0:T(8,128)(2,1)S(1)}, u32[]{:S(2)}, u32[]{:S(2)}) async-start(bf16[32,8,256]{2,1,0:T(8,128)(2,1)} %broadcast_in_dim.11), calls=%async_computation | async-start | bytes 262144 | tf_op jit(solution)/shard_map/all_to_all | solution.py:44
  34.7 1.0 constant_dynamic-slice_fusion.5
  35.7 2.2 %collective-permute-start.1 = (bf16[256,256]{1,0:T(8,128)(2,1)S(1)}, bf16[256,256]{1,0:T(8,128)(2,1)S(1)}, u32[]{:S(2)}, u32[]{:S(2)}) collective-permute-start(bf16[256,256]{1,0:T(8,128)(2,1)S(1)} %get-tuple-element.21), channel_id=1, source_target_pairs={{0,1},{1,0},{2,3},{3,2},{4,5},{5,4},{6,7},{7,6},{8,9},{9,8},{10,11... | collective-permute-start | bytes 393224 | tf_op jit(solution)/shard_map/ppermute | solution.py:36
  38.0 1.7 %constant_dynamic-update-slice_fusion.1 = bf16[512,4096]{1,0:T(8,128)(2,1)S(1)} fusion(bf16[256,4096]{1,0:T(8,128)(2,1)} %param.4), kind=kLoop, calls=%fused_computation.24 | loop fusion | bytes 4194304
  39.9 1.3 fusion
  42.0 0.9 dynamic-slice_bitcast_fusion.2
  42.9 4.6 %collective-permute-start.4 = (bf16[4,256,256]{2,1,0:T(8,128)(2,1)}, bf16[4,256,256]{2,1,0:T(8,128)(2,1)}, u32[]{:S(2)}, u32[]{:S(2)}) collective-permute-start(bf16[4,256,256]{2,1,0:T(8,128)(2,1)} %get-tuple-element.13), channel_id=1, source_target_pairs={{0,512},{8,520},{512,0},{520,8},{1,513},{9,521},{513,1},{521,9},{2... | collective-permute-start | bytes 1572872 | tf_op jit(solution)/shard_map/ppermute | solution.py:13
  47.6 2.8 %collective-permute-start.3 = (bf16[4,256,256]{2,1,0:T(8,128)(2,1)S(1)}, bf16[4,256,256]{2,1,0:T(8,128)(2,1)}, u32[]{:S(2)}, u32[]{:S(2)}) collective-permute-start(bf16[4,256,256]{2,1,0:T(8,128)(2,1)S(1)} %get-tuple-element.14), channel_id=1, source_target_pairs={{0,520},{8,0},{512,8},{520,512},{1,521},{9,1},{513,9},{521,513},{2... | collective-permute-start | bytes 1572872 | tf_op jit(solution)/shard_map/ppermute | solution.py:13
  50.4 2.5 %collective-permute-start.2 = (bf16[4,256,256]{2,1,0:T(8,128)(2,1)S(1)}, bf16[4,256,256]{2,1,0:T(8,128)(2,1)}, u32[]{:S(2)}, u32[]{:S(2)}) collective-permute-start(bf16[4,256,256]{2,1,0:T(8,128)(2,1)S(1)} %get-tuple-element.12), channel_id=1, source_target_pairs={{0,8},{8,512},{512,520},{520,0},{1,9},{9,513},{513,521},{521,1},{2... | collective-permute-start | bytes 1572872 | tf_op jit(solution)/shard_map/ppermute | solution.py:13
  52.9 7.1 %collective-permute-done.4 = bf16[4,256,256]{2,1,0:T(8,128)(2,1)} collective-permute-done((bf16[4,256,256]{2,1,0:T(8,128)(2,1)}, bf16[4,256,256]{2,1,0:T(8,128)(2,1)}, u32[]{:S(2)}, u32[]{:S(2)}) %collective-permute-start.4) | collective-permute-done | bytes 524320 | tf_op jit(solution)/shard_map/ppermute | solution.py:13
  60.0 11.3 %collective-permute-done.3 = bf16[4,256,256]{2,1,0:T(8,128)(2,1)} collective-permute-done((bf16[4,256,256]{2,1,0:T(8,128)(2,1)S(1)}, bf16[4,256,256]{2,1,0:T(8,128)(2,1)}, u32[]{:S(2)}, u32[]{:S(2)}) %collective-permute-start.3) | collective-permute-done | bytes 524320 | tf_op jit(solution)/shard_map/ppermute | solution.py:13
  71.7 1.6 fusion.3
  73.5 18.2 %all_to_all.20 = bf16[4,512,256]{2,1,0:T(8,128)(2,1)S(1)} all-to-all(bf16[4,512,256]{2,1,0:T(8,128)(2,1)S(1)} %pad_maximum_fusion.2), channel_id=1, replica_groups=mesh['xh'=2,'z'=32,'xl'=2,'y'=4,'c'=2] {'y'}, dimensions={0} | all-to-all | bytes 2097152 | tf_op jit(solution)/shard_map/all_to_all | solution.py:61
  91.7 0.8 slice_reduce_fusion
  92.5 4.3 %collective-permute-start.7 = (bf16[4,256,256]{2,1,0:T(8,128)(2,1)S(1)}, bf16[4,256,256]{2,1,0:T(8,128)(2,1)S(1)}, u32[]{:S(2)}, u32[]{:S(2)}) collective-permute-start(bf16[4,256,256]{2,1,0:T(8,128)(2,1)S(1)} %get-tuple-element.17), channel_id=1, source_target_pairs={{0,520},{8,0},{512,8},{520,512},{1,521},{9,1},{513,9},{521,513},{2... | collective-permute-start | bytes 1572872 | tf_op jit(solution)/shard_map/ppermute | solution.py:13
  96.7 2.5 %collective-permute-start.6 = (bf16[4,256,256]{2,1,0:T(8,128)(2,1)S(1)}, bf16[4,256,256]{2,1,0:T(8,128)(2,1)S(1)}, u32[]{:S(2)}, u32[]{:S(2)}) collective-permute-start(bf16[4,256,256]{2,1,0:T(8,128)(2,1)S(1)} %get-tuple-element.17), channel_id=1, source_target_pairs={{0,512},{8,520},{512,0},{520,8},{1,513},{9,521},{513,1},{521,9},{2... | collective-permute-start | bytes 1572872 | tf_op jit(solution)/shard_map/ppermute | solution.py:13
  99.3 2.4 %collective-permute-start.5 = (bf16[4,256,256]{2,1,0:T(8,128)(2,1)S(1)}, bf16[4,256,256]{2,1,0:T(8,128)(2,1)S(1)}, u32[]{:S(2)}, u32[]{:S(2)}) collective-permute-start(bf16[4,256,256]{2,1,0:T(8,128)(2,1)S(1)} %get-tuple-element.17), channel_id=1, source_target_pairs={{0,8},{8,512},{512,520},{520,0},{1,9},{9,513},{513,521},{521,1},{2... | collective-permute-start | bytes 1572872 | tf_op jit(solution)/shard_map/ppermute | solution.py:13
  101.8 21.5 %all-to-all-start.2 = ((bf16[32,8,256]{2,1,0:T(8,128)(2,1)}), bf16[32,8,256]{2,1,0:T(8,128)(2,1)S(1)}, u32[]{:S(2)}, u32[]{:S(2)}) async-start(bf16[32,8,256]{2,1,0:T(8,128)(2,1)} %bitcast.17), calls=%async_computation.2 | async-start | bytes 262144 | tf_op jit(solution)/shard_map/all_to_all | solution.py:63
  123.3 1.9 %collective-permute-done.5 = bf16[4,256,256]{2,1,0:T(8,128)(2,1)S(1)} collective-permute-done((bf16[4,256,256]{2,1,0:T(8,128)(2,1)S(1)}, bf16[4,256,256]{2,1,0:T(8,128)(2,1)S(1)}, u32[]{:S(2)}, u32[]{:S(2)}) %collective-permute-start.5) | collective-permute-done | bytes 524320 | tf_op jit(solution)/shard_map/ppermute | solution.py:13
  126.3 1.9 %copy-done.1 = bf16[512,4096]{1,0:T(8,128)(2,1)S(1)} copy-done((bf16[512,4096]{1,0:T(8,128)(2,1)S(1)}, bf16[512,4096]{1,0:T(8,128)(2,1)}, u32[]{:S(2)}) %copy-start.1) | copy-done | bytes 4194328
  128.2 1.3 convolution_convert_fusion
  129.5 3.1 %collective-permute-start.8 = (bf16[256,256]{0,1:T(8,128)(2,1)S(1)}, bf16[256,256]{0,1:T(8,128)(2,1)S(1)}, u32[]{:S(2)}, u32[]{:S(2)}) collective-permute-start(bf16[256,256]{0,1:T(8,128)(2,1)S(1)} %slice.18), channel_id=1, source_target_pairs={{0,1},{1,0},{2,3},{3,2},{4,5},{5,4},{6,7},{7,6},{8,9},{9,8},{10,11... | collective-permute-start | bytes 393224 | tf_op jit(solution)/shard_map/ppermute | solution.py:80
  132.6 1.0 collective-permute-done.8
  133.6 16.1 %all-to-all-done.2 = bf16[32,8,256]{2,1,0:T(8,128)(2,1)S(1)} async-done(((bf16[32,8,256]{2,1,0:T(8,128)(2,1)}), bf16[32,8,256]{2,1,0:T(8,128)(2,1)S(1)}, u32[]{:S(2)}, u32[]{:S(2)}) %all-to-all-start.2) | async-done | bytes 131104 | tf_op jit(solution)/shard_map/all_to_all | solution.py:63
  149.7 0.6 broadcast_in_dim.26
  150.3 9.2 %all-to-all-start.3 = ((f32[8,8,256]{2,1,0:T(8,128)}), f32[8,8,256]{2,1,0:T(8,128)S(1)}, u32[]{:S(2)}, u32[]{:S(2)}) async-start(f32[8,8,256]{2,1,0:T(8,128)} %broadcast_in_dim.26), calls=%async_computation.3 | async-start | bytes 131072 | tf_op jit(solution)/shard_map/all_to_all | solution.py:68
  159.5 0.8 copy.12
  160.4 4.0 %all-to-all-done.3 = f32[8,8,256]{2,1,0:T(8,128)S(1)} async-done(((f32[8,8,256]{2,1,0:T(8,128)}), f32[8,8,256]{2,1,0:T(8,128)S(1)}, u32[]{:S(2)}, u32[]{:S(2)}) %all-to-all-start.3) | async-done | bytes 65568 | tf_op jit(solution)/shard_map/all_to_all | solution.py:68
  (22 shorter events, 3.2 us)
Async XLA Ops:
  0.6 39.1 %collective-permute-start = (bf16[256,4096]{1,0:T(8,128)(2,1)}, bf16[256,4096]{1,0:T(8,128)(2,1)S(1)}, u32[]{:S(2)}, u32[]{:S(2)}) collective-permute-start(bf16[256,4096]{1,0:T(8,128)(2,1)} %param.4), channel_id=1, source_target_pairs={{0,1},{1,0},{2,3},{3,2},{4,5},{5,4},{6,7},{7,6},{8,9},{9,8},{10,11... | collective-permute-start | bytes 6291464 | tf_op jit(solution)/shard_map/ppermute | solution.py:33
  18.9 54.5 %all-to-all-start = ((bf16[32,8,256]{2,1,0:T(8,128)(2,1)}), bf16[32,8,256]{2,1,0:T(8,128)(2,1)S(1)}, u32[]{:S(2)}, u32[]{:S(2)}) async-start(bf16[32,8,256]{2,1,0:T(8,128)(2,1)} %broadcast_in_dim.11), calls=%async_computation | async-start | bytes 262144 | tf_op jit(solution)/shard_map/all_to_all | solution.py:44
  35.7 4.2 %collective-permute-start.1 = (bf16[256,256]{1,0:T(8,128)(2,1)S(1)}, bf16[256,256]{1,0:T(8,128)(2,1)S(1)}, u32[]{:S(2)}, u32[]{:S(2)}) collective-permute-start(bf16[256,256]{1,0:T(8,128)(2,1)S(1)} %get-tuple-element.21), channel_id=1, source_target_pairs={{0,1},{1,0},{2,3},{3,2},{4,5},{5,4},{6,7},{7,6},{8,9},{9,8},{10,11... | collective-permute-start | bytes 393224 | tf_op jit(solution)/shard_map/ppermute | solution.py:36
  39.8 2.0 %copy-start = (bf16[512,4096]{1,0:T(8,128)(2,1)}, bf16[512,4096]{1,0:T(8,128)(2,1)S(1)}, u32[]{:S(2)}) copy-start(bf16[512,4096]{1,0:T(8,128)(2,1)S(1)} %constant_dynamic-update-slice_fusion) | copy-start | bytes 12582916
  42.9 17.1 %collective-permute-start.4 = (bf16[4,256,256]{2,1,0:T(8,128)(2,1)}, bf16[4,256,256]{2,1,0:T(8,128)(2,1)}, u32[]{:S(2)}, u32[]{:S(2)}) collective-permute-start(bf16[4,256,256]{2,1,0:T(8,128)(2,1)} %get-tuple-element.13), channel_id=1, source_target_pairs={{0,512},{8,520},{512,0},{520,8},{1,513},{9,521},{513,1},{521,9},{2... | collective-permute-start | bytes 1572872 | tf_op jit(solution)/shard_map/ppermute | solution.py:13
  47.6 23.7 %collective-permute-start.3 = (bf16[4,256,256]{2,1,0:T(8,128)(2,1)S(1)}, bf16[4,256,256]{2,1,0:T(8,128)(2,1)}, u32[]{:S(2)}, u32[]{:S(2)}) collective-permute-start(bf16[4,256,256]{2,1,0:T(8,128)(2,1)S(1)} %get-tuple-element.14), channel_id=1, source_target_pairs={{0,520},{8,0},{512,8},{520,512},{1,521},{9,1},{513,9},{521,513},{2... | collective-permute-start | bytes 1572872 | tf_op jit(solution)/shard_map/ppermute | solution.py:13
  50.4 21.4 %collective-permute-start.2 = (bf16[4,256,256]{2,1,0:T(8,128)(2,1)S(1)}, bf16[4,256,256]{2,1,0:T(8,128)(2,1)}, u32[]{:S(2)}, u32[]{:S(2)}) collective-permute-start(bf16[4,256,256]{2,1,0:T(8,128)(2,1)S(1)} %get-tuple-element.12), channel_id=1, source_target_pairs={{0,8},{8,512},{512,520},{520,0},{1,9},{9,513},{513,521},{521,1},{2... | collective-permute-start | bytes 1572872 | tf_op jit(solution)/shard_map/ppermute | solution.py:13
  92.5 30.8 %collective-permute-start.7 = (bf16[4,256,256]{2,1,0:T(8,128)(2,1)S(1)}, bf16[4,256,256]{2,1,0:T(8,128)(2,1)S(1)}, u32[]{:S(2)}, u32[]{:S(2)}) collective-permute-start(bf16[4,256,256]{2,1,0:T(8,128)(2,1)S(1)} %get-tuple-element.17), channel_id=1, source_target_pairs={{0,520},{8,0},{512,8},{520,512},{1,521},{9,1},{513,9},{521,513},{2... | collective-permute-start | bytes 1572872 | tf_op jit(solution)/shard_map/ppermute | solution.py:13
  96.7 26.6 %collective-permute-start.6 = (bf16[4,256,256]{2,1,0:T(8,128)(2,1)S(1)}, bf16[4,256,256]{2,1,0:T(8,128)(2,1)S(1)}, u32[]{:S(2)}, u32[]{:S(2)}) collective-permute-start(bf16[4,256,256]{2,1,0:T(8,128)(2,1)S(1)} %get-tuple-element.17), channel_id=1, source_target_pairs={{0,512},{8,520},{512,0},{520,8},{1,513},{9,521},{513,1},{521,9},{2... | collective-permute-start | bytes 1572872 | tf_op jit(solution)/shard_map/ppermute | solution.py:13
  99.3 26.0 %collective-permute-start.5 = (bf16[4,256,256]{2,1,0:T(8,128)(2,1)S(1)}, bf16[4,256,256]{2,1,0:T(8,128)(2,1)S(1)}, u32[]{:S(2)}, u32[]{:S(2)}) collective-permute-start(bf16[4,256,256]{2,1,0:T(8,128)(2,1)S(1)} %get-tuple-element.17), channel_id=1, source_target_pairs={{0,8},{8,512},{512,520},{520,0},{1,9},{9,513},{513,521},{521,1},{2... | collective-permute-start | bytes 1572872 | tf_op jit(solution)/shard_map/ppermute | solution.py:13
  101.8 47.8 %all-to-all-start.2 = ((bf16[32,8,256]{2,1,0:T(8,128)(2,1)}), bf16[32,8,256]{2,1,0:T(8,128)(2,1)S(1)}, u32[]{:S(2)}, u32[]{:S(2)}) async-start(bf16[32,8,256]{2,1,0:T(8,128)(2,1)} %bitcast.17), calls=%async_computation.2 | async-start | bytes 262144 | tf_op jit(solution)/shard_map/all_to_all | solution.py:63
  126.0 2.2 %copy-start.1 = (bf16[512,4096]{1,0:T(8,128)(2,1)S(1)}, bf16[512,4096]{1,0:T(8,128)(2,1)}, u32[]{:S(2)}) copy-start(bf16[512,4096]{1,0:T(8,128)(2,1)} %copy-done) | copy-start | bytes 12582916
  129.5 4.1 %collective-permute-start.8 = (bf16[256,256]{0,1:T(8,128)(2,1)S(1)}, bf16[256,256]{0,1:T(8,128)(2,1)S(1)}, u32[]{:S(2)}, u32[]{:S(2)}) collective-permute-start(bf16[256,256]{0,1:T(8,128)(2,1)S(1)} %slice.18), channel_id=1, source_target_pairs={{0,1},{1,0},{2,3},{3,2},{4,5},{5,4},{6,7},{7,6},{8,9},{9,8},{10,11... | collective-permute-start | bytes 393224 | tf_op jit(solution)/shard_map/ppermute | solution.py:80
  150.3 14.1 %all-to-all-start.3 = ((f32[8,8,256]{2,1,0:T(8,128)}), f32[8,8,256]{2,1,0:T(8,128)S(1)}, u32[]{:S(2)}, u32[]{:S(2)}) async-start(f32[8,8,256]{2,1,0:T(8,128)} %broadcast_in_dim.26), calls=%async_computation.3 | async-start | bytes 131072 | tf_op jit(solution)/shard_map/all_to_all | solution.py:68

commit v3 on v2

--- a/solution.py
+++ b/solution.py
@@ -13,6 +13,13 @@
     return lax.ppermute(value, X, [(i, (i + shift) % 4) for i in range(4)])
 
 
+def over_z(value, steps):
+    def step(held):
+        return lax.all_to_all(held, "z", split_axis=0, concat_axis=0, tiled=True)
+
+    return lax.cond(steps > 0, step, lambda held: held, value)
+
+
 def pick(stack, index):
     return lax.dynamic_index_in_dim(stack, index, 0, keepdims=False)
 
@@ -22,6 +29,7 @@
     c = lax.axis_index("c")
     y = lax.axis_index("y")
     x = lax.axis_index(X)
+    once = 1 + jnp.minimum(x, 0)
     tok, d_in = activations.shape
     own, cols = weight_codes.shape
     half = cols // 2
@@ -41,7 +49,6 @@
     wide = jnp.repeat(scales.astype(f32), BLOCK, axis=1)
     mine = (codes.astype(f32) * wide).astype(bf16)
     spread = jnp.broadcast_to(mine[None], (n_z, rows, half))
-    col = lax.all_to_all(spread, "z", split_axis=0, concat_axis=0, tiled=True)
 
     dims = (((0,), (0,)), ((), ()))
     acts = jnp.concatenate([activations, other_act], axis=0)
@@ -50,9 +57,14 @@
     grad = (grad * factor).astype(bf16)
     grad = grad.reshape(2, n_z, 2, 4, rows, half)
     grad = grad.transpose(0, 2, 3, 1, 4, 5).reshape(4, 4, column, half)
+    sends = [pick(grad, (x + shift) % 4) for shift in (2, 1, 3)]
+    *sends, spread = lax.optimization_barrier((*sends, spread))
+    parts = [around(send, shift) for send, shift in zip(sends, (2, 1, 3))]
+    col = over_z(spread, once)
+    *parts, col = lax.optimization_barrier((*parts, col))
     total = pick(grad, x).astype(f32)
-    for shift in (1, 3, 2):
-        total += around(pick(grad, (x + shift) % 4), shift).astype(f32)
+    for part in parts:
+        total += part.astype(f32)
     line = total.astype(bf16)
 
     both = jnp.concatenate(
@@ -60,18 +72,19 @@
     )
     both = lax.all_to_all(both, "y", split_axis=0, concat_axis=0, tiled=True)
     plane = jnp.sum(both[:, :column].astype(f32), axis=0).astype(bf16)
-    moved = lax.all_to_all(
-        plane.reshape(n_z, rows, half), "z", split_axis=0, concat_axis=0, tiled=True
-    )
+    slab = both[:, column:]
+    slab, plane = lax.optimization_barrier((slab, plane))
+    held = [around(slab, shift) for shift in (2, 1, 3)]
+    moved = over_z(plane.reshape(n_z, rows, half), once)
+    *held, moved = lax.optimization_barrier((*held, moved))
     piece = jnp.sum(moved.astype(f32), axis=0)
     pieces = jnp.broadcast_to(piece[None], (8, rows, half))
     pieces = lax.all_to_all(pieces, ("y", "c"), split_axis=0, concat_axis=0, tiled=True)
     pieces = pieces.reshape(4, 2, rows, half)
     weight_grads = pieces.transpose(0, 2, 1, 3).reshape(own, cols)
 
-    slab = both[:, column:]
-    held = {shift: around(slab, shift) for shift in (1, 3, 2)}
-    stack = jnp.stack([slab, held[1], held[2], held[3]])
+    two, one, three = held
+    stack = jnp.stack([slab, one, two, three])
     whole = jnp.stack([pick(stack, (x - k) % 4) for k in range(4)])
     whole = whole.reshape(2, 2, 4, n_z, rows, half)
     weight = whole.transpose(0, 3, 1, 2, 4, 5).reshape(d_in, half)

time: 166 us -> 164 us (0.988)
  blocking collectives: 18.2 us -> 94.4 us
  starting transfers between devices: 87 us -> 47.2 us
  waiting for transfers between devices: 41.8 us -> 4.84 us
    all_to_all x0 -> x2, blocking collectives: none -> 79.6 us  [step(): return lax.all_to_all(held, 'z', split_axis=0, concat_axis=0, tiled=True)]
    all_to_all x2 -> x0, starting transfers between devices: 37.3 us -> none  [the longest x1 21.5 us: body(): lax.all_to_all(plane.reshape(n_z, rows, half), 'z', split_axis=0, concat_...]
    ppermute x6, waiting for transfers between devices: 20.7 us -> 0.02 us  [around(): return lax.ppermute(value, X, [(i, (i + shift) % 4) for i in range(4)])]
    all_to_all x2 -> x0, waiting for transfers between devices: 16.1 us -> none  [the longest x1 16.1 us: body(): lax.all_to_all(plane.reshape(n_z, rows, half), 'z', split_axis=0, concat_...]
    all_to_all x1, starting transfers between devices: 9.2 us -> 3.3 us  [body(): lax.all_to_all(pieces, ('y', 'c'), split_axis=0, concat_axis=0, tiled=True)]
    ppermute x1, starting transfers between devices: 3.08 us -> 7.94 us  [body(): got = lax.ppermute(proj[tok:], 'c', SWAP)]
    all_to_all x1, blocking collectives: 18.2 us -> 14.8 us  [body(): both = lax.all_to_all(both, 'y', split_axis=0, concat_axis=0, tiled=True)]
  transfers between devices with their start and end apart: 12 -> 10, of which waited for: 7 -> 1; matrix products, arithmetic and copies ran while one was open for 7% -> 3% of each run, Pallas kernels for 0% -> 0%
where the time goes in v3:
time: 164 us; the launch traced here: 163 us
  blocking collectives  94.4 us (58%)
  starting transfers between devices  47.2 us (29%)
  local copies, waits for them, and re-layouts  9.14 us (6%)
  waiting for transfers between devices  4.84 us (3%)
  other arithmetic  3.88 us (2%)
  matrix products  2.61 us (2%)
    all_to_all x2, blocking collectives, step(): return lax.all_to_all(held, 'z', split_axis=0, concat_axis=0, tiled=True)  79.6 us
    ppermute x6, starting transfers between devices, around(): return lax.ppermute(value, X, [(i, (i + shift) % 4) for i in range(4)])  17.9 us
    ppermute x1, starting transfers between devices, body(): other_act = lax.ppermute(activations, 'c', SWAP)  16.1 us
    all_to_all x1, blocking collectives, body(): both = lax.all_to_all(both, 'y', split_axis=0, concat_axis=0, tiled=True)  14.8 us
    ppermute x1, starting transfers between devices, body(): got = lax.ppermute(proj[tok:], 'c', SWAP)  7.94 us
    unnamed x7, local copies, waits for them, and re-layouts  5.7 us
    all_to_all x1, waiting for transfers between devices, body(): lax.all_to_all(pieces, ('y', 'c'), split_axis=0, concat_axis=0, tiled=True)  4.82 us
    all_to_all x1, starting transfers between devices, body(): lax.all_to_all(pieces, ('y', 'c'), split_axis=0, concat_axis=0, tiled=True)  3.3 us
  transfers between devices with their start and end apart: 10, of which 1 were waited for; matrix products, arithmetic and copies ran while one was open for 3% of the time, Pallas kernels for 0%

profile of v3, /device:TPU:1, one launch (start us, length us, event | category | flops | bytes accessed | tf_op | source)
XLA Modules:
  0.0 163.1 jit_solution(8505013518640439720)
XLA Ops:
  0.6 16.1 %collective-permute-start = (bf16[256,4096]{1,0:T(8,128)(2,1)}, bf16[256,4096]{1,0:T(8,128)(2,1)S(1)}, u32[]{:S(2)}, u32[]{:S(2)}) collective-permute-start(bf16[256,4096]{1,0:T(8,128)(2,1)} %param.8), channel_id=1, source_target_pairs={{0,1},{1,0},{2,3},{3,2},{4,5},{5,4},{6,7},{7,6},{8,9},{9,8},{10,11... | collective-permute-start | bytes 6291464 | tf_op jit(solution)/shard_map/ppermute | solution.py:41
  16.7 1.0 constant_dynamic-slice_fusion.5
  17.7 1.9 %collective-permute-start.1 = (bf16[256,256]{1,0:T(8,128)(2,1)S(1)}, bf16[256,256]{1,0:T(8,128)(2,1)S(1)}, u32[]{:S(2)}, u32[]{:S(2)}) collective-permute-start(bf16[256,256]{1,0:T(8,128)(2,1)S(1)} %get-tuple-element.56), channel_id=1, source_target_pairs={{0,1},{1,0},{2,3},{3,2},{4,5},{5,4},{6,7},{7,6},{8,9},{9,8},{10,11... | collective-permute-start | bytes 393224 | tf_op jit(solution)/shard_map/ppermute | solution.py:44
  19.7 0.8 dynamic-slice_convert_fusion
  20.4 0.8 fusion.7
  21.2 1.7 %constant_dynamic-update-slice_fusion.1 = bf16[512,4096]{1,0:T(8,128)(2,1)S(1)} fusion(bf16[256,4096]{1,0:T(8,128)(2,1)} %param.8), kind=kLoop, calls=%fused_computation.24 | loop fusion | bytes 4194304
  23.1 1.3 fusion
  24.4 0.6 copy-done
  25.2 0.9 dynamic-slice_bitcast_fusion
  26.2 1.9 %collective-permute-start.2 = (bf16[4,256,256]{2,1,0:T(8,128)(2,1)}, bf16[4,256,256]{2,1,0:T(8,128)(2,1)}, u32[]{:S(2)}, u32[]{:S(2)}) collective-permute-start(bf16[4,256,256]{2,1,0:T(8,128)(2,1)} %get-tuple-element.26), channel_id=1, source_target_pairs={{0,512},{8,520},{512,0},{520,8},{1,513},{9,521},{513,1},{521,9},{2... | collective-permute-start | bytes 1572872 | tf_op jit(solution)/shard_map/ppermute | solution.py:13
  28.1 1.9 %collective-permute-start.3 = (bf16[4,256,256]{2,1,0:T(8,128)(2,1)S(1)}, bf16[4,256,256]{2,1,0:T(8,128)(2,1)}, u32[]{:S(2)}, u32[]{:S(2)}) collective-permute-start(bf16[4,256,256]{2,1,0:T(8,128)(2,1)S(1)} %get-tuple-element.27), channel_id=1, source_target_pairs={{0,8},{8,512},{512,520},{520,0},{1,9},{9,513},{513,521},{521,1},{2... | collective-permute-start | bytes 1572872 | tf_op jit(solution)/shard_map/ppermute | solution.py:13
  30.0 4.6 %collective-permute-start.4 = (bf16[4,256,256]{2,1,0:T(8,128)(2,1)S(1)}, bf16[4,256,256]{2,1,0:T(8,128)(2,1)}, u32[]{:S(2)}, u32[]{:S(2)}) collective-permute-start(bf16[4,256,256]{2,1,0:T(8,128)(2,1)S(1)} %get-tuple-element.28), channel_id=1, source_target_pairs={{0,520},{8,0},{512,8},{520,512},{1,521},{9,1},{513,9},{521,513},{2... | collective-permute-start | bytes 1572872 | tf_op jit(solution)/shard_map/ppermute | solution.py:13
  34.6 47.0 %conditional.2 = (bf16[32,8,256]{2,1,0:T(8,128)(2,1)S(1)}) conditional(s32[]{:T(128)} %convert_element_type.48, bf16[32,8,256]{2,1,0:T(8,128)(2,1)S(1)} %broadcast_in_dim.11, bf16[32,8,256]{2,1,0:T(8,128)(2,1)S(1)} %broadcast_in_dim.11), branch_computations={%region_0.1_spmd, %region_1.2_spmd} | conditional | bytes 524296 | solution.py:20
  34.6 47.0 %all_to_all.18 = bf16[32,8,256]{2,1,0:T(8,128)(2,1)S(1)} all-to-all(bf16[32,8,256]{2,1,0:T(8,128)(2,1)S(1)} %copy.16), channel_id=1, replica_groups=mesh['xh'=2,'z'=32,'xl'=2,'y'=4,'c'=2] {'z'}, dimensions={0} | all-to-all | bytes 262144 | tf_op jit(solution)/shard_map/cond/branch_1_fun/all_to_all | solution.py:18
  81.6 1.6 fusion.3
  83.4 14.8 %all_to_all.20 = bf16[4,512,256]{2,1,0:T(8,128)(2,1)S(1)} all-to-all(bf16[4,512,256]{2,1,0:T(8,128)(2,1)S(1)} %pad_maximum_fusion.2), channel_id=1, replica_groups=mesh['xh'=2,'z'=32,'xl'=2,'y'=4,'c'=2] {'y'}, dimensions={0} | all-to-all | bytes 2097152 | tf_op jit(solution)/shard_map/all_to_all | solution.py:73
  98.2 3.0 %collective-permute-start.5 = (bf16[4,256,256]{2,1,0:T(8,128)(2,1)S(1)}, bf16[4,256,256]{2,1,0:T(8,128)(2,1)S(1)}, u32[]{:S(2)}, u32[]{:S(2)}) collective-permute-start(bf16[4,256,256]{2,1,0:T(8,128)(2,1)S(1)} %get-tuple-element.34), channel_id=1, source_target_pairs={{0,512},{8,520},{512,0},{520,8},{1,513},{9,521},{513,1},{521,9},{2... | collective-permute-start | bytes 1572872 | tf_op jit(solution)/shard_map/ppermute | solution.py:13
  101.2 3.1 %collective-permute-start.6 = (bf16[4,256,256]{2,1,0:T(8,128)(2,1)S(1)}, bf16[4,256,256]{2,1,0:T(8,128)(2,1)S(1)}, u32[]{:S(2)}, u32[]{:S(2)}) collective-permute-start(bf16[4,256,256]{2,1,0:T(8,128)(2,1)S(1)} %get-tuple-element.34), channel_id=1, source_target_pairs={{0,8},{8,512},{512,520},{520,0},{1,9},{9,513},{513,521},{521,1},{2... | collective-permute-start | bytes 1572872 | tf_op jit(solution)/shard_map/ppermute | solution.py:13
  104.3 3.4 %collective-permute-start.7 = (bf16[4,256,256]{2,1,0:T(8,128)(2,1)S(1)}, bf16[4,256,256]{2,1,0:T(8,128)(2,1)S(1)}, u32[]{:S(2)}, u32[]{:S(2)}) collective-permute-start(bf16[4,256,256]{2,1,0:T(8,128)(2,1)S(1)} %get-tuple-element.34), channel_id=1, source_target_pairs={{0,520},{8,0},{512,8},{520,512},{1,521},{9,1},{513,9},{521,513},{2... | collective-permute-start | bytes 1572872 | tf_op jit(solution)/shard_map/ppermute | solution.py:13
  107.8 32.7 %conditional.3 = (bf16[32,8,256]{2,1,0:T(8,128)(2,1)S(1)}) conditional(s32[]{:T(128)} %convert_element_type.48, bf16[32,8,256]{2,1,0:T(8,128)(2,1)S(1)} %bitcast.42, bf16[32,8,256]{2,1,0:T(8,128)(2,1)S(1)} %bitcast.43), branch_computations={%region_3.4_spmd, %region_4.5_spmd} | conditional | bytes 524296 | solution.py:20
  107.9 32.7 %all_to_all.19 = bf16[32,8,256]{2,1,0:T(8,128)(2,1)S(1)} all-to-all(bf16[32,8,256]{2,1,0:T(8,128)(2,1)S(1)} %copy.17), channel_id=1, replica_groups=mesh['xh'=2,'z'=32,'xl'=2,'y'=4,'c'=2] {'z'}, dimensions={0} | all-to-all | bytes 262144 | tf_op jit(solution)/shard_map/cond/branch_1_fun/all_to_all | solution.py:18
  140.5 0.3 pad_maximum_fusion
  141.0 0.3 pad_maximum_fusion.1
  141.3 0.3 copy.8
  141.6 1.9 %copy-done.1 = bf16[512,4096]{1,0:T(8,128)(2,1)S(1)} copy-done((bf16[512,4096]{1,0:T(8,128)(2,1)S(1)}, bf16[512,4096]{1,0:T(8,128)(2,1)}, u32[]{:S(2)}) %copy-start.1) | copy-done | bytes 4194328
  143.5 1.3 convolution_convert_fusion
  144.8 7.9 %collective-permute-start.8 = (bf16[256,256]{0,1:T(8,128)(2,1)S(1)}, bf16[256,256]{0,1:T(8,128)(2,1)S(1)}, u32[]{:S(2)}, u32[]{:S(2)}) collective-permute-start(bf16[256,256]{0,1:T(8,128)(2,1)S(1)} %slice.19), channel_id=1, source_target_pairs={{0,1},{1,0},{2,3},{3,2},{4,5},{5,4},{6,7},{7,6},{8,9},{9,8},{10,11... | collective-permute-start | bytes 393224 | tf_op jit(solution)/shard_map/ppermute | solution.py:93
  152.8 0.6 broadcast_in_dim.26
  153.4 3.3 %all-to-all-start.3 = ((f32[8,8,256]{2,1,0:T(8,128)}), f32[8,8,256]{2,1,0:T(8,128)S(1)}, u32[]{:S(2)}, u32[]{:S(2)}) async-start(f32[8,8,256]{2,1,0:T(8,128)} %broadcast_in_dim.26), calls=%async_computation.3 | async-start | bytes 131072 | tf_op jit(solution)/shard_map/all_to_all | solution.py:82
  156.7 4.8 %all-to-all-done.3 = f32[8,8,256]{2,1,0:T(8,128)S(1)} async-done(((f32[8,8,256]{2,1,0:T(8,128)}), f32[8,8,256]{2,1,0:T(8,128)S(1)}, u32[]{:S(2)}, u32[]{:S(2)}) %all-to-all-start.3) | async-done | bytes 65568 | tf_op jit(solution)/shard_map/all_to_all | solution.py:82
  161.6 0.8 copy.9
  162.5 0.6 copy.18
  (24 shorter events, 0.9 us)
Async XLA Ops:
  0.6 22.3 %collective-permute-start = (bf16[256,4096]{1,0:T(8,128)(2,1)}, bf16[256,4096]{1,0:T(8,128)(2,1)S(1)}, u32[]{:S(2)}, u32[]{:S(2)}) collective-permute-start(bf16[256,4096]{1,0:T(8,128)(2,1)} %param.8), channel_id=1, source_target_pairs={{0,1},{1,0},{2,3},{3,2},{4,5},{5,4},{6,7},{7,6},{8,9},{9,8},{10,11... | collective-permute-start | bytes 6291464 | tf_op jit(solution)/shard_map/ppermute | solution.py:41
  17.7 5.4 %collective-permute-start.1 = (bf16[256,256]{1,0:T(8,128)(2,1)S(1)}, bf16[256,256]{1,0:T(8,128)(2,1)S(1)}, u32[]{:S(2)}, u32[]{:S(2)}) collective-permute-start(bf16[256,256]{1,0:T(8,128)(2,1)S(1)} %get-tuple-element.56), channel_id=1, source_target_pairs={{0,1},{1,0},{2,3},{3,2},{4,5},{5,4},{6,7},{7,6},{8,9},{9,8},{10,11... | collective-permute-start | bytes 393224 | tf_op jit(solution)/shard_map/ppermute | solution.py:44
  23.1 1.9 %copy-start = (bf16[512,4096]{1,0:T(8,128)(2,1)}, bf16[512,4096]{1,0:T(8,128)(2,1)S(1)}, u32[]{:S(2)}) copy-start(bf16[512,4096]{1,0:T(8,128)(2,1)S(1)} %constant_dynamic-update-slice_fusion) | copy-start | bytes 12582916
  26.2 55.4 %collective-permute-start.2 = (bf16[4,256,256]{2,1,0:T(8,128)(2,1)}, bf16[4,256,256]{2,1,0:T(8,128)(2,1)}, u32[]{:S(2)}, u32[]{:S(2)}) collective-permute-start(bf16[4,256,256]{2,1,0:T(8,128)(2,1)} %get-tuple-element.26), channel_id=1, source_target_pairs={{0,512},{8,520},{512,0},{520,8},{1,513},{9,521},{513,1},{521,9},{2... | collective-permute-start | bytes 1572872 | tf_op jit(solution)/shard_map/ppermute | solution.py:13
  28.1 53.5 %collective-permute-start.3 = (bf16[4,256,256]{2,1,0:T(8,128)(2,1)S(1)}, bf16[4,256,256]{2,1,0:T(8,128)(2,1)}, u32[]{:S(2)}, u32[]{:S(2)}) collective-permute-start(bf16[4,256,256]{2,1,0:T(8,128)(2,1)S(1)} %get-tuple-element.27), channel_id=1, source_target_pairs={{0,8},{8,512},{512,520},{520,0},{1,9},{9,513},{513,521},{521,1},{2... | collective-permute-start | bytes 1572872 | tf_op jit(solution)/shard_map/ppermute | solution.py:13
  30.0 51.6 %collective-permute-start.4 = (bf16[4,256,256]{2,1,0:T(8,128)(2,1)S(1)}, bf16[4,256,256]{2,1,0:T(8,128)(2,1)}, u32[]{:S(2)}, u32[]{:S(2)}) collective-permute-start(bf16[4,256,256]{2,1,0:T(8,128)(2,1)S(1)} %get-tuple-element.28), channel_id=1, source_target_pairs={{0,520},{8,0},{512,8},{520,512},{1,521},{9,1},{513,9},{521,513},{2... | collective-permute-start | bytes 1572872 | tf_op jit(solution)/shard_map/ppermute | solution.py:13
  98.2 42.3 %collective-permute-start.5 = (bf16[4,256,256]{2,1,0:T(8,128)(2,1)S(1)}, bf16[4,256,256]{2,1,0:T(8,128)(2,1)S(1)}, u32[]{:S(2)}, u32[]{:S(2)}) collective-permute-start(bf16[4,256,256]{2,1,0:T(8,128)(2,1)S(1)} %get-tuple-element.34), channel_id=1, source_target_pairs={{0,512},{8,520},{512,0},{520,8},{1,513},{9,521},{513,1},{521,9},{2... | collective-permute-start | bytes 1572872 | tf_op jit(solution)/shard_map/ppermute | solution.py:13
  101.2 39.3 %collective-permute-start.6 = (bf16[4,256,256]{2,1,0:T(8,128)(2,1)S(1)}, bf16[4,256,256]{2,1,0:T(8,128)(2,1)S(1)}, u32[]{:S(2)}, u32[]{:S(2)}) collective-permute-start(bf16[4,256,256]{2,1,0:T(8,128)(2,1)S(1)} %get-tuple-element.34), channel_id=1, source_target_pairs={{0,8},{8,512},{512,520},{520,0},{1,9},{9,513},{513,521},{521,1},{2... | collective-permute-start | bytes 1572872 | tf_op jit(solution)/shard_map/ppermute | solution.py:13
  104.3 36.2 %collective-permute-start.7 = (bf16[4,256,256]{2,1,0:T(8,128)(2,1)S(1)}, bf16[4,256,256]{2,1,0:T(8,128)(2,1)S(1)}, u32[]{:S(2)}, u32[]{:S(2)}) collective-permute-start(bf16[4,256,256]{2,1,0:T(8,128)(2,1)S(1)} %get-tuple-element.34), channel_id=1, source_target_pairs={{0,520},{8,0},{512,8},{520,512},{1,521},{9,1},{513,9},{521,513},{2... | collective-permute-start | bytes 1572872 | tf_op jit(solution)/shard_map/ppermute | solution.py:13
  141.3 2.2 %copy-start.1 = (bf16[512,4096]{1,0:T(8,128)(2,1)S(1)}, bf16[512,4096]{1,0:T(8,128)(2,1)}, u32[]{:S(2)}) copy-start(bf16[512,4096]{1,0:T(8,128)(2,1)} %copy-done) | copy-start | bytes 12582916
  144.8 16.8 %collective-permute-start.8 = (bf16[256,256]{0,1:T(8,128)(2,1)S(1)}, bf16[256,256]{0,1:T(8,128)(2,1)S(1)}, u32[]{:S(2)}, u32[]{:S(2)}) collective-permute-start(bf16[256,256]{0,1:T(8,128)(2,1)S(1)} %slice.19), channel_id=1, source_target_pairs={{0,1},{1,0},{2,3},{3,2},{4,5},{5,4},{6,7},{7,6},{8,9},{9,8},{10,11... | collective-permute-start | bytes 393224 | tf_op jit(solution)/shard_map/ppermute | solution.py:93
  153.4 8.1 %all-to-all-start.3 = ((f32[8,8,256]{2,1,0:T(8,128)}), f32[8,8,256]{2,1,0:T(8,128)S(1)}, u32[]{:S(2)}, u32[]{:S(2)}) async-start(f32[8,8,256]{2,1,0:T(8,128)} %broadcast_in_dim.26), calls=%async_computation.3 | async-start | bytes 131072 | tf_op jit(solution)/shard_map/all_to_all | solution.py:82

commit v4 on v3

--- a/solution.py
+++ b/solution.py
@@ -13,13 +13,6 @@
     return lax.ppermute(value, X, [(i, (i + shift) % 4) for i in range(4)])
 
 
-def over_z(value, steps):
-    def step(held):
-        return lax.all_to_all(held, "z", split_axis=0, concat_axis=0, tiled=True)
-
-    return lax.cond(steps > 0, step, lambda held: held, value)
-
-
 def pick(stack, index):
     return lax.dynamic_index_in_dim(stack, index, 0, keepdims=False)
 
@@ -29,7 +22,6 @@
     c = lax.axis_index("c")
     y = lax.axis_index("y")
     x = lax.axis_index(X)
-    once = 1 + jnp.minimum(x, 0)
     tok, d_in = activations.shape
     own, cols = weight_codes.shape
     half = cols // 2
@@ -58,10 +50,12 @@
     grad = grad.reshape(2, n_z, 2, 4, rows, half)
     grad = grad.transpose(0, 2, 3, 1, 4, 5).reshape(4, 4, column, half)
     sends = [pick(grad, (x + shift) % 4) for shift in (2, 1, 3)]
-    *sends, spread = lax.optimization_barrier((*sends, spread))
     parts = [around(send, shift) for send, shift in zip(sends, (2, 1, 3))]
-    col = over_z(spread, once)
-    *parts, col = lax.optimization_barrier((*parts, col))
+    turned = [[(k + n_z // 2) % n_z for k in range(n_z)]]
+    col = lax.all_to_all(
+        spread, "z", split_axis=0, concat_axis=0, axis_index_groups=turned, tiled=True
+    )
+    col = jnp.roll(col, n_z // 2, axis=0)
     total = pick(grad, x).astype(f32)
     for part in parts:
         total += part.astype(f32)
@@ -73,9 +67,10 @@
     both = lax.all_to_all(both, "y", split_axis=0, concat_axis=0, tiled=True)
     plane = jnp.sum(both[:, :column].astype(f32), axis=0).astype(bf16)
     slab = both[:, column:]
-    slab, plane = lax.optimization_barrier((slab, plane))
     held = [around(slab, shift) for shift in (2, 1, 3)]
-    moved = over_z(plane.reshape(n_z, rows, half), once)
+    moved = lax.all_to_all(
+        plane.reshape(n_z, rows, half), "z", split_axis=0, concat_axis=0, tiled=True
+    )
     *held, moved = lax.optimization_barrier((*held, moved))
     piece = jnp.sum(moved.astype(f32), axis=0)
     pieces = jnp.broadcast_to(piece[None], (8, rows, half))

time: 164 us -> 156 us (0.951)
  blocking collectives: 94.4 us -> 17.4 us
  waiting for transfers between devices: 4.84 us -> 45.6 us
  starting transfers between devices: 47.2 us -> 73.9 us
    all_to_all x2 -> x0, blocking collectives: 79.6 us -> none  [step(): return lax.all_to_all(held, 'z', split_axis=0, concat_axis=0, tiled=True)]
    ppermute x6, waiting for transfers between devices: 0.02 us -> 40.8 us  [around(): return lax.ppermute(value, X, [(i, (i + shift) % 4) for i in range(4)])]
    all_to_all x0 -> x2, starting transfers between devices: none -> 26.5 us  [the longest x1 22.7 us: body(): lax.all_to_all(spread, 'z', split_axis=0, concat_axis=0, axis_index_group...]
    all_to_all x1, blocking collectives: 14.8 us -> 17.4 us  [body(): both = lax.all_to_all(both, 'y', split_axis=0, concat_axis=0, tiled=True)]
    ppermute x1, starting transfers between devices: 7.94 us -> 5.92 us  [body(): got = lax.ppermute(proj[tok:], 'c', SWAP)]
  transfers between devices with their start and end apart: 10 -> 12, of which waited for: 1 -> 5; matrix products, arithmetic and copies ran while one was open for 3% -> 5% of each run, Pallas kernels for 0% -> 0%
where the time goes in v4:
time: 156 us; the launch traced here: 155 us
  starting transfers between devices  73.9 us (47%)
  waiting for transfers between devices  45.6 us (29%)
  blocking collectives  17.4 us (11%)
  local copies, waits for them, and re-layouts  9.8 us (6%)
  other arithmetic  4.6 us (3%)
  matrix products  2.6 us (2%)
    ppermute x6, waiting for transfers between devices, around(): return lax.ppermute(value, X, [(i, (i + shift) % 4) for i in range(4)])  40.8 us
    all_to_all x1, starting transfers between devices, body(): lax.all_to_all(spread, 'z', split_axis=0, concat_axis=0, axis_index_group...  22.7 us
    ppermute x6, starting transfers between devices, around(): return lax.ppermute(value, X, [(i, (i + shift) % 4) for i in range(4)])  19.6 us
    all_to_all x1, blocking collectives, body(): both = lax.all_to_all(both, 'y', split_axis=0, concat_axis=0, tiled=True)  17.4 us
    ppermute x1, starting transfers between devices, body(): other_act = lax.ppermute(activations, 'c', SWAP)  16.1 us
    ppermute x1, starting transfers between devices, body(): got = lax.ppermute(proj[tok:], 'c', SWAP)  5.92 us
    unnamed x7, local copies, waits for them, and re-layouts  5.72 us
    all_to_all x1, waiting for transfers between devices, body(): lax.all_to_all(pieces, ('y', 'c'), split_axis=0, concat_axis=0, tiled=True)  4.82 us
  transfers between devices with their start and end apart: 12, of which 5 were waited for; matrix products, arithmetic and copies ran while one was open for 5% of the time, Pallas kernels for 0%

profile of v4, /device:TPU:1, one launch (start us, length us, event | category | flops | bytes accessed | tf_op | source)
XLA Modules:
  0.0 155.0 jit_solution(11435342411400634261)
XLA Ops:
  0.6 16.1 %collective-permute-start = (bf16[256,4096]{1,0:T(8,128)(2,1)}, bf16[256,4096]{1,0:T(8,128)(2,1)S(1)}, u32[]{:S(2)}, u32[]{:S(2)}) collective-permute-start(bf16[256,4096]{1,0:T(8,128)(2,1)} %param.4), channel_id=1, source_target_pairs={{0,1},{1,0},{2,3},{3,2},{4,5},{5,4},{6,7},{7,6},{8,9},{9,8},{10,11... | collective-permute-start | bytes 6291464 | tf_op jit(solution)/shard_map/ppermute | solution.py:33
  16.7 0.8 dynamic-slice_convert_fusion
  17.5 0.8 fusion.7
  18.2 0.7 broadcast_in_dim.11
  18.9 22.7 %all-to-all-start = ((bf16[32,8,256]{2,1,0:T(8,128)(2,1)}), bf16[32,8,256]{2,1,0:T(8,128)(2,1)S(1)}, u32[]{:S(2)}, u32[]{:S(2)}) async-start(bf16[32,8,256]{2,1,0:T(8,128)(2,1)} %broadcast_in_dim.11), calls=%async_computation | async-start | bytes 262144 | tf_op jit(solution)/shard_map/all_to_all | solution.py:55
  41.6 1.0 constant_dynamic-slice_fusion.5
  42.6 2.5 %collective-permute-start.1 = (bf16[256,256]{1,0:T(8,128)(2,1)S(1)}, bf16[256,256]{1,0:T(8,128)(2,1)S(1)}, u32[]{:S(2)}, u32[]{:S(2)}) collective-permute-start(bf16[256,256]{1,0:T(8,128)(2,1)S(1)} %get-tuple-element.29), channel_id=1, source_target_pairs={{0,1},{1,0},{2,3},{3,2},{4,5},{5,4},{6,7},{7,6},{8,9},{9,8},{10,11... | collective-permute-start | bytes 393224 | tf_op jit(solution)/shard_map/ppermute | solution.py:36
  45.1 1.7 %constant_dynamic-update-slice_fusion.1 = bf16[512,4096]{1,0:T(8,128)(2,1)S(1)} fusion(bf16[256,4096]{1,0:T(8,128)(2,1)} %param.4), kind=kLoop, calls=%fused_computation.25 | loop fusion | bytes 4194304
  47.0 1.3 fusion
  49.2 0.9 dynamic-slice_bitcast_fusion.2
  50.1 4.4 %collective-permute-start.4 = (bf16[4,256,256]{2,1,0:T(8,128)(2,1)}, bf16[4,256,256]{2,1,0:T(8,128)(2,1)}, u32[]{:S(2)}, u32[]{:S(2)}) collective-permute-start(bf16[4,256,256]{2,1,0:T(8,128)(2,1)} %get-tuple-element.21), channel_id=1, source_target_pairs={{0,520},{8,0},{512,8},{520,512},{1,521},{9,1},{513,9},{521,513},{2... | collective-permute-start | bytes 1572872 | tf_op jit(solution)/shard_map/ppermute | solution.py:13
  54.5 1.9 %collective-permute-start.3 = (bf16[4,256,256]{2,1,0:T(8,128)(2,1)S(1)}, bf16[4,256,256]{2,1,0:T(8,128)(2,1)}, u32[]{:S(2)}, u32[]{:S(2)}) collective-permute-start(bf16[4,256,256]{2,1,0:T(8,128)(2,1)S(1)} %get-tuple-element.22), channel_id=1, source_target_pairs={{0,8},{8,512},{512,520},{520,0},{1,9},{9,513},{513,521},{521,1},{2... | collective-permute-start | bytes 1572872 | tf_op jit(solution)/shard_map/ppermute | solution.py:13
  56.4 3.6 %collective-permute-start.2 = (bf16[4,256,256]{2,1,0:T(8,128)(2,1)S(1)}, bf16[4,256,256]{2,1,0:T(8,128)(2,1)}, u32[]{:S(2)}, u32[]{:S(2)}) collective-permute-start(bf16[4,256,256]{2,1,0:T(8,128)(2,1)S(1)} %get-tuple-element.20), channel_id=1, source_target_pairs={{0,512},{8,520},{512,0},{520,8},{1,513},{9,521},{513,1},{521,9},{2... | collective-permute-start | bytes 1572872 | tf_op jit(solution)/shard_map/ppermute | solution.py:13
  60.1 17.1 %collective-permute-done.4 = bf16[4,256,256]{2,1,0:T(8,128)(2,1)} collective-permute-done((bf16[4,256,256]{2,1,0:T(8,128)(2,1)}, bf16[4,256,256]{2,1,0:T(8,128)(2,1)}, u32[]{:S(2)}, u32[]{:S(2)}) %collective-permute-start.4) | collective-permute-done | bytes 524320 | tf_op jit(solution)/shard_map/ppermute | solution.py:13
  77.2 4.9 %collective-permute-done.3 = bf16[4,256,256]{2,1,0:T(8,128)(2,1)} collective-permute-done((bf16[4,256,256]{2,1,0:T(8,128)(2,1)S(1)}, bf16[4,256,256]{2,1,0:T(8,128)(2,1)}, u32[]{:S(2)}, u32[]{:S(2)}) %collective-permute-start.3) | collective-permute-done | bytes 524320 | tf_op jit(solution)/shard_map/ppermute | solution.py:13
  82.2 1.6 %fusion.3 = bf16[4,256,256]{2,1,0:T(8,128)(2,1)S(1)} fusion(bf16[4,256,256]{2,1,0:T(8,128)(2,1)} %collective-permute-done.4, bf16[4,256,256]{2,1,0:T(8,128)(2,1)} %collective-permute-done.3, bf16[4,256,256]{2,1,0:T(8,128)(2,1)} %collective-permute-done.2, bf16[4,4,256,256]{3,2,1,0:T(8,128)(2,1)S(1)} %bitcast.38, s32[]{:T(128)S(6)} %select_n.85), kind=kLoop, calls=%fused_computation.9 | loop fusion | flops 2097152 | bytes 2621444 | tf_op jit(solution)/shard_map/convert_element_type | solution.py:62
  83.9 17.4 %all_to_all.20 = bf16[4,512,256]{2,1,0:T(8,128)(2,1)S(1)} all-to-all(bf16[4,512,256]{2,1,0:T(8,128)(2,1)S(1)} %pad_maximum_fusion.2), channel_id=1, replica_groups=mesh['xh'=2,'z'=32,'xl'=2,'y'=4,'c'=2] {'y'}, dimensions={0} | all-to-all | bytes 2097152 | tf_op jit(solution)/shard_map/all_to_all | solution.py:67
  101.3 0.8 slice_bitcast_fusion
  102.1 3.9 %all-to-all-start.2 = ((bf16[32,8,256]{2,1,0:T(8,128)(2,1)}), bf16[32,8,256]{2,1,0:T(8,128)(2,1)S(1)}, u32[]{:S(2)}, u32[]{:S(2)}) async-start(bf16[32,8,256]{2,1,0:T(8,128)(2,1)} %bitcast.11), calls=%async_computation.2 | async-start | bytes 262144 | tf_op jit(solution)/shard_map/all_to_all | solution.py:71
  106.0 3.1 %collective-permute-start.5 = (bf16[4,256,256]{2,1,0:T(8,128)(2,1)S(1)}, bf16[4,256,256]{2,1,0:T(8,128)(2,1)S(1)}, u32[]{:S(2)}, u32[]{:S(2)}) collective-permute-start(bf16[4,256,256]{2,1,0:T(8,128)(2,1)S(1)} %get-tuple-element.25), channel_id=1, source_target_pairs={{0,512},{8,520},{512,0},{520,8},{1,513},{9,521},{513,1},{521,9},{2... | collective-permute-start | bytes 1572872 | tf_op jit(solution)/shard_map/ppermute | solution.py:13
  109.1 1.9 %collective-permute-start.6 = (bf16[4,256,256]{2,1,0:T(8,128)(2,1)S(1)}, bf16[4,256,256]{2,1,0:T(8,128)(2,1)S(1)}, u32[]{:S(2)}, u32[]{:S(2)}) collective-permute-start(bf16[4,256,256]{2,1,0:T(8,128)(2,1)S(1)} %get-tuple-element.25), channel_id=1, source_target_pairs={{0,8},{8,512},{512,520},{520,0},{1,9},{9,513},{513,521},{521,1},{2... | collective-permute-start | bytes 1572872 | tf_op jit(solution)/shard_map/ppermute | solution.py:13
  111.0 4.6 %collective-permute-start.7 = (bf16[4,256,256]{2,1,0:T(8,128)(2,1)S(1)}, bf16[4,256,256]{2,1,0:T(8,128)(2,1)S(1)}, u32[]{:S(2)}, u32[]{:S(2)}) collective-permute-start(bf16[4,256,256]{2,1,0:T(8,128)(2,1)S(1)} %get-tuple-element.25), channel_id=1, source_target_pairs={{0,520},{8,0},{512,8},{520,512},{1,521},{9,1},{513,9},{521,513},{2... | collective-permute-start | bytes 1572872 | tf_op jit(solution)/shard_map/ppermute | solution.py:13
  115.7 4.5 %collective-permute-done.5 = bf16[4,256,256]{2,1,0:T(8,128)(2,1)S(1)} collective-permute-done((bf16[4,256,256]{2,1,0:T(8,128)(2,1)S(1)}, bf16[4,256,256]{2,1,0:T(8,128)(2,1)S(1)}, u32[]{:S(2)}, u32[]{:S(2)}) %collective-permute-start.5) | collective-permute-done | bytes 524320 | tf_op jit(solution)/shard_map/ppermute | solution.py:13
  120.2 14.2 %collective-permute-done.6 = bf16[4,256,256]{2,1,0:T(8,128)(2,1)S(1)} collective-permute-done((bf16[4,256,256]{2,1,0:T(8,128)(2,1)S(1)}, bf16[4,256,256]{2,1,0:T(8,128)(2,1)S(1)}, u32[]{:S(2)}, u32[]{:S(2)}) %collective-permute-start.6) | collective-permute-done | bytes 524320 | tf_op jit(solution)/shard_map/ppermute | solution.py:13
  135.5 1.9 %copy-done.1 = bf16[512,4096]{1,0:T(8,128)(2,1)S(1)} copy-done((bf16[512,4096]{1,0:T(8,128)(2,1)S(1)}, bf16[512,4096]{1,0:T(8,128)(2,1)}, u32[]{:S(2)}) %copy-start.1) | copy-done | bytes 4194328
  137.4 1.3 convolution_convert_fusion
  138.7 5.9 %collective-permute-start.8 = (bf16[256,256]{0,1:T(8,128)(2,1)S(1)}, bf16[256,256]{0,1:T(8,128)(2,1)S(1)}, u32[]{:S(2)}, u32[]{:S(2)}) collective-permute-start(bf16[256,256]{0,1:T(8,128)(2,1)S(1)} %slice.31), channel_id=1, source_target_pairs={{0,1},{1,0},{2,3},{3,2},{4,5},{5,4},{6,7},{7,6},{8,9},{9,8},{10,11... | collective-permute-start | bytes 393224 | tf_op jit(solution)/shard_map/ppermute | solution.py:88
  144.7 0.6 broadcast_in_dim.26
  145.3 3.3 %all-to-all-start.3 = ((f32[8,8,256]{2,1,0:T(8,128)}), f32[8,8,256]{2,1,0:T(8,128)S(1)}, u32[]{:S(2)}, u32[]{:S(2)}) async-start(f32[8,8,256]{2,1,0:T(8,128)} %broadcast_in_dim.26), calls=%async_computation.3 | async-start | bytes 131072 | tf_op jit(solution)/shard_map/all_to_all | solution.py:77
  148.6 4.8 %all-to-all-done.3 = f32[8,8,256]{2,1,0:T(8,128)S(1)} async-done(((f32[8,8,256]{2,1,0:T(8,128)}), f32[8,8,256]{2,1,0:T(8,128)S(1)}, u32[]{:S(2)}, u32[]{:S(2)}) %all-to-all-start.3) | async-done | bytes 65568 | tf_op jit(solution)/shard_map/all_to_all | solution.py:77
  153.5 0.8 copy.12
  154.3 0.6 copy.15
  (24 shorter events, 2.2 us)
Async XLA Ops:
  0.6 46.2 %collective-permute-start = (bf16[256,4096]{1,0:T(8,128)(2,1)}, bf16[256,4096]{1,0:T(8,128)(2,1)S(1)}, u32[]{:S(2)}, u32[]{:S(2)}) collective-permute-start(bf16[256,4096]{1,0:T(8,128)(2,1)} %param.4), channel_id=1, source_target_pairs={{0,1},{1,0},{2,3},{3,2},{4,5},{5,4},{6,7},{7,6},{8,9},{9,8},{10,11... | collective-permute-start | bytes 6291464 | tf_op jit(solution)/shard_map/ppermute | solution.py:33
  18.9 41.2 %all-to-all-start = ((bf16[32,8,256]{2,1,0:T(8,128)(2,1)}), bf16[32,8,256]{2,1,0:T(8,128)(2,1)S(1)}, u32[]{:S(2)}, u32[]{:S(2)}) async-start(bf16[32,8,256]{2,1,0:T(8,128)(2,1)} %broadcast_in_dim.11), calls=%async_computation | async-start | bytes 262144 | tf_op jit(solution)/shard_map/all_to_all | solution.py:55
  42.6 4.4 %collective-permute-start.1 = (bf16[256,256]{1,0:T(8,128)(2,1)S(1)}, bf16[256,256]{1,0:T(8,128)(2,1)S(1)}, u32[]{:S(2)}, u32[]{:S(2)}) collective-permute-start(bf16[256,256]{1,0:T(8,128)(2,1)S(1)} %get-tuple-element.29), channel_id=1, source_target_pairs={{0,1},{1,0},{2,3},{3,2},{4,5},{5,4},{6,7},{7,6},{8,9},{9,8},{10,11... | collective-permute-start | bytes 393224 | tf_op jit(solution)/shard_map/ppermute | solution.py:36
  47.0 2.0 %copy-start = (bf16[512,4096]{1,0:T(8,128)(2,1)}, bf16[512,4096]{1,0:T(8,128)(2,1)S(1)}, u32[]{:S(2)}) copy-start(bf16[512,4096]{1,0:T(8,128)(2,1)S(1)} %constant_dynamic-update-slice_fusion) | copy-start | bytes 12582916
  50.1 27.1 %collective-permute-start.4 = (bf16[4,256,256]{2,1,0:T(8,128)(2,1)}, bf16[4,256,256]{2,1,0:T(8,128)(2,1)}, u32[]{:S(2)}, u32[]{:S(2)}) collective-permute-start(bf16[4,256,256]{2,1,0:T(8,128)(2,1)} %get-tuple-element.21), channel_id=1, source_target_pairs={{0,520},{8,0},{512,8},{520,512},{1,521},{9,1},{513,9},{521,513},{2... | collective-permute-start | bytes 1572872 | tf_op jit(solution)/shard_map/ppermute | solution.py:13
  54.5 27.7 %collective-permute-start.3 = (bf16[4,256,256]{2,1,0:T(8,128)(2,1)S(1)}, bf16[4,256,256]{2,1,0:T(8,128)(2,1)}, u32[]{:S(2)}, u32[]{:S(2)}) collective-permute-start(bf16[4,256,256]{2,1,0:T(8,128)(2,1)S(1)} %get-tuple-element.22), channel_id=1, source_target_pairs={{0,8},{8,512},{512,520},{520,0},{1,9},{9,513},{513,521},{521,1},{2... | collective-permute-start | bytes 1572872 | tf_op jit(solution)/shard_map/ppermute | solution.py:13
  56.4 25.7 %collective-permute-start.2 = (bf16[4,256,256]{2,1,0:T(8,128)(2,1)S(1)}, bf16[4,256,256]{2,1,0:T(8,128)(2,1)}, u32[]{:S(2)}, u32[]{:S(2)}) collective-permute-start(bf16[4,256,256]{2,1,0:T(8,128)(2,1)S(1)} %get-tuple-element.20), channel_id=1, source_target_pairs={{0,512},{8,520},{512,0},{520,8},{1,513},{9,521},{513,1},{521,9},{2... | collective-permute-start | bytes 1572872 | tf_op jit(solution)/shard_map/ppermute | solution.py:13
  102.1 32.4 %all-to-all-start.2 = ((bf16[32,8,256]{2,1,0:T(8,128)(2,1)}), bf16[32,8,256]{2,1,0:T(8,128)(2,1)S(1)}, u32[]{:S(2)}, u32[]{:S(2)}) async-start(bf16[32,8,256]{2,1,0:T(8,128)(2,1)} %bitcast.11), calls=%async_computation.2 | async-start | bytes 262144 | tf_op jit(solution)/shard_map/all_to_all | solution.py:71
  106.0 14.2 %collective-permute-start.5 = (bf16[4,256,256]{2,1,0:T(8,128)(2,1)S(1)}, bf16[4,256,256]{2,1,0:T(8,128)(2,1)S(1)}, u32[]{:S(2)}, u32[]{:S(2)}) collective-permute-start(bf16[4,256,256]{2,1,0:T(8,128)(2,1)S(1)} %get-tuple-element.25), channel_id=1, source_target_pairs={{0,512},{8,520},{512,0},{520,8},{1,513},{9,521},{513,1},{521,9},{2... | collective-permute-start | bytes 1572872 | tf_op jit(solution)/shard_map/ppermute | solution.py:13
  109.1 25.3 %collective-permute-start.6 = (bf16[4,256,256]{2,1,0:T(8,128)(2,1)S(1)}, bf16[4,256,256]{2,1,0:T(8,128)(2,1)S(1)}, u32[]{:S(2)}, u32[]{:S(2)}) collective-permute-start(bf16[4,256,256]{2,1,0:T(8,128)(2,1)S(1)} %get-tuple-element.25), channel_id=1, source_target_pairs={{0,8},{8,512},{512,520},{520,0},{1,9},{9,513},{513,521},{521,1},{2... | collective-permute-start | bytes 1572872 | tf_op jit(solution)/shard_map/ppermute | solution.py:13
  111.0 23.4 %collective-permute-start.7 = (bf16[4,256,256]{2,1,0:T(8,128)(2,1)S(1)}, bf16[4,256,256]{2,1,0:T(8,128)(2,1)S(1)}, u32[]{:S(2)}, u32[]{:S(2)}) collective-permute-start(bf16[4,256,256]{2,1,0:T(8,128)(2,1)S(1)} %get-tuple-element.25), channel_id=1, source_target_pairs={{0,520},{8,0},{512,8},{520,512},{1,521},{9,1},{513,9},{521,513},{2... | collective-permute-start | bytes 1572872 | tf_op jit(solution)/shard_map/ppermute | solution.py:13
  135.2 2.2 %copy-start.1 = (bf16[512,4096]{1,0:T(8,128)(2,1)S(1)}, bf16[512,4096]{1,0:T(8,128)(2,1)}, u32[]{:S(2)}) copy-start(bf16[512,4096]{1,0:T(8,128)(2,1)} %copy-done) | copy-start | bytes 12582916
  138.7 14.7 %collective-permute-start.8 = (bf16[256,256]{0,1:T(8,128)(2,1)S(1)}, bf16[256,256]{0,1:T(8,128)(2,1)S(1)}, u32[]{:S(2)}, u32[]{:S(2)}) collective-permute-start(bf16[256,256]{0,1:T(8,128)(2,1)S(1)} %slice.31), channel_id=1, source_target_pairs={{0,1},{1,0},{2,3},{3,2},{4,5},{5,4},{6,7},{7,6},{8,9},{9,8},{10,11... | collective-permute-start | bytes 393224 | tf_op jit(solution)/shard_map/ppermute | solution.py:88
  145.3 8.1 %all-to-all-start.3 = ((f32[8,8,256]{2,1,0:T(8,128)}), f32[8,8,256]{2,1,0:T(8,128)S(1)}, u32[]{:S(2)}, u32[]{:S(2)}) async-start(f32[8,8,256]{2,1,0:T(8,128)} %broadcast_in_dim.26), calls=%async_computation.3 | async-start | bytes 131072 | tf_op jit(solution)/shard_map/all_to_all | solution.py:77

commit v5 on v4

--- a/solution.py
+++ b/solution.py
@@ -11,6 +11,14 @@
 
 def around(value, shift):
     return lax.ppermute(value, X, [(i, (i + shift) % 4) for i in range(4)])
+
+
+def over_z(value):
+    n = value.shape[0]
+    turned = [[(k + n // 2) % n for k in range(n)]]
+    return lax.all_to_all(
+        value, "z", split_axis=0, concat_axis=0, axis_index_groups=turned, tiled=True
+    )
 
 
 def pick(stack, index):
@@ -50,11 +58,10 @@
     grad = grad.reshape(2, n_z, 2, 4, rows, half)
     grad = grad.transpose(0, 2, 3, 1, 4, 5).reshape(4, 4, column, half)
     sends = [pick(grad, (x + shift) % 4) for shift in (2, 1, 3)]
+    *sends, spread = lax.optimization_barrier((*sends, spread))
     parts = [around(send, shift) for send, shift in zip(sends, (2, 1, 3))]
-    turned = [[(k + n_z // 2) % n_z for k in range(n_z)]]
-    col = lax.all_to_all(
-        spread, "z", split_axis=0, concat_axis=0, axis_index_groups=turned, tiled=True
-    )
+    col = lax.cond(x >= 0, over_z, lambda held: held, spread)
+    *parts, col = lax.optimization_barrier((*parts, col))
     col = jnp.roll(col, n_z // 2, axis=0)
     total = pick(grad, x).astype(f32)
     for part in parts:
@@ -68,15 +75,7 @@
     plane = jnp.sum(both[:, :column].astype(f32), axis=0).astype(bf16)
     slab = both[:, column:]
     held = [around(slab, shift) for shift in (2, 1, 3)]
-    moved = lax.all_to_all(
-        plane.reshape(n_z, rows, half), "z", split_axis=0, concat_axis=0, tiled=True
-    )
-    *held, moved = lax.optimization_barrier((*held, moved))
-    piece = jnp.sum(moved.astype(f32), axis=0)
-    pieces = jnp.broadcast_to(piece[None], (8, rows, half))
-    pieces = lax.all_to_all(pieces, ("y", "c"), split_axis=0, concat_axis=0, tiled=True)
-    pieces = pieces.reshape(4, 2, rows, half)
-    weight_grads = pieces.transpose(0, 2, 1, 3).reshape(own, cols)
+    moved = over_z(jnp.roll(plane.reshape(n_z, rows, half), n_z // 2, axis=0))
 
     two, one, three = held
     stack = jnp.stack([slab, one, two, three])
@@ -85,6 +84,13 @@
     weight = whole.transpose(0, 3, 1, 2, 4, 5).reshape(d_in, half)
 
     proj = jnp.dot(acts, weight, preferred_element_type=f32).astype(bf16)
+    proj, moved = lax.optimization_barrier((proj, moved))
+    piece = jnp.sum(moved.astype(f32), axis=0)
+    pieces = jnp.broadcast_to(piece[None], (8, rows, half))
+    pieces = lax.all_to_all(pieces, ("y", "c"), split_axis=0, concat_axis=0, tiled=True)
+    pieces = pieces.reshape(4, 2, rows, half)
+    weight_grads = pieces.transpose(0, 2, 1, 3).reshape(own, cols)
+
     got = lax.ppermute(proj[tok:], "c", SWAP)
     kept = proj[:tok]
     left = jnp.where(c == 0, kept, got)

time: 156 us -> 147 us (0.942)
  blocking collectives: 17.4 us -> 54.9 us
  waiting for transfers between devices: 45.6 us -> 11.9 us
  starting transfers between devices: 73.9 us -> 62 us
    ppermute x6, waiting for transfers between devices: 40.8 us -> 1.4 us  [around(): return lax.ppermute(value, X, [(i, (i + shift) % 4) for i in range(4)])]
    all_to_all x0 -> x1, blocking collectives: none -> 37.3 us  [over_z(): lax.all_to_all(value, 'z', split_axis=0, concat_axis=0, axis_index_groups...]
    all_to_all x2 -> x1, waiting for transfers between devices: 0.01 us -> 5.62 us  [over_z(): lax.all_to_all(value, 'z', split_axis=0, concat_axis=0, axis_index_groups...]
    all_to_all x2 -> x1, starting transfers between devices: 26.5 us -> 21.4 us  [over_z(): lax.all_to_all(value, 'z', split_axis=0, concat_axis=0, axis_index_groups...]
    ppermute x6, starting transfers between devices: 19.6 us -> 15.6 us  [around(): return lax.ppermute(value, X, [(i, (i + shift) % 4) for i in range(4)])]
    ppermute x1, starting transfers between devices: 5.92 us -> 3.68 us  [body(): got = lax.ppermute(proj[tok:], 'c', SWAP)]
    unnamed x7 -> x6, local copies, waits for them, and re-layouts: 5.72 us -> 4.87 us
  transfers between devices with their start and end apart: 12 -> 11, of which waited for: 5 -> 3; matrix products, arithmetic and copies ran while one was open for 5% -> 5% of each run, Pallas kernels for 0% -> 0%
where the time goes in v5:
time: 147 us; the launch traced here: 146 us
  starting transfers between devices  62 us (42%)
  blocking collectives  54.9 us (37%)
  waiting for transfers between devices  11.9 us (8%)
  local copies, waits for them, and re-layouts  8.31 us (6%)
  other arithmetic  5.29 us (4%)
  matrix products  2.57 us (2%)
    all_to_all x1, blocking collectives, over_z(): lax.all_to_all(value, 'z', split_axis=0, concat_axis=0, axis_index_groups...  37.3 us
    all_to_all x1, starting transfers between devices, over_z(): lax.all_to_all(value, 'z', split_axis=0, concat_axis=0, axis_index_groups...  21.4 us
    all_to_all x1, blocking collectives, body(): both = lax.all_to_all(both, 'y', split_axis=0, concat_axis=0, tiled=True)  17.5 us
    ppermute x1, starting transfers between devices, body(): other_act = lax.ppermute(activations, 'c', SWAP)  16.1 us
    ppermute x6, starting transfers between devices, around(): return lax.ppermute(value, X, [(i, (i + shift) % 4) for i in range(4)])  15.6 us
    all_to_all x1, waiting for transfers between devices, over_z(): lax.all_to_all(value, 'z', split_axis=0, concat_axis=0, axis_index_groups...  5.62 us
    unnamed x6, local copies, waits for them, and re-layouts  4.87 us
    all_to_all x1, waiting for transfers between devices, body(): lax.all_to_all(pieces, ('y', 'c'), split_axis=0, concat_axis=0, tiled=True)  4.82 us
  transfers between devices with their start and end apart: 11, of which 3 were waited for; matrix products, arithmetic and copies ran while one was open for 5% of the time, Pallas kernels for 0%

profile of v5, /device:TPU:1, one launch (start us, length us, event | category | flops | bytes accessed | tf_op | source)
XLA Modules:
  0.0 146.0 jit_solution(1196516567670444429)
XLA Ops:
  0.6 16.1 %collective-permute-start = (bf16[256,4096]{1,0:T(8,128)(2,1)}, bf16[256,4096]{1,0:T(8,128)(2,1)S(1)}, u32[]{:S(2)}, u32[]{:S(2)}) collective-permute-start(bf16[256,4096]{1,0:T(8,128)(2,1)} %param.6), channel_id=1, source_target_pairs={{0,1},{1,0},{2,3},{3,2},{4,5},{5,4},{6,7},{7,6},{8,9},{9,8},{10,11... | collective-permute-start | bytes 6291464 | tf_op jit(solution)/shard_map/ppermute | solution.py:41
  16.7 1.0 constant_dynamic-slice_fusion.5
  17.7 1.9 %collective-permute-start.1 = (bf16[256,256]{1,0:T(8,128)(2,1)S(1)}, bf16[256,256]{1,0:T(8,128)(2,1)S(1)}, u32[]{:S(2)}, u32[]{:S(2)}) collective-permute-start(bf16[256,256]{1,0:T(8,128)(2,1)S(1)} %get-tuple-element.40), channel_id=1, source_target_pairs={{0,1},{1,0},{2,3},{3,2},{4,5},{5,4},{6,7},{7,6},{8,9},{9,8},{10,11... | collective-permute-start | bytes 393224 | tf_op jit(solution)/shard_map/ppermute | solution.py:44
  19.7 0.8 dynamic-slice_convert_fusion
  20.4 0.8 fusion.7
  21.2 1.7 %constant_dynamic-update-slice_fusion.1 = bf16[512,4096]{1,0:T(8,128)(2,1)S(1)} fusion(bf16[256,4096]{1,0:T(8,128)(2,1)} %param.6), kind=kLoop, calls=%fused_computation.28 | loop fusion | bytes 4194304
  23.1 1.3 fusion
  24.4 0.6 copy-done
  25.3 0.9 dynamic-slice_bitcast_fusion
  26.2 1.9 %collective-permute-start.2 = (bf16[4,256,256]{2,1,0:T(8,128)(2,1)}, bf16[4,256,256]{2,1,0:T(8,128)(2,1)}, u32[]{:S(2)}, u32[]{:S(2)}) collective-permute-start(bf16[4,256,256]{2,1,0:T(8,128)(2,1)} %get-tuple-element.17), channel_id=1, source_target_pairs={{0,512},{8,520},{512,0},{520,8},{1,513},{9,521},{513,1},{521,9},{2... | collective-permute-start | bytes 1572872 | tf_op jit(solution)/shard_map/ppermute | solution.py:13
  28.1 1.9 %collective-permute-start.3 = (bf16[4,256,256]{2,1,0:T(8,128)(2,1)S(1)}, bf16[4,256,256]{2,1,0:T(8,128)(2,1)}, u32[]{:S(2)}, u32[]{:S(2)}) collective-permute-start(bf16[4,256,256]{2,1,0:T(8,128)(2,1)S(1)} %get-tuple-element.18), channel_id=1, source_target_pairs={{0,8},{8,512},{512,520},{520,0},{1,9},{9,513},{513,521},{521,1},{2... | collective-permute-start | bytes 1572872 | tf_op jit(solution)/shard_map/ppermute | solution.py:13
  30.1 4.6 %collective-permute-start.4 = (bf16[4,256,256]{2,1,0:T(8,128)(2,1)S(1)}, bf16[4,256,256]{2,1,0:T(8,128)(2,1)}, u32[]{:S(2)}, u32[]{:S(2)}) collective-permute-start(bf16[4,256,256]{2,1,0:T(8,128)(2,1)S(1)} %get-tuple-element.19), channel_id=1, source_target_pairs={{0,520},{8,0},{512,8},{520,512},{1,521},{9,1},{513,9},{521,513},{2... | collective-permute-start | bytes 1572872 | tf_op jit(solution)/shard_map/ppermute | solution.py:13
  34.6 37.4 %conditional.1 = (bf16[32,8,256]{2,1,0:T(8,128)(2,1)S(1)}) conditional(s32[]{:T(128)} %convert_element_type.47, bf16[32,8,256]{2,1,0:T(8,128)(2,1)S(1)} %broadcast_in_dim.11, bf16[32,8,256]{2,1,0:T(8,128)(2,1)S(1)} %broadcast_in_dim.11), branch_computations={%region_0.1_spmd, %region_1.2_spmd} | conditional | bytes 524296 | solution.py:63
  34.7 37.3 %all_to_all.19 = bf16[32,8,256]{2,1,0:T(8,128)(2,1)S(1)} all-to-all(bf16[32,8,256]{2,1,0:T(8,128)(2,1)S(1)} %copy.14), channel_id=1, replica_groups={{256,272,288,304,320,336,352,368,384,400,416,432,448,464,480,496,0,16,3..., dimensions={0} | all-to-all | bytes 262144 | tf_op jit(solution)/shard_map/cond/branch_1_fun/all_to_all | solution.py:19
  72.0 1.6 %fusion.3 = bf16[4,256,256]{2,1,0:T(8,128)(2,1)S(1)} fusion(bf16[4,256,256]{2,1,0:T(8,128)(2,1)} %collective-permute-done.4, bf16[4,256,256]{2,1,0:T(8,128)(2,1)} %collective-permute-done.3, bf16[4,256,256]{2,1,0:T(8,128)(2,1)} %collective-permute-done.2, bf16[4,4,256,256]{3,2,1,0:T(8,128)(2,1)S(1)} %bitcast.41, s32[]{:T(128)S(6)} %select_n.85), kind=kLoop, calls=%fused_computation.9 | loop fusion | flops 2097152 | bytes 2621444 | tf_op jit(solution)/shard_map/convert_element_type | solution.py:69
  73.8 17.5 %all_to_all.20 = bf16[4,512,256]{2,1,0:T(8,128)(2,1)S(1)} all-to-all(bf16[4,512,256]{2,1,0:T(8,128)(2,1)S(1)} %pad_maximum_fusion.2), channel_id=1, replica_groups=mesh['xh'=2,'z'=32,'xl'=2,'y'=4,'c'=2] {'y'}, dimensions={0} | all-to-all | bytes 2097152 | tf_op jit(solution)/shard_map/all_to_all | solution.py:74
  91.4 2.3 %collective-permute-start.7 = (bf16[4,256,256]{2,1,0:T(8,128)(2,1)S(1)}, bf16[4,256,256]{2,1,0:T(8,128)(2,1)S(1)}, u32[]{:S(2)}, u32[]{:S(2)}) collective-permute-start(bf16[4,256,256]{2,1,0:T(8,128)(2,1)S(1)} %get-tuple-element.36), channel_id=1, source_target_pairs={{0,520},{8,0},{512,8},{520,512},{1,521},{9,1},{513,9},{521,513},{2... | collective-permute-start | bytes 1572872 | tf_op jit(solution)/shard_map/ppermute | solution.py:13
  93.8 2.4 %collective-permute-start.6 = (bf16[4,256,256]{2,1,0:T(8,128)(2,1)S(1)}, bf16[4,256,256]{2,1,0:T(8,128)(2,1)S(1)}, u32[]{:S(2)}, u32[]{:S(2)}) collective-permute-start(bf16[4,256,256]{2,1,0:T(8,128)(2,1)S(1)} %get-tuple-element.36), channel_id=1, source_target_pairs={{0,512},{8,520},{512,0},{520,8},{1,513},{9,521},{513,1},{521,9},{2... | collective-permute-start | bytes 1572872 | tf_op jit(solution)/shard_map/ppermute | solution.py:13
  96.2 2.5 %collective-permute-start.5 = (bf16[4,256,256]{2,1,0:T(8,128)(2,1)S(1)}, bf16[4,256,256]{2,1,0:T(8,128)(2,1)S(1)}, u32[]{:S(2)}, u32[]{:S(2)}) collective-permute-start(bf16[4,256,256]{2,1,0:T(8,128)(2,1)S(1)} %get-tuple-element.36), channel_id=1, source_target_pairs={{0,8},{8,512},{512,520},{520,0},{1,9},{9,513},{513,521},{521,1},{2... | collective-permute-start | bytes 1572872 | tf_op jit(solution)/shard_map/ppermute | solution.py:13
  98.7 0.7 pad_maximum_fusion.4
  99.4 21.4 %all-to-all-start.2 = ((bf16[32,8,256]{2,1,0:T(8,128)(2,1)}), bf16[32,8,256]{2,1,0:T(8,128)(2,1)S(1)}, u32[]{:S(2)}, u32[]{:S(2)}) async-start(bf16[32,8,256]{2,1,0:T(8,128)(2,1)} %pad_maximum_fusion.4), calls=%async_computation.2 | async-start | bytes 262144 | tf_op jit(solution)/shard_map/all_to_all | solution.py:19
  120.9 1.4 collective-permute-done.5
  123.0 0.3 copy.9
  123.3 1.9 %copy-done.1 = bf16[512,4096]{1,0:T(8,128)(2,1)S(1)} copy-done((bf16[512,4096]{1,0:T(8,128)(2,1)S(1)}, bf16[512,4096]{1,0:T(8,128)(2,1)}, u32[]{:S(2)}) %copy-start.1) | copy-done | bytes 4194328
  125.2 1.2 convolution_convert_fusion
  126.4 5.6 %all-to-all-done.2 = bf16[32,8,256]{2,1,0:T(8,128)(2,1)S(1)} async-done(((bf16[32,8,256]{2,1,0:T(8,128)(2,1)}), bf16[32,8,256]{2,1,0:T(8,128)(2,1)S(1)}, u32[]{:S(2)}, u32[]{:S(2)}) %all-to-all-start.2) | async-done | bytes 131104 | tf_op jit(solution)/shard_map/all_to_all | solution.py:19
  132.1 3.7 %collective-permute-start.8 = (bf16[256,256]{1,0:T(8,128)(2,1)S(1)}, bf16[256,256]{1,0:T(8,128)(2,1)S(1)}, u32[]{:S(2)}, u32[]{:S(2)}) collective-permute-start(bf16[256,256]{1,0:T(8,128)(2,1)S(1)} %slice.41), channel_id=1, source_target_pairs={{0,1},{1,0},{2,3},{3,2},{4,5},{5,4},{6,7},{7,6},{8,9},{9,8},{10,11... | collective-permute-start | bytes 393224 | tf_op jit(solution)/shard_map/ppermute | solution.py:94
  135.8 0.6 broadcast_in_dim.26
  136.5 3.3 %all-to-all-start.3 = ((f32[8,8,256]{2,1,0:T(8,128)}), f32[8,8,256]{2,1,0:T(8,128)S(1)}, u32[]{:S(2)}, u32[]{:S(2)}) async-start(f32[8,8,256]{2,1,0:T(8,128)} %broadcast_in_dim.26), calls=%async_computation.3 | async-start | bytes 131072 | tf_op jit(solution)/shard_map/all_to_all | solution.py:90
  139.8 4.8 %all-to-all-done.3 = f32[8,8,256]{2,1,0:T(8,128)S(1)} async-done(((f32[8,8,256]{2,1,0:T(8,128)}), f32[8,8,256]{2,1,0:T(8,128)S(1)}, u32[]{:S(2)}, u32[]{:S(2)}) %all-to-all-start.3) | async-done | bytes 65568 | tf_op jit(solution)/shard_map/all_to_all | solution.py:90
  144.6 0.7 pad_maximum_fusion.3
  145.3 0.6 copy.15
  (26 shorter events, 1.4 us)
Async XLA Ops:
  0.6 22.3 %collective-permute-start = (bf16[256,4096]{1,0:T(8,128)(2,1)}, bf16[256,4096]{1,0:T(8,128)(2,1)S(1)}, u32[]{:S(2)}, u32[]{:S(2)}) collective-permute-start(bf16[256,4096]{1,0:T(8,128)(2,1)} %param.6), channel_id=1, source_target_pairs={{0,1},{1,0},{2,3},{3,2},{4,5},{5,4},{6,7},{7,6},{8,9},{9,8},{10,11... | collective-permute-start | bytes 6291464 | tf_op jit(solution)/shard_map/ppermute | solution.py:41
  17.7 5.4 %collective-permute-start.1 = (bf16[256,256]{1,0:T(8,128)(2,1)S(1)}, bf16[256,256]{1,0:T(8,128)(2,1)S(1)}, u32[]{:S(2)}, u32[]{:S(2)}) collective-permute-start(bf16[256,256]{1,0:T(8,128)(2,1)S(1)} %get-tuple-element.40), channel_id=1, source_target_pairs={{0,1},{1,0},{2,3},{3,2},{4,5},{5,4},{6,7},{7,6},{8,9},{9,8},{10,11... | collective-permute-start | bytes 393224 | tf_op jit(solution)/shard_map/ppermute | solution.py:44
  23.1 2.0 %copy-start = (bf16[512,4096]{1,0:T(8,128)(2,1)}, bf16[512,4096]{1,0:T(8,128)(2,1)S(1)}, u32[]{:S(2)}) copy-start(bf16[512,4096]{1,0:T(8,128)(2,1)S(1)} %constant_dynamic-update-slice_fusion) | copy-start | bytes 12582916
  26.2 45.8 %collective-permute-start.2 = (bf16[4,256,256]{2,1,0:T(8,128)(2,1)}, bf16[4,256,256]{2,1,0:T(8,128)(2,1)}, u32[]{:S(2)}, u32[]{:S(2)}) collective-permute-start(bf16[4,256,256]{2,1,0:T(8,128)(2,1)} %get-tuple-element.17), channel_id=1, source_target_pairs={{0,512},{8,520},{512,0},{520,8},{1,513},{9,521},{513,1},{521,9},{2... | collective-permute-start | bytes 1572872 | tf_op jit(solution)/shard_map/ppermute | solution.py:13
  28.1 43.9 %collective-permute-start.3 = (bf16[4,256,256]{2,1,0:T(8,128)(2,1)S(1)}, bf16[4,256,256]{2,1,0:T(8,128)(2,1)}, u32[]{:S(2)}, u32[]{:S(2)}) collective-permute-start(bf16[4,256,256]{2,1,0:T(8,128)(2,1)S(1)} %get-tuple-element.18), channel_id=1, source_target_pairs={{0,8},{8,512},{512,520},{520,0},{1,9},{9,513},{513,521},{521,1},{2... | collective-permute-start | bytes 1572872 | tf_op jit(solution)/shard_map/ppermute | solution.py:13
  30.1 42.0 %collective-permute-start.4 = (bf16[4,256,256]{2,1,0:T(8,128)(2,1)S(1)}, bf16[4,256,256]{2,1,0:T(8,128)(2,1)}, u32[]{:S(2)}, u32[]{:S(2)}) collective-permute-start(bf16[4,256,256]{2,1,0:T(8,128)(2,1)S(1)} %get-tuple-element.19), channel_id=1, source_target_pairs={{0,520},{8,0},{512,8},{520,512},{1,521},{9,1},{513,9},{521,513},{2... | collective-permute-start | bytes 1572872 | tf_op jit(solution)/shard_map/ppermute | solution.py:13
  91.4 29.4 %collective-permute-start.7 = (bf16[4,256,256]{2,1,0:T(8,128)(2,1)S(1)}, bf16[4,256,256]{2,1,0:T(8,128)(2,1)S(1)}, u32[]{:S(2)}, u32[]{:S(2)}) collective-permute-start(bf16[4,256,256]{2,1,0:T(8,128)(2,1)S(1)} %get-tuple-element.36), channel_id=1, source_target_pairs={{0,520},{8,0},{512,8},{520,512},{1,521},{9,1},{513,9},{521,513},{2... | collective-permute-start | bytes 1572872 | tf_op jit(solution)/shard_map/ppermute | solution.py:13
  93.8 27.1 %collective-permute-start.6 = (bf16[4,256,256]{2,1,0:T(8,128)(2,1)S(1)}, bf16[4,256,256]{2,1,0:T(8,128)(2,1)S(1)}, u32[]{:S(2)}, u32[]{:S(2)}) collective-permute-start(bf16[4,256,256]{2,1,0:T(8,128)(2,1)S(1)} %get-tuple-element.36), channel_id=1, source_target_pairs={{0,512},{8,520},{512,0},{520,8},{1,513},{9,521},{513,1},{521,9},{2... | collective-permute-start | bytes 1572872 | tf_op jit(solution)/shard_map/ppermute | solution.py:13
  96.2 26.1 %collective-permute-start.5 = (bf16[4,256,256]{2,1,0:T(8,128)(2,1)S(1)}, bf16[4,256,256]{2,1,0:T(8,128)(2,1)S(1)}, u32[]{:S(2)}, u32[]{:S(2)}) collective-permute-start(bf16[4,256,256]{2,1,0:T(8,128)(2,1)S(1)} %get-tuple-element.36), channel_id=1, source_target_pairs={{0,8},{8,512},{512,520},{520,0},{1,9},{9,513},{513,521},{521,1},{2... | collective-permute-start | bytes 1572872 | tf_op jit(solution)/shard_map/ppermute | solution.py:13
  99.4 32.7 %all-to-all-start.2 = ((bf16[32,8,256]{2,1,0:T(8,128)(2,1)}), bf16[32,8,256]{2,1,0:T(8,128)(2,1)S(1)}, u32[]{:S(2)}, u32[]{:S(2)}) async-start(bf16[32,8,256]{2,1,0:T(8,128)(2,1)} %pad_maximum_fusion.4), calls=%async_computation.2 | async-start | bytes 262144 | tf_op jit(solution)/shard_map/all_to_all | solution.py:19
  123.0 2.2 %copy-start.1 = (bf16[512,4096]{1,0:T(8,128)(2,1)S(1)}, bf16[512,4096]{1,0:T(8,128)(2,1)}, u32[]{:S(2)}) copy-start(bf16[512,4096]{1,0:T(8,128)(2,1)} %copy-done) | copy-start | bytes 12582916
  132.1 12.5 %collective-permute-start.8 = (bf16[256,256]{1,0:T(8,128)(2,1)S(1)}, bf16[256,256]{1,0:T(8,128)(2,1)S(1)}, u32[]{:S(2)}, u32[]{:S(2)}) collective-permute-start(bf16[256,256]{1,0:T(8,128)(2,1)S(1)} %slice.41), channel_id=1, source_target_pairs={{0,1},{1,0},{2,3},{3,2},{4,5},{5,4},{6,7},{7,6},{8,9},{9,8},{10,11... | collective-permute-start | bytes 393224 | tf_op jit(solution)/shard_map/ppermute | solution.py:94
  136.5 8.1 %all-to-all-start.3 = ((f32[8,8,256]{2,1,0:T(8,128)}), f32[8,8,256]{2,1,0:T(8,128)S(1)}, u32[]{:S(2)}, u32[]{:S(2)}) async-start(f32[8,8,256]{2,1,0:T(8,128)} %broadcast_in_dim.26), calls=%async_computation.3 | async-start | bytes 131072 | tf_op jit(solution)/shard_map/all_to_all | solution.py:90

commit v6 on v5

--- a/solution.py
+++ b/solution.py
@@ -9,8 +9,17 @@
 SWAP = [(0, 1), (1, 0)]
 
 
-def around(value, shift):
-    return lax.ppermute(value, X, [(i, (i + shift) % 4) for i in range(4)])
+def around(value, axes, shift):
+    return lax.ppermute(value, axes, [(i, (i + shift) % 4) for i in range(4)])
+
+
+def spread_sum(stack, axes):
+    me = lax.axis_index(axes)
+    parts = [around(pick(stack, (me + shift) % 4), axes, shift) for shift in (2, 1, 3)]
+    total = pick(stack, me).astype(jnp.float32)
+    for part in parts:
+        total += part.astype(jnp.float32)
+    return total.astype(stack.dtype)
 
 
 def over_z(value):
@@ -57,24 +66,16 @@
     grad = (grad * factor).astype(bf16)
     grad = grad.reshape(2, n_z, 2, 4, rows, half)
     grad = grad.transpose(0, 2, 3, 1, 4, 5).reshape(4, 4, column, half)
-    sends = [pick(grad, (x + shift) % 4) for shift in (2, 1, 3)]
-    *sends, spread = lax.optimization_barrier((*sends, spread))
-    parts = [around(send, shift) for send, shift in zip(sends, (2, 1, 3))]
-    col = lax.cond(x >= 0, over_z, lambda held: held, spread)
-    *parts, col = lax.optimization_barrier((*parts, col))
+    grad, spread = lax.optimization_barrier((grad, spread))
+    col = over_z(spread)
+    plane = spread_sum(spread_sum(grad, X), "y")
+    col, plane = lax.optimization_barrier((col, plane))
     col = jnp.roll(col, n_z // 2, axis=0)
-    total = pick(grad, x).astype(f32)
-    for part in parts:
-        total += part.astype(f32)
-    line = total.astype(bf16)
 
-    both = jnp.concatenate(
-        [line, jnp.broadcast_to(col.reshape(1, column, half), (4, column, half))], axis=1
-    )
-    both = lax.all_to_all(both, "y", split_axis=0, concat_axis=0, tiled=True)
-    plane = jnp.sum(both[:, :column].astype(f32), axis=0).astype(bf16)
-    slab = both[:, column:]
-    held = [around(slab, shift) for shift in (2, 1, 3)]
+    slab = jnp.broadcast_to(col.reshape(1, column, half), (4, column, half))
+    slab = lax.all_to_all(slab, "y", split_axis=0, concat_axis=0, tiled=True)
+    slab, plane = lax.optimization_barrier((slab, plane))
+    held = [around(slab, X, shift) for shift in (2, 1, 3)]
     moved = over_z(jnp.roll(plane.reshape(n_z, rows, half), n_z // 2, axis=0))
 
     two, one, three = held
@@ -84,15 +85,15 @@
     weight = whole.transpose(0, 3, 1, 2, 4, 5).reshape(d_in, half)
 
     proj = jnp.dot(acts, weight, preferred_element_type=f32).astype(bf16)
-    proj, moved = lax.optimization_barrier((proj, moved))
+    got = lax.ppermute(proj[tok:], "c", SWAP)
+    kept = proj[:tok]
+    got, kept, moved = lax.optimization_barrier((got, kept, moved))
     piece = jnp.sum(moved.astype(f32), axis=0)
     pieces = jnp.broadcast_to(piece[None], (8, rows, half))
     pieces = lax.all_to_all(pieces, ("y", "c"), split_axis=0, concat_axis=0, tiled=True)
     pieces = pieces.reshape(4, 2, rows, half)
     weight_grads = pieces.transpose(0, 2, 1, 3).reshape(own, cols)
 
-    got = lax.ppermute(proj[tok:], "c", SWAP)
-    kept = proj[:tok]
     left = jnp.where(c == 0, kept, got)
     right = jnp.where(c == 0, got, kept)
     projected = jnp.concatenate([left, right], axis=1)

time: 147 us -> 141 us (0.959)
  blocking collectives: 54.9 us -> 9.77 us
  starting transfers between devices: 62 us -> 103 us
  waiting for transfers between devices: 11.9 us -> 9.66 us
    all_to_all x2 -> x1, blocking collectives: 54.9 us -> 9.77 us  [body(): slab = lax.all_to_all(slab, 'y', split_axis=0, concat_axis=0, tiled=True)]
    all_to_all x1 -> x2, starting transfers between devices: 21.4 us -> 46.7 us  [over_z(): lax.all_to_all(value, 'z', split_axis=0, concat_axis=0, axis_index_groups...]
    ppermute x6 -> x9, starting transfers between devices: 15.6 us -> 26.3 us  [around(): return lax.ppermute(value, axes, [(i, (i + shift) % 4) for i in range(4)])]
    all_to_all x1 -> x2, waiting for transfers between devices: 5.62 us -> 0.01 us  [over_z(): lax.all_to_all(value, 'z', split_axis=0, concat_axis=0, axis_index_groups...]
    ppermute x1, starting transfers between devices: 3.68 us -> 8.06 us  [body(): got = lax.ppermute(proj[tok:], 'c', SWAP)]
    ppermute x6 -> x9, waiting for transfers between devices: 1.4 us -> 4.57 us  [around(): return lax.ppermute(value, axes, [(i, (i + shift) % 4) for i in range(4)])]
  transfers between devices with their start and end apart: 11 -> 15, of which waited for: 3 -> 4; matrix products, arithmetic and copies ran while one was open for 5% -> 7% of each run, Pallas kernels for 0% -> 0%
where the time goes in v6:
time: 141 us; the launch traced here: 140 us
  starting transfers between devices  103 us (73%)
  blocking collectives  9.77 us (7%)
  waiting for transfers between devices  9.66 us (7%)
  local copies, waits for them, and re-layouts  8.98 us (6%)
  other arithmetic  5.2 us (4%)
  matrix products  2.57 us (2%)
    all_to_all x2, starting transfers between devices, over_z(): lax.all_to_all(value, 'z', split_axis=0, concat_axis=0, axis_index_groups...  46.7 us
    ppermute x9, starting transfers between devices, around(): return lax.ppermute(value, axes, [(i, (i + shift) % 4) for i in range(4)])  26.3 us
    ppermute x1, starting transfers between devices, body(): other_act = lax.ppermute(activations, 'c', SWAP)  16.1 us
    all_to_all x1, blocking collectives, body(): slab = lax.all_to_all(slab, 'y', split_axis=0, concat_axis=0, tiled=True)  9.77 us
    ppermute x1, starting transfers between devices, body(): got = lax.ppermute(proj[tok:], 'c', SWAP)  8.06 us
    unnamed x6, local copies, waits for them, and re-layouts  4.85 us
    ppermute x9, waiting for transfers between devices, around(): return lax.ppermute(value, axes, [(i, (i + shift) % 4) for i in range(4)])  4.57 us
    all_to_all x1, waiting for transfers between devices, body(): lax.all_to_all(pieces, ('y', 'c'), split_axis=0, concat_axis=0, tiled=True)  4.12 us
  transfers between devices with their start and end apart: 15, of which 4 were waited for; matrix products, arithmetic and copies ran while one was open for 7% of the time, Pallas kernels for 0%

profile of v6, /device:TPU:1, one launch (start us, length us, event | category | flops | bytes accessed | tf_op | source)
XLA Modules:
  0.0 140.2 jit_solution(879373206864376904)
XLA Ops:
  0.6 16.1 %collective-permute-start = (bf16[256,4096]{1,0:T(8,128)(2,1)}, bf16[256,4096]{1,0:T(8,128)(2,1)S(1)}, u32[]{:S(2)}, u32[]{:S(2)}) collective-permute-start(bf16[256,4096]{1,0:T(8,128)(2,1)} %param.4), channel_id=1, source_target_pairs={{0,1},{1,0},{2,3},{3,2},{4,5},{5,4},{6,7},{7,6},{8,9},{9,8},{10,11... | collective-permute-start | bytes 6291464 | tf_op jit(solution)/shard_map/ppermute | solution.py:50
  16.7 1.0 constant_dynamic-slice_fusion.5
  17.7 1.9 %collective-permute-start.1 = (bf16[256,256]{1,0:T(8,128)(2,1)S(1)}, bf16[256,256]{1,0:T(8,128)(2,1)S(1)}, u32[]{:S(2)}, u32[]{:S(2)}) collective-permute-start(bf16[256,256]{1,0:T(8,128)(2,1)S(1)} %get-tuple-element.35), channel_id=1, source_target_pairs={{0,1},{1,0},{2,3},{3,2},{4,5},{5,4},{6,7},{7,6},{8,9},{9,8},{10,11... | collective-permute-start | bytes 393224 | tf_op jit(solution)/shard_map/ppermute | solution.py:53
  19.7 0.8 dynamic-slice_convert_fusion
  20.4 0.8 fusion.10
  21.2 1.7 %constant_dynamic-update-slice_fusion.1 = bf16[512,4096]{1,0:T(8,128)(2,1)S(1)} fusion(bf16[256,4096]{1,0:T(8,128)(2,1)} %param.4), kind=kLoop, calls=%fused_computation.33 | loop fusion | bytes 4194304
  23.1 1.3 fusion
  25.2 0.7 broadcast_in_dim.11
  25.9 0.9 dynamic-slice_bitcast_fusion.2
  26.8 1.9 %collective-permute-start.4 = (bf16[4,256,256]{2,1,0:T(8,128)(2,1)}, bf16[4,256,256]{2,1,0:T(8,128)(2,1)}, u32[]{:S(2)}, u32[]{:S(2)}) collective-permute-start(bf16[4,256,256]{2,1,0:T(8,128)(2,1)} %get-tuple-element.25), channel_id=1, source_target_pairs={{0,520},{8,0},{512,8},{520,512},{1,521},{9,1},{513,9},{521,513},{2... | collective-permute-start | bytes 1572872 | tf_op jit(solution)/shard_map/ppermute | solution.py:13
  28.7 3.4 %collective-permute-start.3 = (bf16[4,256,256]{2,1,0:T(8,128)(2,1)S(1)}, bf16[4,256,256]{2,1,0:T(8,128)(2,1)}, u32[]{:S(2)}, u32[]{:S(2)}) collective-permute-start(bf16[4,256,256]{2,1,0:T(8,128)(2,1)S(1)} %get-tuple-element.26), channel_id=1, source_target_pairs={{0,8},{8,512},{512,520},{520,0},{1,9},{9,513},{513,521},{521,1},{2... | collective-permute-start | bytes 1572872 | tf_op jit(solution)/shard_map/ppermute | solution.py:13
  32.1 1.9 %collective-permute-start.2 = (bf16[4,256,256]{2,1,0:T(8,128)(2,1)S(1)}, bf16[4,256,256]{2,1,0:T(8,128)(2,1)}, u32[]{:S(2)}, u32[]{:S(2)}) collective-permute-start(bf16[4,256,256]{2,1,0:T(8,128)(2,1)S(1)} %get-tuple-element.24), channel_id=1, source_target_pairs={{0,512},{8,520},{512,0},{520,8},{1,513},{9,521},{513,1},{521,9},{2... | collective-permute-start | bytes 1572872 | tf_op jit(solution)/shard_map/ppermute | solution.py:13
  34.0 25.4 %all-to-all-start = ((bf16[32,8,256]{2,1,0:T(8,128)(2,1)}), bf16[32,8,256]{2,1,0:T(8,128)(2,1)S(1)}, u32[]{:S(2)}, u32[]{:S(2)}) async-start(bf16[32,8,256]{2,1,0:T(8,128)(2,1)} %broadcast_in_dim.11), calls=%async_computation | async-start | bytes 262144 | tf_op jit(solution)/shard_map/all_to_all | solution.py:28
  59.5 1.6 %fusion.3 = bf16[4,256,256]{2,1,0:T(8,128)(2,1)S(1)} fusion(bf16[4,256,256]{2,1,0:T(8,128)(2,1)} %collective-permute-done.4, bf16[4,256,256]{2,1,0:T(8,128)(2,1)} %collective-permute-done.3, bf16[4,256,256]{2,1,0:T(8,128)(2,1)} %collective-permute-done.2, bf16[4,4,256,256]{3,2,1,0:T(8,128)(2,1)S(1)} %bitcast.49, s32[]{:T(128)S(6)} %select_n.112), kind=kLoop, calls=%fused_computation.8 | loop fusion | flops 2097152 | bytes 2621444 | tf_op jit(solution)/shard_map/convert_element_type | solution.py:22
  61.2 4.6 %collective-permute-start.7 = (bf16[256,256]{1,0:T(8,128)(2,1)S(1)}, bf16[256,256]{1,0:T(8,128)(2,1)S(1)}, u32[]{:S(2)}, u32[]{:S(2)}) collective-permute-start(bf16[256,256]{1,0:T(8,128)(2,1)S(1)} %get-tuple-element.28), channel_id=1, source_target_pairs={{0,6},{2,0},{4,2},{6,4},{1,7},{3,1},{5,3},{7,5},{8,14},{10,8},{12,... | collective-permute-start | bytes 393224 | tf_op jit(solution)/shard_map/ppermute | solution.py:13
  65.9 1.9 %collective-permute-start.6 = (bf16[256,256]{1,0:T(8,128)(2,1)S(1)}, bf16[256,256]{1,0:T(8,128)(2,1)S(1)}, u32[]{:S(2)}, u32[]{:S(2)}) collective-permute-start(bf16[256,256]{1,0:T(8,128)(2,1)S(1)} %get-tuple-element.29), channel_id=1, source_target_pairs={{0,2},{2,4},{4,6},{6,0},{1,3},{3,5},{5,7},{7,1},{8,10},{10,12},{12... | collective-permute-start | bytes 393224 | tf_op jit(solution)/shard_map/ppermute | solution.py:13
  67.8 3.5 %collective-permute-start.5 = (bf16[256,256]{1,0:T(8,128)(2,1)S(1)}, bf16[256,256]{1,0:T(8,128)(2,1)S(1)}, u32[]{:S(2)}, u32[]{:S(2)}) collective-permute-start(bf16[256,256]{1,0:T(8,128)(2,1)S(1)} %get-tuple-element.27), channel_id=1, source_target_pairs={{0,4},{2,6},{4,0},{6,2},{1,5},{3,7},{5,1},{7,3},{8,12},{10,14},{12... | collective-permute-start | bytes 393224 | tf_op jit(solution)/shard_map/ppermute | solution.py:13
  71.3 1.4 %collective-permute-done.6 = bf16[256,256]{1,0:T(8,128)(2,1)S(1)} collective-permute-done((bf16[256,256]{1,0:T(8,128)(2,1)S(1)}, bf16[256,256]{1,0:T(8,128)(2,1)S(1)}, u32[]{:S(2)}, u32[]{:S(2)}) %collective-permute-start.6) | collective-permute-done | bytes 131104 | tf_op jit(solution)/shard_map/ppermute | solution.py:13
  72.8 3.1 %collective-permute-done.5 = bf16[256,256]{1,0:T(8,128)(2,1)S(1)} collective-permute-done((bf16[256,256]{1,0:T(8,128)(2,1)S(1)}, bf16[256,256]{1,0:T(8,128)(2,1)S(1)}, u32[]{:S(2)}, u32[]{:S(2)}) %collective-permute-start.5) | collective-permute-done | bytes 131104 | tf_op jit(solution)/shard_map/ppermute | solution.py:13
  76.1 9.8 %all_to_all.20 = bf16[4,256,256]{2,1,0:T(8,128)(2,1)S(1)} all-to-all(bf16[4,256,256]{2,1,0:T(8,128)(2,1)S(1)} %broadcast_in_dim.25), channel_id=1, replica_groups=mesh['xh'=2,'z'=32,'xl'=2,'y'=4,'c'=2] {'y'}, dimensions={0} | all-to-all | bytes 1048576 | tf_op jit(solution)/shard_map/all_to_all | solution.py:76
  85.8 2.9 %collective-permute-start.10 = (bf16[4,256,256]{2,1,0:T(8,128)(2,1)S(1)}, bf16[4,256,256]{2,1,0:T(8,128)(2,1)S(1)}, u32[]{:S(2)}, u32[]{:S(2)}) collective-permute-start(bf16[4,256,256]{2,1,0:T(8,128)(2,1)S(1)} %all_to_all.20), channel_id=1, source_target_pairs={{0,520},{8,0},{512,8},{520,512},{1,521},{9,1},{513,9},{521,513},{2... | collective-permute-start | bytes 1572872 | tf_op jit(solution)/shard_map/ppermute | solution.py:13
  88.7 4.3 %collective-permute-start.9 = (bf16[4,256,256]{2,1,0:T(8,128)(2,1)S(1)}, bf16[4,256,256]{2,1,0:T(8,128)(2,1)S(1)}, u32[]{:S(2)}, u32[]{:S(2)}) collective-permute-start(bf16[4,256,256]{2,1,0:T(8,128)(2,1)S(1)} %all_to_all.20), channel_id=1, source_target_pairs={{0,512},{8,520},{512,0},{520,8},{1,513},{9,521},{513,1},{521,9},{2... | collective-permute-start | bytes 1572872 | tf_op jit(solution)/shard_map/ppermute | solution.py:13
  93.0 1.9 %collective-permute-start.8 = (bf16[4,256,256]{2,1,0:T(8,128)(2,1)S(1)}, bf16[4,256,256]{2,1,0:T(8,128)(2,1)S(1)}, u32[]{:S(2)}, u32[]{:S(2)}) collective-permute-start(bf16[4,256,256]{2,1,0:T(8,128)(2,1)S(1)} %all_to_all.20), channel_id=1, source_target_pairs={{0,8},{8,512},{512,520},{520,0},{1,9},{9,513},{513,521},{521,1},{2... | collective-permute-start | bytes 1572872 | tf_op jit(solution)/shard_map/ppermute | solution.py:13
  95.0 0.7 pad_maximum_fusion.3
  95.7 21.2 %all-to-all-start.2 = ((bf16[32,8,256]{2,1,0:T(8,128)(2,1)}), bf16[32,8,256]{2,1,0:T(8,128)(2,1)S(1)}, u32[]{:S(2)}, u32[]{:S(2)}) async-start(bf16[32,8,256]{2,1,0:T(8,128)(2,1)} %pad_maximum_fusion.3), calls=%async_computation.2 | async-start | bytes 262144 | tf_op jit(solution)/shard_map/all_to_all | solution.py:28
  118.0 1.9 %copy-done.1 = bf16[512,4096]{1,0:T(8,128)(2,1)S(1)} copy-done((bf16[512,4096]{1,0:T(8,128)(2,1)S(1)}, bf16[512,4096]{1,0:T(8,128)(2,1)}, u32[]{:S(2)}) %copy-start.1) | copy-done | bytes 4194328
  119.9 1.2 convolution_convert_fusion
  121.2 8.1 %collective-permute-start.11 = (bf16[256,256]{1,0:T(8,128)(2,1)S(1)}, bf16[256,256]{1,0:T(8,128)(2,1)S(1)}, u32[]{:S(2)}, u32[]{:S(2)}) collective-permute-start(bf16[256,256]{1,0:T(8,128)(2,1)S(1)} %get-tuple-element.33), channel_id=1, source_target_pairs={{0,1},{1,0},{2,3},{3,2},{4,5},{5,4},{6,7},{7,6},{8,9},{9,8},{10,11... | collective-permute-start | bytes 393224 | tf_op jit(solution)/shard_map/ppermute | solution.py:88
  129.2 1.0 collective-permute-done.11
  130.9 3.9 %all-to-all-start.3 = ((f32[8,8,256]{2,1,0:T(8,128)}), f32[8,8,256]{2,1,0:T(8,128)S(1)}, u32[]{:S(2)}, u32[]{:S(2)}) async-start(f32[8,8,256]{2,1,0:T(8,128)} %broadcast_in_dim.26), calls=%async_computation.3 | async-start | bytes 131072 | tf_op jit(solution)/shard_map/all_to_all | solution.py:93
  134.8 0.7 pad_maximum_fusion.2
  135.5 4.1 %all-to-all-done.3 = f32[8,8,256]{2,1,0:T(8,128)S(1)} async-done(((f32[8,8,256]{2,1,0:T(8,128)}), f32[8,8,256]{2,1,0:T(8,128)S(1)}, u32[]{:S(2)}, u32[]{:S(2)}) %all-to-all-start.3) | async-done | bytes 65568 | tf_op jit(solution)/shard_map/all_to_all | solution.py:93
  (31 shorter events, 3.5 us)
Async XLA Ops:
  0.6 22.3 %collective-permute-start = (bf16[256,4096]{1,0:T(8,128)(2,1)}, bf16[256,4096]{1,0:T(8,128)(2,1)S(1)}, u32[]{:S(2)}, u32[]{:S(2)}) collective-permute-start(bf16[256,4096]{1,0:T(8,128)(2,1)} %param.4), channel_id=1, source_target_pairs={{0,1},{1,0},{2,3},{3,2},{4,5},{5,4},{6,7},{7,6},{8,9},{9,8},{10,11... | collective-permute-start | bytes 6291464 | tf_op jit(solution)/shard_map/ppermute | solution.py:50
  17.7 5.4 %collective-permute-start.1 = (bf16[256,256]{1,0:T(8,128)(2,1)S(1)}, bf16[256,256]{1,0:T(8,128)(2,1)S(1)}, u32[]{:S(2)}, u32[]{:S(2)}) collective-permute-start(bf16[256,256]{1,0:T(8,128)(2,1)S(1)} %get-tuple-element.35), channel_id=1, source_target_pairs={{0,1},{1,0},{2,3},{3,2},{4,5},{5,4},{6,7},{7,6},{8,9},{9,8},{10,11... | collective-permute-start | bytes 393224 | tf_op jit(solution)/shard_map/ppermute | solution.py:53
  23.1 1.9 %copy-start = (bf16[512,4096]{1,0:T(8,128)(2,1)}, bf16[512,4096]{1,0:T(8,128)(2,1)S(1)}, u32[]{:S(2)}) copy-start(bf16[512,4096]{1,0:T(8,128)(2,1)S(1)} %constant_dynamic-update-slice_fusion) | copy-start | bytes 12582916
  26.8 32.7 %collective-permute-start.4 = (bf16[4,256,256]{2,1,0:T(8,128)(2,1)}, bf16[4,256,256]{2,1,0:T(8,128)(2,1)}, u32[]{:S(2)}, u32[]{:S(2)}) collective-permute-start(bf16[4,256,256]{2,1,0:T(8,128)(2,1)} %get-tuple-element.25), channel_id=1, source_target_pairs={{0,520},{8,0},{512,8},{520,512},{1,521},{9,1},{513,9},{521,513},{2... | collective-permute-start | bytes 1572872 | tf_op jit(solution)/shard_map/ppermute | solution.py:13
  28.7 30.8 %collective-permute-start.3 = (bf16[4,256,256]{2,1,0:T(8,128)(2,1)S(1)}, bf16[4,256,256]{2,1,0:T(8,128)(2,1)}, u32[]{:S(2)}, u32[]{:S(2)}) collective-permute-start(bf16[4,256,256]{2,1,0:T(8,128)(2,1)S(1)} %get-tuple-element.26), channel_id=1, source_target_pairs={{0,8},{8,512},{512,520},{520,0},{1,9},{9,513},{513,521},{521,1},{2... | collective-permute-start | bytes 1572872 | tf_op jit(solution)/shard_map/ppermute | solution.py:13
  32.1 27.4 %collective-permute-start.2 = (bf16[4,256,256]{2,1,0:T(8,128)(2,1)S(1)}, bf16[4,256,256]{2,1,0:T(8,128)(2,1)}, u32[]{:S(2)}, u32[]{:S(2)}) collective-permute-start(bf16[4,256,256]{2,1,0:T(8,128)(2,1)S(1)} %get-tuple-element.24), channel_id=1, source_target_pairs={{0,512},{8,520},{512,0},{520,8},{1,513},{9,521},{513,1},{521,9},{2... | collective-permute-start | bytes 1572872 | tf_op jit(solution)/shard_map/ppermute | solution.py:13
  34.0 41.9 %all-to-all-start = ((bf16[32,8,256]{2,1,0:T(8,128)(2,1)}), bf16[32,8,256]{2,1,0:T(8,128)(2,1)S(1)}, u32[]{:S(2)}, u32[]{:S(2)}) async-start(bf16[32,8,256]{2,1,0:T(8,128)(2,1)} %broadcast_in_dim.11), calls=%async_computation | async-start | bytes 262144 | tf_op jit(solution)/shard_map/all_to_all | solution.py:28
  61.2 10.1 %collective-permute-start.7 = (bf16[256,256]{1,0:T(8,128)(2,1)S(1)}, bf16[256,256]{1,0:T(8,128)(2,1)S(1)}, u32[]{:S(2)}, u32[]{:S(2)}) collective-permute-start(bf16[256,256]{1,0:T(8,128)(2,1)S(1)} %get-tuple-element.28), channel_id=1, source_target_pairs={{0,6},{2,0},{4,2},{6,4},{1,7},{3,1},{5,3},{7,5},{8,14},{10,8},{12,... | collective-permute-start | bytes 393224 | tf_op jit(solution)/shard_map/ppermute | solution.py:13
  65.9 6.9 %collective-permute-start.6 = (bf16[256,256]{1,0:T(8,128)(2,1)S(1)}, bf16[256,256]{1,0:T(8,128)(2,1)S(1)}, u32[]{:S(2)}, u32[]{:S(2)}) collective-permute-start(bf16[256,256]{1,0:T(8,128)(2,1)S(1)} %get-tuple-element.29), channel_id=1, source_target_pairs={{0,2},{2,4},{4,6},{6,0},{1,3},{3,5},{5,7},{7,1},{8,10},{10,12},{12... | collective-permute-start | bytes 393224 | tf_op jit(solution)/shard_map/ppermute | solution.py:13
  67.8 8.1 %collective-permute-start.5 = (bf16[256,256]{1,0:T(8,128)(2,1)S(1)}, bf16[256,256]{1,0:T(8,128)(2,1)S(1)}, u32[]{:S(2)}, u32[]{:S(2)}) collective-permute-start(bf16[256,256]{1,0:T(8,128)(2,1)S(1)} %get-tuple-element.27), channel_id=1, source_target_pairs={{0,4},{2,6},{4,0},{6,2},{1,5},{3,7},{5,1},{7,3},{8,12},{10,14},{12... | collective-permute-start | bytes 393224 | tf_op jit(solution)/shard_map/ppermute | solution.py:13
  85.8 31.1 %collective-permute-start.10 = (bf16[4,256,256]{2,1,0:T(8,128)(2,1)S(1)}, bf16[4,256,256]{2,1,0:T(8,128)(2,1)S(1)}, u32[]{:S(2)}, u32[]{:S(2)}) collective-permute-start(bf16[4,256,256]{2,1,0:T(8,128)(2,1)S(1)} %all_to_all.20), channel_id=1, source_target_pairs={{0,520},{8,0},{512,8},{520,512},{1,521},{9,1},{513,9},{521,513},{2... | collective-permute-start | bytes 1572872 | tf_op jit(solution)/shard_map/ppermute | solution.py:13
  88.7 28.2 %collective-permute-start.9 = (bf16[4,256,256]{2,1,0:T(8,128)(2,1)S(1)}, bf16[4,256,256]{2,1,0:T(8,128)(2,1)S(1)}, u32[]{:S(2)}, u32[]{:S(2)}) collective-permute-start(bf16[4,256,256]{2,1,0:T(8,128)(2,1)S(1)} %all_to_all.20), channel_id=1, source_target_pairs={{0,512},{8,520},{512,0},{520,8},{1,513},{9,521},{513,1},{521,9},{2... | collective-permute-start | bytes 1572872 | tf_op jit(solution)/shard_map/ppermute | solution.py:13
  93.0 24.0 %collective-permute-start.8 = (bf16[4,256,256]{2,1,0:T(8,128)(2,1)S(1)}, bf16[4,256,256]{2,1,0:T(8,128)(2,1)S(1)}, u32[]{:S(2)}, u32[]{:S(2)}) collective-permute-start(bf16[4,256,256]{2,1,0:T(8,128)(2,1)S(1)} %all_to_all.20), channel_id=1, source_target_pairs={{0,8},{8,512},{512,520},{520,0},{1,9},{9,513},{513,521},{521,1},{2... | collective-permute-start | bytes 1572872 | tf_op jit(solution)/shard_map/ppermute | solution.py:13
  95.7 34.5 %all-to-all-start.2 = ((bf16[32,8,256]{2,1,0:T(8,128)(2,1)}), bf16[32,8,256]{2,1,0:T(8,128)(2,1)S(1)}, u32[]{:S(2)}, u32[]{:S(2)}) async-start(bf16[32,8,256]{2,1,0:T(8,128)(2,1)} %pad_maximum_fusion.3), calls=%async_computation.2 | async-start | bytes 262144 | tf_op jit(solution)/shard_map/all_to_all | solution.py:28
  117.7 2.2 %copy-start.1 = (bf16[512,4096]{1,0:T(8,128)(2,1)S(1)}, bf16[512,4096]{1,0:T(8,128)(2,1)}, u32[]{:S(2)}) copy-start(bf16[512,4096]{1,0:T(8,128)(2,1)} %copy-done) | copy-start | bytes 12582916
  121.2 9.0 %collective-permute-start.11 = (bf16[256,256]{1,0:T(8,128)(2,1)S(1)}, bf16[256,256]{1,0:T(8,128)(2,1)S(1)}, u32[]{:S(2)}, u32[]{:S(2)}) collective-permute-start(bf16[256,256]{1,0:T(8,128)(2,1)S(1)} %get-tuple-element.33), channel_id=1, source_target_pairs={{0,1},{1,0},{2,3},{3,2},{4,5},{5,4},{6,7},{7,6},{8,9},{9,8},{10,11... | collective-permute-start | bytes 393224 | tf_op jit(solution)/shard_map/ppermute | solution.py:88
  130.9 8.7 %all-to-all-start.3 = ((f32[8,8,256]{2,1,0:T(8,128)}), f32[8,8,256]{2,1,0:T(8,128)S(1)}, u32[]{:S(2)}, u32[]{:S(2)}) async-start(f32[8,8,256]{2,1,0:T(8,128)} %broadcast_in_dim.26), calls=%async_computation.3 | async-start | bytes 131072 | tf_op jit(solution)/shard_map/all_to_all | solution.py:93

commit v7 on v6

--- a/solution.py
+++ b/solution.py
@@ -13,18 +13,19 @@
     return lax.ppermute(value, axes, [(i, (i + shift) % 4) for i in range(4)])
 
 
-def spread_sum(stack, axes):
+def spread_sum(piece, axes):
     me = lax.axis_index(axes)
-    parts = [around(pick(stack, (me + shift) % 4), axes, shift) for shift in (2, 1, 3)]
-    total = pick(stack, me).astype(jnp.float32)
+    parts = [around(piece((me + shift) % 4), axes, shift) for shift in (2, 1, 3)]
+    mine = piece(me)
+    total = mine.astype(jnp.float32)
     for part in parts:
         total += part.astype(jnp.float32)
-    return total.astype(stack.dtype)
+    return total.astype(mine.dtype)
 
 
-def over_z(value):
+def over_z(value, first):
     n = value.shape[0]
-    turned = [[(k + n // 2) % n for k in range(n)]]
+    turned = [[(k + first) % n for k in range(n)]]
     return lax.all_to_all(
         value, "z", split_axis=0, concat_axis=0, axis_index_groups=turned, tiled=True
     )
@@ -65,18 +66,24 @@
     grad = lax.dot_general(acts, cots, dims, preferred_element_type=f32)
     grad = (grad * factor).astype(bf16)
     grad = grad.reshape(2, n_z, 2, 4, rows, half)
-    grad = grad.transpose(0, 2, 3, 1, 4, 5).reshape(4, 4, column, half)
     grad, spread = lax.optimization_barrier((grad, spread))
-    col = over_z(spread)
-    plane = spread_sum(spread_sum(grad, X), "y")
+    first = 3 * n_z // 4
+    col = over_z(spread, first)
+
+    def to_x(k):
+        start = (k // 2, 0, k % 2, 0, 0, 0)
+        return lax.dynamic_slice(grad, start, (1, n_z, 1, 4, rows, half)).reshape(n_z, 4, rows, half)
+
+    line = spread_sum(to_x, X)
+    plane = spread_sum(lambda k: lax.dynamic_index_in_dim(line, k, 1, keepdims=False), "y")
     col, plane = lax.optimization_barrier((col, plane))
-    col = jnp.roll(col, n_z // 2, axis=0)
+    col = jnp.roll(col, first, axis=0)
 
     slab = jnp.broadcast_to(col.reshape(1, column, half), (4, column, half))
     slab = lax.all_to_all(slab, "y", split_axis=0, concat_axis=0, tiled=True)
     slab, plane = lax.optimization_barrier((slab, plane))
     held = [around(slab, X, shift) for shift in (2, 1, 3)]
-    moved = over_z(jnp.roll(plane.reshape(n_z, rows, half), n_z // 2, axis=0))
+    moved = over_z(jnp.roll(plane, n_z // 2, axis=0), n_z // 2)
 
     two, one, three = held
     stack = jnp.stack([slab, one, two, three])

time: 141 us -> 140 us (level)
  starting transfers between devices: 103 us -> 95.2 us
  waiting for transfers between devices: 9.66 us -> 14.9 us
    ppermute x9, waiting for transfers between devices: 4.57 us -> 9.03 us  [around(): return lax.ppermute(value, axes, [(i, (i + shift) % 4) for i in range(4)])]
    all_to_all x2, starting transfers between devices: 46.7 us -> 42.6 us  [over_z(): lax.all_to_all(value, 'z', split_axis=0, concat_axis=0, axis_index_groups...]
    ppermute x9, starting transfers between devices: 26.3 us -> 23.4 us  [around(): return lax.ppermute(value, axes, [(i, (i + shift) % 4) for i in range(4)])]
  transfers between devices with their start and end apart: 15 -> 15, of which waited for: 4 -> 6; matrix products, arithmetic and copies ran while one was open for 7% -> 7% of each run, Pallas kernels for 0% -> 0%
where the time goes in v7:
time: 140 us; the launch traced here: 139 us
  starting transfers between devices  95.2 us (68%)
  waiting for transfers between devices  14.9 us (11%)
  blocking collectives  10.9 us (8%)
  local copies, waits for them, and re-layouts  8.85 us (6%)
  other arithmetic  5.3 us (4%)
  matrix products  2.56 us (2%)
    all_to_all x2, starting transfers between devices, over_z(): lax.all_to_all(value, 'z', split_axis=0, concat_axis=0, axis_index_groups...  42.6 us
    ppermute x9, starting transfers between devices, around(): return lax.ppermute(value, axes, [(i, (i + shift) % 4) for i in range(4)])  23.4 us
    ppermute x1, starting transfers between devices, body(): other_act = lax.ppermute(activations, 'c', SWAP)  16.1 us
    all_to_all x1, blocking collectives, body(): slab = lax.all_to_all(slab, 'y', split_axis=0, concat_axis=0, tiled=True)  10.9 us
    ppermute x9, waiting for transfers between devices, around(): return lax.ppermute(value, axes, [(i, (i + shift) % 4) for i in range(4)])  9.03 us
    ppermute x1, starting transfers between devices, body(): got = lax.ppermute(proj[tok:], 'c', SWAP)  6.75 us
    unnamed x6, local copies, waits for them, and re-layouts  4.86 us
    all_to_all x1, starting transfers between devices, body(): lax.all_to_all(pieces, ('y', 'c'), split_axis=0, concat_axis=0, tiled=True)  4.43 us
  transfers between devices with their start and end apart: 15, of which 6 were waited for; matrix products, arithmetic and copies ran while one was open for 7% of the time, Pallas kernels for 0%

profile of v7, /device:TPU:1, one launch (start us, length us, event | category | flops | bytes accessed | tf_op | source)
XLA Modules:
  0.0 139.0 jit_solution(10845618788035848037)
XLA Ops:
  0.6 16.1 %collective-permute-start = (bf16[256,4096]{1,0:T(8,128)(2,1)}, bf16[256,4096]{1,0:T(8,128)(2,1)S(1)}, u32[]{:S(2)}, u32[]{:S(2)}) collective-permute-start(bf16[256,4096]{1,0:T(8,128)(2,1)} %param.4), channel_id=1, source_target_pairs={{0,1},{1,0},{2,3},{3,2},{4,5},{5,4},{6,7},{7,6},{8,9},{9,8},{10,11... | collective-permute-start | bytes 6291464 | tf_op jit(solution)/shard_map/ppermute | solution.py:51
  16.7 1.0 constant_dynamic-slice_fusion.5
  17.7 1.9 %collective-permute-start.1 = (bf16[256,256]{1,0:T(8,128)(2,1)S(1)}, bf16[256,256]{1,0:T(8,128)(2,1)S(1)}, u32[]{:S(2)}, u32[]{:S(2)}) collective-permute-start(bf16[256,256]{1,0:T(8,128)(2,1)S(1)} %get-tuple-element.35), channel_id=1, source_target_pairs={{0,1},{1,0},{2,3},{3,2},{4,5},{5,4},{6,7},{7,6},{8,9},{9,8},{10,11... | collective-permute-start | bytes 393224 | tf_op jit(solution)/shard_map/ppermute | solution.py:54
  19.8 0.8 dynamic-slice_convert_fusion
  20.5 0.8 fusion.10
  21.3 1.7 %constant_dynamic-update-slice_fusion.1 = bf16[512,4096]{1,0:T(8,128)(2,1)S(1)} fusion(bf16[256,4096]{1,0:T(8,128)(2,1)} %param.4), kind=kLoop, calls=%fused_computation.31 | loop fusion | bytes 4194304
  23.2 1.3 fusion
  25.8 0.9 dynamic-slice_bitcast_fusion.2
  26.7 1.9 %collective-permute-start.4 = (bf16[32,4,8,256]{3,2,1,0:T(8,128)(2,1)}, bf16[32,4,8,256]{3,2,1,0:T(8,128)(2,1)}, u32[]{:S(2)}, u32[]{:S(2)}) collective-permute-start(bf16[32,4,8,256]{3,2,1,0:T(8,128)(2,1)} %get-tuple-element.25), channel_id=1, source_target_pairs={{0,520},{8,0},{512,8},{520,512},{1,521},{9,1},{513,9},{521,513},{2... | collective-permute-start | bytes 1572872 | tf_op jit(solution)/shard_map/ppermute | solution.py:13
  28.7 3.4 %collective-permute-start.3 = (bf16[32,4,8,256]{3,2,1,0:T(8,128)(2,1)S(1)}, bf16[32,4,8,256]{3,2,1,0:T(8,128)(2,1)}, u32[]{:S(2)}, u32[]{:S(2)}) collective-permute-start(bf16[32,4,8,256]{3,2,1,0:T(8,128)(2,1)S(1)} %get-tuple-element.26), channel_id=1, source_target_pairs={{0,8},{8,512},{512,520},{520,0},{1,9},{9,513},{513,521},{521,1},{2... | collective-permute-start | bytes 1572872 | tf_op jit(solution)/shard_map/ppermute | solution.py:13
  32.0 1.9 %collective-permute-start.2 = (bf16[32,4,8,256]{3,2,1,0:T(8,128)(2,1)S(1)}, bf16[32,4,8,256]{3,2,1,0:T(8,128)(2,1)}, u32[]{:S(2)}, u32[]{:S(2)}) collective-permute-start(bf16[32,4,8,256]{3,2,1,0:T(8,128)(2,1)S(1)} %get-tuple-element.24), channel_id=1, source_target_pairs={{0,512},{8,520},{512,0},{520,8},{1,513},{9,521},{513,1},{521,9},{2... | collective-permute-start | bytes 1572872 | tf_op jit(solution)/shard_map/ppermute | solution.py:13
  34.0 18.6 %all-to-all-start = ((bf16[32,8,256]{2,1,0:T(8,128)(2,1)}), bf16[32,8,256]{2,1,0:T(8,128)(2,1)S(1)}, u32[]{:S(2)}, u32[]{:S(2)}) async-start(bf16[32,8,256]{2,1,0:T(8,128)(2,1)} %broadcast_in_dim.11), calls=%async_computation | async-start | bytes 262144 | tf_op jit(solution)/shard_map/all_to_all | solution.py:29
  52.6 3.4 %collective-permute-done.3 = bf16[32,4,8,256]{3,2,1,0:T(8,128)(2,1)} collective-permute-done((bf16[32,4,8,256]{3,2,1,0:T(8,128)(2,1)S(1)}, bf16[32,4,8,256]{3,2,1,0:T(8,128)(2,1)}, u32[]{:S(2)}, u32[]{:S(2)}) %collective-permute-start.3) | collective-permute-done | bytes 524320 | tf_op jit(solution)/shard_map/ppermute | solution.py:13
  56.1 1.7 %fusion.3 = bf16[32,4,8,256]{3,2,1,0:T(8,128)(2,1)S(1)} fusion(bf16[32,4,8,256]{3,2,1,0:T(8,128)(2,1)} %collective-permute-done.4, bf16[32,4,8,256]{3,2,1,0:T(8,128)(2,1)} %collective-permute-done.3, bf16[32,4,8,256]{3,2,1,0:T(8,128)(2,1)} %collective-permute-done.2, bf16[2,32,2,4,8,256]{5,4,3,2,1,0:T(8,128)(2,1)S(1)} %bitcast.43, s32[]{:T(128)S(6)} %select_n.154, ...), kind=kLoop, calls=%fused_computation.8 | loop fusion | flops 2097152 | bytes 2621448 | tf_op jit(solution)/shard_map/convert_element_type | solution.py:23
  57.9 1.9 %collective-permute-start.7 = (bf16[32,8,256]{2,1,0:T(8,128)(2,1)S(1)}, bf16[32,8,256]{2,1,0:T(8,128)(2,1)S(1)}, u32[]{:S(2)}, u32[]{:S(2)}) collective-permute-start(bf16[32,8,256]{2,1,0:T(8,128)(2,1)S(1)} %get-tuple-element.28), channel_id=1, source_target_pairs={{0,6},{2,0},{4,2},{6,4},{1,7},{3,1},{5,3},{7,5},{8,14},{10,8},{12,... | collective-permute-start | bytes 393224 | tf_op jit(solution)/shard_map/ppermute | solution.py:13
  59.8 3.4 %collective-permute-start.6 = (bf16[32,8,256]{2,1,0:T(8,128)(2,1)S(1)}, bf16[32,8,256]{2,1,0:T(8,128)(2,1)S(1)}, u32[]{:S(2)}, u32[]{:S(2)}) collective-permute-start(bf16[32,8,256]{2,1,0:T(8,128)(2,1)S(1)} %get-tuple-element.29), channel_id=1, source_target_pairs={{0,2},{2,4},{4,6},{6,0},{1,3},{3,5},{5,7},{7,1},{8,10},{10,12},{12... | collective-permute-start | bytes 393224 | tf_op jit(solution)/shard_map/ppermute | solution.py:13
  63.2 1.9 %collective-permute-start.5 = (bf16[32,8,256]{2,1,0:T(8,128)(2,1)S(1)}, bf16[32,8,256]{2,1,0:T(8,128)(2,1)S(1)}, u32[]{:S(2)}, u32[]{:S(2)}) collective-permute-start(bf16[32,8,256]{2,1,0:T(8,128)(2,1)S(1)} %get-tuple-element.27), channel_id=1, source_target_pairs={{0,4},{2,6},{4,0},{6,2},{1,5},{3,7},{5,1},{7,3},{8,12},{10,14},{12... | collective-permute-start | bytes 393224 | tf_op jit(solution)/shard_map/ppermute | solution.py:13
  65.1 1.9 %collective-permute-done.6 = bf16[32,8,256]{2,1,0:T(8,128)(2,1)S(1)} collective-permute-done((bf16[32,8,256]{2,1,0:T(8,128)(2,1)S(1)}, bf16[32,8,256]{2,1,0:T(8,128)(2,1)S(1)}, u32[]{:S(2)}, u32[]{:S(2)}) %collective-permute-start.6) | collective-permute-done | bytes 131104 | tf_op jit(solution)/shard_map/ppermute | solution.py:13
  67.0 3.7 %collective-permute-done.5 = bf16[32,8,256]{2,1,0:T(8,128)(2,1)S(1)} collective-permute-done((bf16[32,8,256]{2,1,0:T(8,128)(2,1)S(1)}, bf16[32,8,256]{2,1,0:T(8,128)(2,1)S(1)}, u32[]{:S(2)}, u32[]{:S(2)}) %collective-permute-start.5) | collective-permute-done | bytes 131104 | tf_op jit(solution)/shard_map/ppermute | solution.py:13
  70.8 0.8 all-to-all-done
  71.7 10.9 %all_to_all.20 = bf16[4,256,256]{2,1,0:T(8,128)(2,1)S(1)} all-to-all(bf16[4,256,256]{2,1,0:T(8,128)(2,1)S(1)} %broadcast_in_dim.25), channel_id=1, replica_groups=mesh['xh'=2,'z'=32,'xl'=2,'y'=4,'c'=2] {'y'}, dimensions={0} | all-to-all | bytes 1048576 | tf_op jit(solution)/shard_map/all_to_all | solution.py:83
  82.6 2.5 %collective-permute-start.10 = (bf16[4,256,256]{2,1,0:T(8,128)(2,1)S(1)}, bf16[4,256,256]{2,1,0:T(8,128)(2,1)S(1)}, u32[]{:S(2)}, u32[]{:S(2)}) collective-permute-start(bf16[4,256,256]{2,1,0:T(8,128)(2,1)S(1)} %all_to_all.20), channel_id=1, source_target_pairs={{0,520},{8,0},{512,8},{520,512},{1,521},{9,1},{513,9},{521,513},{2... | collective-permute-start | bytes 1572872 | tf_op jit(solution)/shard_map/ppermute | solution.py:13
  85.1 4.6 %collective-permute-start.9 = (bf16[4,256,256]{2,1,0:T(8,128)(2,1)S(1)}, bf16[4,256,256]{2,1,0:T(8,128)(2,1)S(1)}, u32[]{:S(2)}, u32[]{:S(2)}) collective-permute-start(bf16[4,256,256]{2,1,0:T(8,128)(2,1)S(1)} %all_to_all.20), channel_id=1, source_target_pairs={{0,512},{8,520},{512,0},{520,8},{1,513},{9,521},{513,1},{521,9},{2... | collective-permute-start | bytes 1572872 | tf_op jit(solution)/shard_map/ppermute | solution.py:13
  89.7 1.9 %collective-permute-start.8 = (bf16[4,256,256]{2,1,0:T(8,128)(2,1)S(1)}, bf16[4,256,256]{2,1,0:T(8,128)(2,1)S(1)}, u32[]{:S(2)}, u32[]{:S(2)}) collective-permute-start(bf16[4,256,256]{2,1,0:T(8,128)(2,1)S(1)} %all_to_all.20), channel_id=1, source_target_pairs={{0,8},{8,512},{512,520},{520,0},{1,9},{9,513},{513,521},{521,1},{2... | collective-permute-start | bytes 1572872 | tf_op jit(solution)/shard_map/ppermute | solution.py:13
  92.4 24.0 %all-to-all-start.2 = ((bf16[32,8,256]{2,1,0:T(8,128)(2,1)}), bf16[32,8,256]{2,1,0:T(8,128)(2,1)S(1)}, u32[]{:S(2)}, u32[]{:S(2)}) async-start(bf16[32,8,256]{2,1,0:T(8,128)(2,1)} %pad_maximum_fusion.3), calls=%async_computation.2 | async-start | bytes 262144 | tf_op jit(solution)/shard_map/all_to_all | solution.py:29
  117.5 1.9 %copy-done.1 = bf16[512,4096]{1,0:T(8,128)(2,1)S(1)} copy-done((bf16[512,4096]{1,0:T(8,128)(2,1)S(1)}, bf16[512,4096]{1,0:T(8,128)(2,1)}, u32[]{:S(2)}) %copy-start.1) | copy-done | bytes 4194328
  119.4 1.2 convolution_convert_fusion
  120.7 6.7 %collective-permute-start.11 = (bf16[256,256]{1,0:T(8,128)(2,1)S(1)}, bf16[256,256]{1,0:T(8,128)(2,1)S(1)}, u32[]{:S(2)}, u32[]{:S(2)}) collective-permute-start(bf16[256,256]{1,0:T(8,128)(2,1)S(1)} %get-tuple-element.33), channel_id=1, source_target_pairs={{0,1},{1,0},{2,3},{3,2},{4,5},{5,4},{6,7},{7,6},{8,9},{9,8},{10,11... | collective-permute-start | bytes 393224 | tf_op jit(solution)/shard_map/ppermute | solution.py:95
  127.5 1.0 collective-permute-done.11
  129.1 4.4 %all-to-all-start.3 = ((f32[8,8,256]{2,1,0:T(8,128)}), f32[8,8,256]{2,1,0:T(8,128)S(1)}, u32[]{:S(2)}, u32[]{:S(2)}) async-start(f32[8,8,256]{2,1,0:T(8,128)} %broadcast_in_dim.26), calls=%async_computation.3 | async-start | bytes 131072 | tf_op jit(solution)/shard_map/all_to_all | solution.py:100
  133.5 0.7 pad_maximum_fusion.2
  134.3 4.1 %all-to-all-done.3 = f32[8,8,256]{2,1,0:T(8,128)S(1)} async-done(((f32[8,8,256]{2,1,0:T(8,128)}), f32[8,8,256]{2,1,0:T(8,128)S(1)}, u32[]{:S(2)}, u32[]{:S(2)}) %all-to-all-start.3) | async-done | bytes 65568 | tf_op jit(solution)/shard_map/all_to_all | solution.py:100
  (31 shorter events, 4.7 us)
Async XLA Ops:
  0.6 22.4 %collective-permute-start = (bf16[256,4096]{1,0:T(8,128)(2,1)}, bf16[256,4096]{1,0:T(8,128)(2,1)S(1)}, u32[]{:S(2)}, u32[]{:S(2)}) collective-permute-start(bf16[256,4096]{1,0:T(8,128)(2,1)} %param.4), channel_id=1, source_target_pairs={{0,1},{1,0},{2,3},{3,2},{4,5},{5,4},{6,7},{7,6},{8,9},{9,8},{10,11... | collective-permute-start | bytes 6291464 | tf_op jit(solution)/shard_map/ppermute | solution.py:51
  17.7 5.5 %collective-permute-start.1 = (bf16[256,256]{1,0:T(8,128)(2,1)S(1)}, bf16[256,256]{1,0:T(8,128)(2,1)S(1)}, u32[]{:S(2)}, u32[]{:S(2)}) collective-permute-start(bf16[256,256]{1,0:T(8,128)(2,1)S(1)} %get-tuple-element.35), channel_id=1, source_target_pairs={{0,1},{1,0},{2,3},{3,2},{4,5},{5,4},{6,7},{7,6},{8,9},{9,8},{10,11... | collective-permute-start | bytes 393224 | tf_op jit(solution)/shard_map/ppermute | solution.py:54
  23.2 1.9 %copy-start = (bf16[512,4096]{1,0:T(8,128)(2,1)}, bf16[512,4096]{1,0:T(8,128)(2,1)S(1)}, u32[]{:S(2)}) copy-start(bf16[512,4096]{1,0:T(8,128)(2,1)S(1)} %constant_dynamic-update-slice_fusion) | copy-start | bytes 12582916
  26.7 25.9 %collective-permute-start.4 = (bf16[32,4,8,256]{3,2,1,0:T(8,128)(2,1)}, bf16[32,4,8,256]{3,2,1,0:T(8,128)(2,1)}, u32[]{:S(2)}, u32[]{:S(2)}) collective-permute-start(bf16[32,4,8,256]{3,2,1,0:T(8,128)(2,1)} %get-tuple-element.25), channel_id=1, source_target_pairs={{0,520},{8,0},{512,8},{520,512},{1,521},{9,1},{513,9},{521,513},{2... | collective-permute-start | bytes 1572872 | tf_op jit(solution)/shard_map/ppermute | solution.py:13
  28.7 27.4 %collective-permute-start.3 = (bf16[32,4,8,256]{3,2,1,0:T(8,128)(2,1)S(1)}, bf16[32,4,8,256]{3,2,1,0:T(8,128)(2,1)}, u32[]{:S(2)}, u32[]{:S(2)}) collective-permute-start(bf16[32,4,8,256]{3,2,1,0:T(8,128)(2,1)S(1)} %get-tuple-element.26), channel_id=1, source_target_pairs={{0,8},{8,512},{512,520},{520,0},{1,9},{9,513},{513,521},{521,1},{2... | collective-permute-start | bytes 1572872 | tf_op jit(solution)/shard_map/ppermute | solution.py:13
  32.0 24.1 %collective-permute-start.2 = (bf16[32,4,8,256]{3,2,1,0:T(8,128)(2,1)S(1)}, bf16[32,4,8,256]{3,2,1,0:T(8,128)(2,1)}, u32[]{:S(2)}, u32[]{:S(2)}) collective-permute-start(bf16[32,4,8,256]{3,2,1,0:T(8,128)(2,1)S(1)} %get-tuple-element.24), channel_id=1, source_target_pairs={{0,512},{8,520},{512,0},{520,8},{1,513},{9,521},{513,1},{521,9},{2... | collective-permute-start | bytes 1572872 | tf_op jit(solution)/shard_map/ppermute | solution.py:13
  34.0 37.6 %all-to-all-start = ((bf16[32,8,256]{2,1,0:T(8,128)(2,1)}), bf16[32,8,256]{2,1,0:T(8,128)(2,1)S(1)}, u32[]{:S(2)}, u32[]{:S(2)}) async-start(bf16[32,8,256]{2,1,0:T(8,128)(2,1)} %broadcast_in_dim.11), calls=%async_computation | async-start | bytes 262144 | tf_op jit(solution)/shard_map/all_to_all | solution.py:29
  57.9 7.2 %collective-permute-start.7 = (bf16[32,8,256]{2,1,0:T(8,128)(2,1)S(1)}, bf16[32,8,256]{2,1,0:T(8,128)(2,1)S(1)}, u32[]{:S(2)}, u32[]{:S(2)}) collective-permute-start(bf16[32,8,256]{2,1,0:T(8,128)(2,1)S(1)} %get-tuple-element.28), channel_id=1, source_target_pairs={{0,6},{2,0},{4,2},{6,4},{1,7},{3,1},{5,3},{7,5},{8,14},{10,8},{12,... | collective-permute-start | bytes 393224 | tf_op jit(solution)/shard_map/ppermute | solution.py:13
  59.8 7.2 %collective-permute-start.6 = (bf16[32,8,256]{2,1,0:T(8,128)(2,1)S(1)}, bf16[32,8,256]{2,1,0:T(8,128)(2,1)S(1)}, u32[]{:S(2)}, u32[]{:S(2)}) collective-permute-start(bf16[32,8,256]{2,1,0:T(8,128)(2,1)S(1)} %get-tuple-element.29), channel_id=1, source_target_pairs={{0,2},{2,4},{4,6},{6,0},{1,3},{3,5},{5,7},{7,1},{8,10},{10,12},{12... | collective-permute-start | bytes 393224 | tf_op jit(solution)/shard_map/ppermute | solution.py:13
  63.2 7.5 %collective-permute-start.5 = (bf16[32,8,256]{2,1,0:T(8,128)(2,1)S(1)}, bf16[32,8,256]{2,1,0:T(8,128)(2,1)S(1)}, u32[]{:S(2)}, u32[]{:S(2)}) collective-permute-start(bf16[32,8,256]{2,1,0:T(8,128)(2,1)S(1)} %get-tuple-element.27), channel_id=1, source_target_pairs={{0,4},{2,6},{4,0},{6,2},{1,5},{3,7},{5,1},{7,3},{8,12},{10,14},{12... | collective-permute-start | bytes 393224 | tf_op jit(solution)/shard_map/ppermute | solution.py:13
  82.6 33.9 %collective-permute-start.10 = (bf16[4,256,256]{2,1,0:T(8,128)(2,1)S(1)}, bf16[4,256,256]{2,1,0:T(8,128)(2,1)S(1)}, u32[]{:S(2)}, u32[]{:S(2)}) collective-permute-start(bf16[4,256,256]{2,1,0:T(8,128)(2,1)S(1)} %all_to_all.20), channel_id=1, source_target_pairs={{0,520},{8,0},{512,8},{520,512},{1,521},{9,1},{513,9},{521,513},{2... | collective-permute-start | bytes 1572872 | tf_op jit(solution)/shard_map/ppermute | solution.py:13
  85.1 31.4 %collective-permute-start.9 = (bf16[4,256,256]{2,1,0:T(8,128)(2,1)S(1)}, bf16[4,256,256]{2,1,0:T(8,128)(2,1)S(1)}, u32[]{:S(2)}, u32[]{:S(2)}) collective-permute-start(bf16[4,256,256]{2,1,0:T(8,128)(2,1)S(1)} %all_to_all.20), channel_id=1, source_target_pairs={{0,512},{8,520},{512,0},{520,8},{1,513},{9,521},{513,1},{521,9},{2... | collective-permute-start | bytes 1572872 | tf_op jit(solution)/shard_map/ppermute | solution.py:13
  89.7 26.7 %collective-permute-start.8 = (bf16[4,256,256]{2,1,0:T(8,128)(2,1)S(1)}, bf16[4,256,256]{2,1,0:T(8,128)(2,1)S(1)}, u32[]{:S(2)}, u32[]{:S(2)}) collective-permute-start(bf16[4,256,256]{2,1,0:T(8,128)(2,1)S(1)} %all_to_all.20), channel_id=1, source_target_pairs={{0,8},{8,512},{512,520},{520,0},{1,9},{9,513},{513,521},{521,1},{2... | collective-permute-start | bytes 1572872 | tf_op jit(solution)/shard_map/ppermute | solution.py:13
  92.4 36.0 %all-to-all-start.2 = ((bf16[32,8,256]{2,1,0:T(8,128)(2,1)}), bf16[32,8,256]{2,1,0:T(8,128)(2,1)S(1)}, u32[]{:S(2)}, u32[]{:S(2)}) async-start(bf16[32,8,256]{2,1,0:T(8,128)(2,1)} %pad_maximum_fusion.3), calls=%async_computation.2 | async-start | bytes 262144 | tf_op jit(solution)/shard_map/all_to_all | solution.py:29
  117.2 2.2 %copy-start.1 = (bf16[512,4096]{1,0:T(8,128)(2,1)S(1)}, bf16[512,4096]{1,0:T(8,128)(2,1)}, u32[]{:S(2)}) copy-start(bf16[512,4096]{1,0:T(8,128)(2,1)} %copy-done) | copy-start | bytes 12582916
  120.7 7.7 %collective-permute-start.11 = (bf16[256,256]{1,0:T(8,128)(2,1)S(1)}, bf16[256,256]{1,0:T(8,128)(2,1)S(1)}, u32[]{:S(2)}, u32[]{:S(2)}) collective-permute-start(bf16[256,256]{1,0:T(8,128)(2,1)S(1)} %get-tuple-element.33), channel_id=1, source_target_pairs={{0,1},{1,0},{2,3},{3,2},{4,5},{5,4},{6,7},{7,6},{8,9},{9,8},{10,11... | collective-permute-start | bytes 393224 | tf_op jit(solution)/shard_map/ppermute | solution.py:95
  129.1 9.3 %all-to-all-start.3 = ((f32[8,8,256]{2,1,0:T(8,128)}), f32[8,8,256]{2,1,0:T(8,128)S(1)}, u32[]{:S(2)}, u32[]{:S(2)}) async-start(f32[8,8,256]{2,1,0:T(8,128)} %broadcast_in_dim.26), calls=%async_computation.3 | async-start | bytes 131072 | tf_op jit(solution)/shard_map/all_to_all | solution.py:100

commit v8 on v7

--- a/solution.py
+++ b/solution.py
@@ -82,25 +82,24 @@
     slab = jnp.broadcast_to(col.reshape(1, column, half), (4, column, half))
     slab = lax.all_to_all(slab, "y", split_axis=0, concat_axis=0, tiled=True)
     slab, plane = lax.optimization_barrier((slab, plane))
-    held = [around(slab, X, shift) for shift in (2, 1, 3)]
+    one, three = around(slab, X, 1), around(slab, X, 3)
     moved = over_z(jnp.roll(plane, n_z // 2, axis=0), n_z // 2)
-
-    two, one, three = held
+    two = jnp.concatenate([around(one[:2], X, 1), around(three[2:], X, 3)])
+    piece = jnp.sum(moved.astype(f32), axis=0)
+    pieces = jnp.broadcast_to(piece[None], (8, rows, half))
+    pieces = lax.all_to_all(pieces, ("y", "c"), split_axis=0, concat_axis=0, tiled=True)
     stack = jnp.stack([slab, one, two, three])
     whole = jnp.stack([pick(stack, (x - k) % 4) for k in range(4)])
     whole = whole.reshape(2, 2, 4, n_z, rows, half)
     weight = whole.transpose(0, 3, 1, 2, 4, 5).reshape(d_in, half)
 
     proj = jnp.dot(acts, weight, preferred_element_type=f32).astype(bf16)
-    got = lax.ppermute(proj[tok:], "c", SWAP)
-    kept = proj[:tok]
-    got, kept, moved = lax.optimization_barrier((got, kept, moved))
-    piece = jnp.sum(moved.astype(f32), axis=0)
-    pieces = jnp.broadcast_to(piece[None], (8, rows, half))
-    pieces = lax.all_to_all(pieces, ("y", "c"), split_axis=0, concat_axis=0, tiled=True)
+    proj, pieces = lax.optimization_barrier((proj, pieces))
     pieces = pieces.reshape(4, 2, rows, half)
     weight_grads = pieces.transpose(0, 2, 1, 3).reshape(own, cols)
 
+    got = lax.ppermute(proj[tok:], "c", SWAP)
+    kept = proj[:tok]
     left = jnp.where(c == 0, kept, got)
     right = jnp.where(c == 0, got, kept)
     projected = jnp.concatenate([left, right], axis=1)

time: 140 us -> 148 us (1.057)
  waiting for transfers between devices: 14.9 us -> 18.9 us
  starting transfers between devices: 95.2 us -> 98.8 us
  matrix products: 2.56 us -> 4.75 us
  local copies, waits for them, and re-layouts: 8.85 us -> 6.97 us
    ppermute x9 -> x10, waiting for transfers between devices: 9.03 us -> 15.6 us  [around(): return lax.ppermute(value, axes, [(i, (i + shift) % 4) for i in range(4)])]
    all_to_all x1, starting transfers between devices: 4.43 us -> 9.24 us  [body(): lax.all_to_all(pieces, ('y', 'c'), split_axis=0, concat_axis=0, tiled=True)]
    ppermute x1, starting transfers between devices: 6.75 us -> 2.69 us  [body(): got = lax.ppermute(proj[tok:], 'c', SWAP)]
    ppermute x9 -> x10, starting transfers between devices: 23.4 us -> 26.2 us  [around(): return lax.ppermute(value, axes, [(i, (i + shift) % 4) for i in range(4)])]
    all_to_all x1, waiting for transfers between devices: 4.12 us -> 1.43 us  [body(): lax.all_to_all(pieces, ('y', 'c'), split_axis=0, concat_axis=0, tiled=True)]
    dot_general x1, matrix products: 1.25 us -> 3.43 us  [body(): proj = jnp.dot(acts, weight, preferred_element_type=f32).astype(bf16)]
    unnamed x6 -> x4, local copies, waits for them, and re-layouts: 4.86 us -> 2.95 us
  transfers between devices with their start and end apart: 15 -> 16, of which waited for: 6 -> 8; matrix products, arithmetic and copies ran while one was open for 7% -> 8% of each run, Pallas kernels for 0% -> 0%
where the time goes in v8:
time: 148 us; the launch traced here: 147 us
  starting transfers between devices  98.8 us (67%)
  waiting for transfers between devices  18.9 us (13%)
  blocking collectives  10.9 us (7%)
  local copies, waits for them, and re-layouts  6.97 us (5%)
  other arithmetic  5.34 us (4%)
  matrix products  4.75 us (3%)
    all_to_all x2, starting transfers between devices, over_z(): lax.all_to_all(value, 'z', split_axis=0, concat_axis=0, axis_index_groups...  42.7 us
    ppermute x10, starting transfers between devices, around(): return lax.ppermute(value, axes, [(i, (i + shift) % 4) for i in range(4)])  26.2 us
    ppermute x1, starting transfers between devices, body(): other_act = lax.ppermute(activations, 'c', SWAP)  16.1 us
    ppermute x10, waiting for transfers between devices, around(): return lax.ppermute(value, axes, [(i, (i + shift) % 4) for i in range(4)])  15.6 us
    all_to_all x1, blocking collectives, body(): slab = lax.all_to_all(slab, 'y', split_axis=0, concat_axis=0, tiled=True)  10.9 us
    all_to_all x1, starting transfers between devices, body(): lax.all_to_all(pieces, ('y', 'c'), split_axis=0, concat_axis=0, tiled=True)  9.24 us
    dot_general x1, matrix products, body(): proj = jnp.dot(acts, weight, preferred_element_type=f32).astype(bf16)  3.43 us
  transfers between devices with their start and end apart: 16, of which 8 were waited for; matrix products, arithmetic and copies ran while one was open for 8% of the time, Pallas kernels for 0%

profile of v8, /device:TPU:1, one launch (start us, length us, event | category | flops | bytes accessed | tf_op | source)
XLA Modules:
  0.0 146.9 jit_solution(12342605677207258471)
XLA Ops:
  0.6 16.1 %collective-permute-start = (bf16[256,4096]{1,0:T(8,128)(2,1)}, bf16[256,4096]{1,0:T(8,128)(2,1)S(1)}, u32[]{:S(2)}, u32[]{:S(2)}) collective-permute-start(bf16[256,4096]{1,0:T(8,128)(2,1)} %param.4), channel_id=1, source_target_pairs={{0,1},{1,0},{2,3},{3,2},{4,5},{5,4},{6,7},{7,6},{8,9},{9,8},{10,11... | collective-permute-start | bytes 6291464 | tf_op jit(solution)/shard_map/ppermute | solution.py:51
  16.7 1.0 constant_dynamic-slice_fusion.5
  17.7 1.9 %collective-permute-start.1 = (bf16[256,256]{1,0:T(8,128)(2,1)S(1)}, bf16[256,256]{1,0:T(8,128)(2,1)S(1)}, u32[]{:S(2)}, u32[]{:S(2)}) collective-permute-start(bf16[256,256]{1,0:T(8,128)(2,1)S(1)} %get-tuple-element.31), channel_id=1, source_target_pairs={{0,1},{1,0},{2,3},{3,2},{4,5},{5,4},{6,7},{7,6},{8,9},{9,8},{10,11... | collective-permute-start | bytes 393224 | tf_op jit(solution)/shard_map/ppermute | solution.py:54
  19.8 0.8 dynamic-slice_convert_fusion
  21.3 1.7 %constant_dynamic-update-slice_fusion.1 = bf16[512,4096]{1,0:T(8,128)(2,1)S(1)} fusion(bf16[256,4096]{1,0:T(8,128)(2,1)} %param.4), kind=kLoop, calls=%fused_computation.32 | loop fusion | bytes 4194304
  23.2 1.3 fusion
  25.8 1.0 dynamic-slice_bitcast_fusion.2
  26.7 1.9 %collective-permute-start.4 = (bf16[32,4,8,256]{3,2,1,0:T(8,128)(2,1)}, bf16[32,4,8,256]{3,2,1,0:T(8,128)(2,1)}, u32[]{:S(2)}, u32[]{:S(2)}) collective-permute-start(bf16[32,4,8,256]{3,2,1,0:T(8,128)(2,1)} %get-tuple-element.23), channel_id=1, source_target_pairs={{0,520},{8,0},{512,8},{520,512},{1,521},{9,1},{513,9},{521,513},{2... | collective-permute-start | bytes 1572872 | tf_op jit(solution)/shard_map/ppermute | solution.py:13
  28.6 3.4 %collective-permute-start.3 = (bf16[32,4,8,256]{3,2,1,0:T(8,128)(2,1)S(1)}, bf16[32,4,8,256]{3,2,1,0:T(8,128)(2,1)}, u32[]{:S(2)}, u32[]{:S(2)}) collective-permute-start(bf16[32,4,8,256]{3,2,1,0:T(8,128)(2,1)S(1)} %get-tuple-element.24), channel_id=1, source_target_pairs={{0,8},{8,512},{512,520},{520,0},{1,9},{9,513},{513,521},{521,1},{2... | collective-permute-start | bytes 1572872 | tf_op jit(solution)/shard_map/ppermute | solution.py:13
  32.0 1.9 %collective-permute-start.2 = (bf16[32,4,8,256]{3,2,1,0:T(8,128)(2,1)S(1)}, bf16[32,4,8,256]{3,2,1,0:T(8,128)(2,1)}, u32[]{:S(2)}, u32[]{:S(2)}) collective-permute-start(bf16[32,4,8,256]{3,2,1,0:T(8,128)(2,1)S(1)} %get-tuple-element.22), channel_id=1, source_target_pairs={{0,512},{8,520},{512,0},{520,8},{1,513},{9,521},{513,1},{521,9},{2... | collective-permute-start | bytes 1572872 | tf_op jit(solution)/shard_map/ppermute | solution.py:13
  34.0 18.6 %all-to-all-start = ((bf16[32,8,256]{2,1,0:T(8,128)(2,1)}), bf16[32,8,256]{2,1,0:T(8,128)(2,1)S(1)}, u32[]{:S(2)}, u32[]{:S(2)}) async-start(bf16[32,8,256]{2,1,0:T(8,128)(2,1)} %broadcast_in_dim.11), calls=%async_computation | async-start | bytes 262144 | tf_op jit(solution)/shard_map/all_to_all | solution.py:29
  52.6 3.4 %collective-permute-done.3 = bf16[32,4,8,256]{3,2,1,0:T(8,128)(2,1)} collective-permute-done((bf16[32,4,8,256]{3,2,1,0:T(8,128)(2,1)S(1)}, bf16[32,4,8,256]{3,2,1,0:T(8,128)(2,1)}, u32[]{:S(2)}, u32[]{:S(2)}) %collective-permute-start.3) | collective-permute-done | bytes 524320 | tf_op jit(solution)/shard_map/ppermute | solution.py:13
  56.1 1.7 %fusion.3 = bf16[32,4,8,256]{3,2,1,0:T(8,128)(2,1)S(1)} fusion(bf16[32,4,8,256]{3,2,1,0:T(8,128)(2,1)} %collective-permute-done.4, bf16[32,4,8,256]{3,2,1,0:T(8,128)(2,1)} %collective-permute-done.3, bf16[32,4,8,256]{3,2,1,0:T(8,128)(2,1)} %collective-permute-done.2, bf16[2,32,2,4,8,256]{5,4,3,2,1,0:T(8,128)(2,1)S(1)} %bitcast.44, s32[]{:T(128)S(6)} %select_n.154, ...), kind=kLoop, calls=%fused_computation.8 | loop fusion | flops 2097152 | bytes 2621448 | tf_op jit(solution)/shard_map/convert_element_type | solution.py:23
  57.9 1.9 %collective-permute-start.7 = (bf16[32,8,256]{2,1,0:T(8,128)(2,1)S(1)}, bf16[32,8,256]{2,1,0:T(8,128)(2,1)S(1)}, u32[]{:S(2)}, u32[]{:S(2)}) collective-permute-start(bf16[32,8,256]{2,1,0:T(8,128)(2,1)S(1)} %get-tuple-element.26), channel_id=1, source_target_pairs={{0,6},{2,0},{4,2},{6,4},{1,7},{3,1},{5,3},{7,5},{8,14},{10,8},{12,... | collective-permute-start | bytes 393224 | tf_op jit(solution)/shard_map/ppermute | solution.py:13
  59.8 3.4 %collective-permute-start.6 = (bf16[32,8,256]{2,1,0:T(8,128)(2,1)S(1)}, bf16[32,8,256]{2,1,0:T(8,128)(2,1)S(1)}, u32[]{:S(2)}, u32[]{:S(2)}) collective-permute-start(bf16[32,8,256]{2,1,0:T(8,128)(2,1)S(1)} %get-tuple-element.27), channel_id=1, source_target_pairs={{0,2},{2,4},{4,6},{6,0},{1,3},{3,5},{5,7},{7,1},{8,10},{10,12},{12... | collective-permute-start | bytes 393224 | tf_op jit(solution)/shard_map/ppermute | solution.py:13
  63.2 1.9 %collective-permute-start.5 = (bf16[32,8,256]{2,1,0:T(8,128)(2,1)S(1)}, bf16[32,8,256]{2,1,0:T(8,128)(2,1)S(1)}, u32[]{:S(2)}, u32[]{:S(2)}) collective-permute-start(bf16[32,8,256]{2,1,0:T(8,128)(2,1)S(1)} %get-tuple-element.25), channel_id=1, source_target_pairs={{0,4},{2,6},{4,0},{6,2},{1,5},{3,7},{5,1},{7,3},{8,12},{10,14},{12... | collective-permute-start | bytes 393224 | tf_op jit(solution)/shard_map/ppermute | solution.py:13
  65.1 1.9 %collective-permute-done.6 = bf16[32,8,256]{2,1,0:T(8,128)(2,1)S(1)} collective-permute-done((bf16[32,8,256]{2,1,0:T(8,128)(2,1)S(1)}, bf16[32,8,256]{2,1,0:T(8,128)(2,1)S(1)}, u32[]{:S(2)}, u32[]{:S(2)}) %collective-permute-start.6) | collective-permute-done | bytes 131104 | tf_op jit(solution)/shard_map/ppermute | solution.py:13
  67.0 3.7 %collective-permute-done.5 = bf16[32,8,256]{2,1,0:T(8,128)(2,1)S(1)} collective-permute-done((bf16[32,8,256]{2,1,0:T(8,128)(2,1)S(1)}, bf16[32,8,256]{2,1,0:T(8,128)(2,1)S(1)}, u32[]{:S(2)}, u32[]{:S(2)}) %collective-permute-start.5) | collective-permute-done | bytes 131104 | tf_op jit(solution)/shard_map/ppermute | solution.py:13
  70.8 0.8 all-to-all-done
  71.7 10.9 %all_to_all.20 = bf16[4,256,256]{2,1,0:T(8,128)(2,1)S(1)} all-to-all(bf16[4,256,256]{2,1,0:T(8,128)(2,1)S(1)} %broadcast_in_dim.25), channel_id=1, replica_groups=mesh['xh'=2,'z'=32,'xl'=2,'y'=4,'c'=2] {'y'}, dimensions={0} | all-to-all | bytes 1048576 | tf_op jit(solution)/shard_map/all_to_all | solution.py:83
  82.6 2.5 %collective-permute-start.10 = (bf16[4,256,256]{2,1,0:T(8,128)(2,1)S(1)}, bf16[4,256,256]{2,1,0:T(8,128)(2,1)S(1)}, u32[]{:S(2)}, u32[]{:S(2)}) collective-permute-start(bf16[4,256,256]{2,1,0:T(8,128)(2,1)S(1)} %all_to_all.20), channel_id=1, source_target_pairs={{0,520},{8,0},{512,8},{520,512},{1,521},{9,1},{513,9},{521,513},{2... | collective-permute-start | bytes 1572872 | tf_op jit(solution)/shard_map/ppermute | solution.py:13
  85.1 2.9 %collective-permute-start.8 = (bf16[4,256,256]{2,1,0:T(8,128)(2,1)S(1)}, bf16[4,256,256]{2,1,0:T(8,128)(2,1)S(1)}, u32[]{:S(2)}, u32[]{:S(2)}) collective-permute-start(bf16[4,256,256]{2,1,0:T(8,128)(2,1)S(1)} %all_to_all.20), channel_id=1, source_target_pairs={{0,8},{8,512},{512,520},{520,0},{1,9},{9,513},{513,521},{521,1},{2... | collective-permute-start | bytes 1572872 | tf_op jit(solution)/shard_map/ppermute | solution.py:13
  88.6 24.1 %all-to-all-start.2 = ((bf16[32,8,256]{2,1,0:T(8,128)(2,1)}), bf16[32,8,256]{2,1,0:T(8,128)(2,1)S(1)}, u32[]{:S(2)}, u32[]{:S(2)}) async-start(bf16[32,8,256]{2,1,0:T(8,128)(2,1)} %pad_maximum_fusion.3), calls=%async_computation.2 | async-start | bytes 262144 | tf_op jit(solution)/shard_map/all_to_all | solution.py:29
  112.8 4.5 %collective-permute-start.11 = (bf16[2,256,256]{2,1,0:T(8,128)(2,1)S(1)}, bf16[2,256,256]{2,1,0:T(8,128)(2,1)S(1)}, u32[]{:S(2)}, u32[]{:S(2)}) collective-permute-start(bf16[2,256,256]{2,1,0:T(8,128)(2,1)S(1)} %slice.37), channel_id=1, source_target_pairs={{0,520},{8,0},{512,8},{520,512},{1,521},{9,1},{513,9},{521,513},{2... | collective-permute-start | bytes 786440 | tf_op jit(solution)/shard_map/ppermute | solution.py:13
  117.3 1.9 %collective-permute-start.9 = (bf16[2,256,256]{2,1,0:T(8,128)(2,1)S(1)}, bf16[2,256,256]{2,1,0:T(8,128)(2,1)S(1)}, u32[]{:S(2)}, u32[]{:S(2)}) collective-permute-start(bf16[2,256,256]{2,1,0:T(8,128)(2,1)S(1)} %slice.36), channel_id=1, source_target_pairs={{0,8},{8,512},{512,520},{520,0},{1,9},{9,513},{513,521},{521,1},{2... | collective-permute-start | bytes 786440 | tf_op jit(solution)/shard_map/ppermute | solution.py:13
  119.4 1.3 collective-permute-done.11
  120.6 5.4 %collective-permute-done.9 = bf16[2,256,256]{2,1,0:T(8,128)(2,1)S(1)} collective-permute-done((bf16[2,256,256]{2,1,0:T(8,128)(2,1)S(1)}, bf16[2,256,256]{2,1,0:T(8,128)(2,1)S(1)}, u32[]{:S(2)}, u32[]{:S(2)}) %collective-permute-start.9) | collective-permute-done | bytes 262176 | tf_op jit(solution)/shard_map/ppermute | solution.py:13
  127.8 9.2 %all-to-all-start.3 = ((f32[8,8,256]{2,1,0:T(8,128)}), f32[8,8,256]{2,1,0:T(8,128)S(1)}, u32[]{:S(2)}, u32[]{:S(2)}) async-start(f32[8,8,256]{2,1,0:T(8,128)} %broadcast_in_dim.26), calls=%async_computation.3 | async-start | bytes 131072 | tf_op jit(solution)/shard_map/all_to_all | solution.py:90
  137.0 3.4 %convolution_convert_fusion = bf16[512,256]{1,0:T(8,128)(2,1)S(1)} fusion(bf16[512,4096]{1,0:T(8,128)(2,1)} %copy-done, bf16[4096,256]{1,0:T(8,128)(2,1)S(1)} %bitcast.45), kind=kOutput, calls=%fused_computation.4 | convolution fusion | flops 1073872896 | bytes 6553600 | tf_op jit(solution)/shard_map/dot_general | solution.py:96
  140.4 1.4 all-to-all-done.3
  141.9 2.7 %collective-permute-start.12 = (bf16[256,256]{1,0:T(8,128)(2,1)S(1)}, bf16[256,256]{1,0:T(8,128)(2,1)S(1)}, u32[]{:S(2)}, u32[]{:S(2)}) collective-permute-start(bf16[256,256]{1,0:T(8,128)(2,1)S(1)} %slice.35), channel_id=1, source_target_pairs={{0,1},{1,0},{2,3},{3,2},{4,5},{5,4},{6,7},{7,6},{8,9},{9,8},{10,11... | collective-permute-start | bytes 393224 | tf_op jit(solution)/shard_map/ppermute | solution.py:101
  144.6 1.0 collective-permute-done.12
  (34 shorter events, 6.2 us)
Async XLA Ops:
  0.6 22.4 %collective-permute-start = (bf16[256,4096]{1,0:T(8,128)(2,1)}, bf16[256,4096]{1,0:T(8,128)(2,1)S(1)}, u32[]{:S(2)}, u32[]{:S(2)}) collective-permute-start(bf16[256,4096]{1,0:T(8,128)(2,1)} %param.4), channel_id=1, source_target_pairs={{0,1},{1,0},{2,3},{3,2},{4,5},{5,4},{6,7},{7,6},{8,9},{9,8},{10,11... | collective-permute-start | bytes 6291464 | tf_op jit(solution)/shard_map/ppermute | solution.py:51
  17.7 5.5 %collective-permute-start.1 = (bf16[256,256]{1,0:T(8,128)(2,1)S(1)}, bf16[256,256]{1,0:T(8,128)(2,1)S(1)}, u32[]{:S(2)}, u32[]{:S(2)}) collective-permute-start(bf16[256,256]{1,0:T(8,128)(2,1)S(1)} %get-tuple-element.31), channel_id=1, source_target_pairs={{0,1},{1,0},{2,3},{3,2},{4,5},{5,4},{6,7},{7,6},{8,9},{9,8},{10,11... | collective-permute-start | bytes 393224 | tf_op jit(solution)/shard_map/ppermute | solution.py:54
  23.2 1.9 %copy-start = (bf16[512,4096]{1,0:T(8,128)(2,1)}, bf16[512,4096]{1,0:T(8,128)(2,1)S(1)}, u32[]{:S(2)}) copy-start(bf16[512,4096]{1,0:T(8,128)(2,1)S(1)} %constant_dynamic-update-slice_fusion) | copy-start | bytes 12582916
  26.7 25.9 %collective-permute-start.4 = (bf16[32,4,8,256]{3,2,1,0:T(8,128)(2,1)}, bf16[32,4,8,256]{3,2,1,0:T(8,128)(2,1)}, u32[]{:S(2)}, u32[]{:S(2)}) collective-permute-start(bf16[32,4,8,256]{3,2,1,0:T(8,128)(2,1)} %get-tuple-element.23), channel_id=1, source_target_pairs={{0,520},{8,0},{512,8},{520,512},{1,521},{9,1},{513,9},{521,513},{2... | collective-permute-start | bytes 1572872 | tf_op jit(solution)/shard_map/ppermute | solution.py:13
  28.6 27.4 %collective-permute-start.3 = (bf16[32,4,8,256]{3,2,1,0:T(8,128)(2,1)S(1)}, bf16[32,4,8,256]{3,2,1,0:T(8,128)(2,1)}, u32[]{:S(2)}, u32[]{:S(2)}) collective-permute-start(bf16[32,4,8,256]{3,2,1,0:T(8,128)(2,1)S(1)} %get-tuple-element.24), channel_id=1, source_target_pairs={{0,8},{8,512},{512,520},{520,0},{1,9},{9,513},{513,521},{521,1},{2... | collective-permute-start | bytes 1572872 | tf_op jit(solution)/shard_map/ppermute | solution.py:13
  32.0 24.1 %collective-permute-start.2 = (bf16[32,4,8,256]{3,2,1,0:T(8,128)(2,1)S(1)}, bf16[32,4,8,256]{3,2,1,0:T(8,128)(2,1)}, u32[]{:S(2)}, u32[]{:S(2)}) collective-permute-start(bf16[32,4,8,256]{3,2,1,0:T(8,128)(2,1)S(1)} %get-tuple-element.22), channel_id=1, source_target_pairs={{0,512},{8,520},{512,0},{520,8},{1,513},{9,521},{513,1},{521,9},{2... | collective-permute-start | bytes 1572872 | tf_op jit(solution)/shard_map/ppermute | solution.py:13
  34.0 37.6 %all-to-all-start = ((bf16[32,8,256]{2,1,0:T(8,128)(2,1)}), bf16[32,8,256]{2,1,0:T(8,128)(2,1)S(1)}, u32[]{:S(2)}, u32[]{:S(2)}) async-start(bf16[32,8,256]{2,1,0:T(8,128)(2,1)} %broadcast_in_dim.11), calls=%async_computation | async-start | bytes 262144 | tf_op jit(solution)/shard_map/all_to_all | solution.py:29
  57.9 7.2 %collective-permute-start.7 = (bf16[32,8,256]{2,1,0:T(8,128)(2,1)S(1)}, bf16[32,8,256]{2,1,0:T(8,128)(2,1)S(1)}, u32[]{:S(2)}, u32[]{:S(2)}) collective-permute-start(bf16[32,8,256]{2,1,0:T(8,128)(2,1)S(1)} %get-tuple-element.26), channel_id=1, source_target_pairs={{0,6},{2,0},{4,2},{6,4},{1,7},{3,1},{5,3},{7,5},{8,14},{10,8},{12,... | collective-permute-start | bytes 393224 | tf_op jit(solution)/shard_map/ppermute | solution.py:13
  59.8 7.2 %collective-permute-start.6 = (bf16[32,8,256]{2,1,0:T(8,128)(2,1)S(1)}, bf16[32,8,256]{2,1,0:T(8,128)(2,1)S(1)}, u32[]{:S(2)}, u32[]{:S(2)}) collective-permute-start(bf16[32,8,256]{2,1,0:T(8,128)(2,1)S(1)} %get-tuple-element.27), channel_id=1, source_target_pairs={{0,2},{2,4},{4,6},{6,0},{1,3},{3,5},{5,7},{7,1},{8,10},{10,12},{12... | collective-permute-start | bytes 393224 | tf_op jit(solution)/shard_map/ppermute | solution.py:13
  63.2 7.5 %collective-permute-start.5 = (bf16[32,8,256]{2,1,0:T(8,128)(2,1)S(1)}, bf16[32,8,256]{2,1,0:T(8,128)(2,1)S(1)}, u32[]{:S(2)}, u32[]{:S(2)}) collective-permute-start(bf16[32,8,256]{2,1,0:T(8,128)(2,1)S(1)} %get-tuple-element.25), channel_id=1, source_target_pairs={{0,4},{2,6},{4,0},{6,2},{1,5},{3,7},{5,1},{7,3},{8,12},{10,14},{12... | collective-permute-start | bytes 393224 | tf_op jit(solution)/shard_map/ppermute | solution.py:13
  82.6 30.2 %collective-permute-start.10 = (bf16[4,256,256]{2,1,0:T(8,128)(2,1)S(1)}, bf16[4,256,256]{2,1,0:T(8,128)(2,1)S(1)}, u32[]{:S(2)}, u32[]{:S(2)}) collective-permute-start(bf16[4,256,256]{2,1,0:T(8,128)(2,1)S(1)} %all_to_all.20), channel_id=1, source_target_pairs={{0,520},{8,0},{512,8},{520,512},{1,521},{9,1},{513,9},{521,513},{2... | collective-permute-start | bytes 1572872 | tf_op jit(solution)/shard_map/ppermute | solution.py:13
  85.1 32.2 %collective-permute-start.8 = (bf16[4,256,256]{2,1,0:T(8,128)(2,1)S(1)}, bf16[4,256,256]{2,1,0:T(8,128)(2,1)S(1)}, u32[]{:S(2)}, u32[]{:S(2)}) collective-permute-start(bf16[4,256,256]{2,1,0:T(8,128)(2,1)S(1)} %all_to_all.20), channel_id=1, source_target_pairs={{0,8},{8,512},{512,520},{520,0},{1,9},{9,513},{513,521},{521,1},{2... | collective-permute-start | bytes 1572872 | tf_op jit(solution)/shard_map/ppermute | solution.py:13
  88.6 38.4 %all-to-all-start.2 = ((bf16[32,8,256]{2,1,0:T(8,128)(2,1)}), bf16[32,8,256]{2,1,0:T(8,128)(2,1)S(1)}, u32[]{:S(2)}, u32[]{:S(2)}) async-start(bf16[32,8,256]{2,1,0:T(8,128)(2,1)} %pad_maximum_fusion.3), calls=%async_computation.2 | async-start | bytes 262144 | tf_op jit(solution)/shard_map/all_to_all | solution.py:29
  112.8 7.8 %collective-permute-start.11 = (bf16[2,256,256]{2,1,0:T(8,128)(2,1)S(1)}, bf16[2,256,256]{2,1,0:T(8,128)(2,1)S(1)}, u32[]{:S(2)}, u32[]{:S(2)}) collective-permute-start(bf16[2,256,256]{2,1,0:T(8,128)(2,1)S(1)} %slice.37), channel_id=1, source_target_pairs={{0,520},{8,0},{512,8},{520,512},{1,521},{9,1},{513,9},{521,513},{2... | collective-permute-start | bytes 786440 | tf_op jit(solution)/shard_map/ppermute | solution.py:13
  117.3 8.6 %collective-permute-start.9 = (bf16[2,256,256]{2,1,0:T(8,128)(2,1)S(1)}, bf16[2,256,256]{2,1,0:T(8,128)(2,1)S(1)}, u32[]{:S(2)}, u32[]{:S(2)}) collective-permute-start(bf16[2,256,256]{2,1,0:T(8,128)(2,1)S(1)} %slice.36), channel_id=1, source_target_pairs={{0,8},{8,512},{512,520},{520,0},{1,9},{9,513},{513,521},{521,1},{2... | collective-permute-start | bytes 786440 | tf_op jit(solution)/shard_map/ppermute | solution.py:13
  127.8 14.1 %all-to-all-start.3 = ((f32[8,8,256]{2,1,0:T(8,128)}), f32[8,8,256]{2,1,0:T(8,128)S(1)}, u32[]{:S(2)}, u32[]{:S(2)}) async-start(f32[8,8,256]{2,1,0:T(8,128)} %broadcast_in_dim.26), calls=%async_computation.3 | async-start | bytes 131072 | tf_op jit(solution)/shard_map/all_to_all | solution.py:90
  141.9 3.7 %collective-permute-start.12 = (bf16[256,256]{1,0:T(8,128)(2,1)S(1)}, bf16[256,256]{1,0:T(8,128)(2,1)S(1)}, u32[]{:S(2)}, u32[]{:S(2)}) collective-permute-start(bf16[256,256]{1,0:T(8,128)(2,1)S(1)} %slice.35), channel_id=1, source_target_pairs={{0,1},{1,0},{2,3},{3,2},{4,5},{5,4},{6,7},{7,6},{8,9},{9,8},{10,11... | collective-permute-start | bytes 393224 | tf_op jit(solution)/shard_map/ppermute | solution.py:101

commit v9 on v7

--- a/solution.py
+++ b/solution.py
@@ -49,9 +49,7 @@
     factor = float(tok * n_z * 32) ** (-0.5)
 
     other_act = lax.ppermute(activations, "c", SWAP)
-    my_cot = lax.dynamic_slice(cotangent, (0, c * half), (tok, half))
-    send_cot = lax.dynamic_slice(cotangent, (0, (1 - c) * half), (tok, half))
-    other_cot = lax.ppermute(send_cot, "c", SWAP)
+    other_cot = lax.ppermute(cotangent, "c", SWAP)
 
     blocks = half // BLOCK
     codes = lax.dynamic_slice(weight_codes, (y * rows, c * half), (rows, half))
@@ -62,11 +60,11 @@
 
     dims = (((0,), (0,)), ((), ()))
     acts = jnp.concatenate([activations, other_act], axis=0)
-    cots = jnp.concatenate([my_cot, other_cot], axis=0)
+    cots = jnp.concatenate([cotangent, other_cot], axis=0)
+    cots = lax.dynamic_slice(cots, (0, c * half), (2 * tok, half))
     grad = lax.dot_general(acts, cots, dims, preferred_element_type=f32)
     grad = (grad * factor).astype(bf16)
     grad = grad.reshape(2, n_z, 2, 4, rows, half)
-    grad, spread = lax.optimization_barrier((grad, spread))
     first = 3 * n_z // 4
     col = over_z(spread, first)
 

time: 140 us -> 138 us (0.986)
    ppermute x9, waiting for transfers between devices: 9.03 us -> 6.75 us  [around(): return lax.ppermute(value, axes, [(i, (i + shift) % 4) for i in range(4)])]
    all_to_all x2, waiting for transfers between devices: 0.82 us -> 2.59 us  [over_z(): lax.all_to_all(value, 'z', split_axis=0, concat_axis=0, axis_index_groups...]
    unnamed x6 -> x10, local copies, waits for them, and re-layouts: 4.86 us -> 4.67 us
  transfers between devices with their start and end apart: 15 -> 15, of which waited for: 6 -> 9; matrix products, arithmetic and copies ran while one was open for 7% -> 6% of each run, Pallas kernels for 0% -> 0%
where the time goes in v9:
time: 138 us
  starting transfers between devices  95.7 us (69%)
  waiting for transfers between devices  14.8 us (11%)
  blocking collectives  10.9 us (8%)
  local copies, waits for them, and re-layouts  7.69 us (6%)
  other arithmetic  4.62 us (3%)
  matrix products  2.55 us (2%)
    all_to_all x2, starting transfers between devices, over_z(): lax.all_to_all(value, 'z', split_axis=0, concat_axis=0, axis_index_groups...  42.6 us
    ppermute x9, starting transfers between devices, around(): return lax.ppermute(value, axes, [(i, (i + shift) % 4) for i in range(4)])  24.4 us
    ppermute x1, starting transfers between devices, body(): other_act = lax.ppermute(activations, 'c', SWAP)  16.1 us
    all_to_all x1, blocking collectives, body(): slab = lax.all_to_all(slab, 'y', split_axis=0, concat_axis=0, tiled=True)  10.9 us
    ppermute x9, waiting for transfers between devices, around(): return lax.ppermute(value, axes, [(i, (i + shift) % 4) for i in range(4)])  6.75 us
    ppermute x1, starting transfers between devices, body(): got = lax.ppermute(proj[tok:], 'c', SWAP)  5.53 us
    all_to_all x1, starting transfers between devices, body(): lax.all_to_all(pieces, ('y', 'c'), split_axis=0, concat_axis=0, tiled=True)  5.16 us
    unnamed x10, local copies, waits for them, and re-layouts  4.67 us
  transfers between devices with their start and end apart: 15, of which 9 were waited for; matrix products, arithmetic and copies ran while one was open for 6% of the time, Pallas kernels for 0%

profile of v9, /device:TPU:1, one launch (start us, length us, event | category | flops | bytes accessed | tf_op | source)
XLA Modules:
  0.0 137.5 jit_solution(3803550999807901273)
XLA Ops:
  0.6 16.1 %collective-permute-start = (bf16[256,4096]{1,0:T(8,128)(2,1)}, bf16[256,4096]{1,0:T(8,128)(2,1)S(1)}, u32[]{:S(2)}, u32[]{:S(2)}) collective-permute-start(bf16[256,4096]{1,0:T(8,128)(2,1)} %param.4), channel_id=1, source_target_pairs={{0,1},{1,0},{2,3},{3,2},{4,5},{5,4},{6,7},{7,6},{8,9},{9,8},{10,11... | collective-permute-start | bytes 6291464 | tf_op jit(solution)/shard_map/ppermute | solution.py:51
  16.7 1.9 %collective-permute-start.1 = (bf16[256,512]{1,0:T(8,128)(2,1)}, bf16[256,512]{1,0:T(8,128)(2,1)S(1)}, u32[]{:S(2)}, u32[]{:S(2)}) collective-permute-start(bf16[256,512]{1,0:T(8,128)(2,1)} %param.7), channel_id=1, source_target_pairs={{0,1},{1,0},{2,3},{3,2},{4,5},{5,4},{6,7},{7,6},{8,9},{9,8},{10,11... | collective-permute-start | bytes 786440 | tf_op jit(solution)/shard_map/ppermute | solution.py:52
  18.8 1.7 %constant_dynamic-update-slice_fusion.1 = bf16[512,4096]{1,0:T(8,128)(2,1)S(1)} fusion(bf16[256,4096]{1,0:T(8,128)(2,1)} %param.4), kind=kLoop, calls=%fused_computation.31 | loop fusion | bytes 4194304
  21.5 1.3 fusion
  22.8 1.0 dynamic-slice_bitcast_fusion.2
  23.8 1.9 %collective-permute-start.4 = (bf16[32,4,8,256]{3,2,1,0:T(8,128)(2,1)}, bf16[32,4,8,256]{3,2,1,0:T(8,128)(2,1)}, u32[]{:S(2)}, u32[]{:S(2)}) collective-permute-start(bf16[32,4,8,256]{3,2,1,0:T(8,128)(2,1)} %get-tuple-element.21), channel_id=1, source_target_pairs={{0,520},{8,0},{512,8},{520,512},{1,521},{9,1},{513,9},{521,513},{2... | collective-permute-start | bytes 1572872 | tf_op jit(solution)/shard_map/ppermute | solution.py:13
  25.7 3.4 %collective-permute-start.3 = (bf16[32,4,8,256]{3,2,1,0:T(8,128)(2,1)S(1)}, bf16[32,4,8,256]{3,2,1,0:T(8,128)(2,1)}, u32[]{:S(2)}, u32[]{:S(2)}) collective-permute-start(bf16[32,4,8,256]{3,2,1,0:T(8,128)(2,1)S(1)} %get-tuple-element.22), channel_id=1, source_target_pairs={{0,8},{8,512},{512,520},{520,0},{1,9},{9,513},{513,521},{521,1},{2... | collective-permute-start | bytes 1572872 | tf_op jit(solution)/shard_map/ppermute | solution.py:13
  29.0 1.9 %collective-permute-start.2 = (bf16[32,4,8,256]{3,2,1,0:T(8,128)(2,1)S(1)}, bf16[32,4,8,256]{3,2,1,0:T(8,128)(2,1)}, u32[]{:S(2)}, u32[]{:S(2)}) collective-permute-start(bf16[32,4,8,256]{3,2,1,0:T(8,128)(2,1)S(1)} %get-tuple-element.20), channel_id=1, source_target_pairs={{0,512},{8,520},{512,0},{520,8},{1,513},{9,521},{513,1},{521,9},{2... | collective-permute-start | bytes 1572872 | tf_op jit(solution)/shard_map/ppermute | solution.py:13
  31.1 0.8 fusion.9
  31.8 0.7 broadcast_in_dim.11
  32.5 18.6 %all-to-all-start = ((bf16[32,8,256]{2,1,0:T(8,128)(2,1)}), bf16[32,8,256]{2,1,0:T(8,128)(2,1)S(1)}, u32[]{:S(2)}, u32[]{:S(2)}) async-start(bf16[32,8,256]{2,1,0:T(8,128)(2,1)} %broadcast_in_dim.11), calls=%async_computation | async-start | bytes 262144 | tf_op jit(solution)/shard_map/all_to_all | solution.py:29
  51.2 2.0 %collective-permute-done.3 = bf16[32,4,8,256]{3,2,1,0:T(8,128)(2,1)} collective-permute-done((bf16[32,4,8,256]{3,2,1,0:T(8,128)(2,1)S(1)}, bf16[32,4,8,256]{3,2,1,0:T(8,128)(2,1)}, u32[]{:S(2)}, u32[]{:S(2)}) %collective-permute-start.3) | collective-permute-done | bytes 524320 | tf_op jit(solution)/shard_map/ppermute | solution.py:13
  53.1 1.7 %fusion.3 = bf16[32,4,8,256]{3,2,1,0:T(8,128)(2,1)S(1)} fusion(bf16[32,4,8,256]{3,2,1,0:T(8,128)(2,1)} %collective-permute-done.4, bf16[32,4,8,256]{3,2,1,0:T(8,128)(2,1)} %collective-permute-done.3, bf16[32,4,8,256]{3,2,1,0:T(8,128)(2,1)} %collective-permute-done.2, bf16[2,32,2,4,8,256]{5,4,3,2,1,0:T(8,128)(2,1)S(1)} %bitcast.43, s32[]{:T(128)S(6)} %select_n.150, ...), kind=kLoop, calls=%fused_computation.8 | loop fusion | flops 2097152 | bytes 2621448 | tf_op jit(solution)/shard_map/convert_element_type | solution.py:23
  54.9 2.7 %collective-permute-start.7 = (bf16[32,8,256]{2,1,0:T(8,128)(2,1)S(1)}, bf16[32,8,256]{2,1,0:T(8,128)(2,1)S(1)}, u32[]{:S(2)}, u32[]{:S(2)}) collective-permute-start(bf16[32,8,256]{2,1,0:T(8,128)(2,1)S(1)} %get-tuple-element.24), channel_id=1, source_target_pairs={{0,6},{2,0},{4,2},{6,4},{1,7},{3,1},{5,3},{7,5},{8,14},{10,8},{12,... | collective-permute-start | bytes 393224 | tf_op jit(solution)/shard_map/ppermute | solution.py:13
  57.6 2.6 %collective-permute-start.6 = (bf16[32,8,256]{2,1,0:T(8,128)(2,1)S(1)}, bf16[32,8,256]{2,1,0:T(8,128)(2,1)S(1)}, u32[]{:S(2)}, u32[]{:S(2)}) collective-permute-start(bf16[32,8,256]{2,1,0:T(8,128)(2,1)S(1)} %get-tuple-element.25), channel_id=1, source_target_pairs={{0,2},{2,4},{4,6},{6,0},{1,3},{3,5},{5,7},{7,1},{8,10},{10,12},{12... | collective-permute-start | bytes 393224 | tf_op jit(solution)/shard_map/ppermute | solution.py:13
  60.2 2.9 %collective-permute-start.5 = (bf16[32,8,256]{2,1,0:T(8,128)(2,1)S(1)}, bf16[32,8,256]{2,1,0:T(8,128)(2,1)S(1)}, u32[]{:S(2)}, u32[]{:S(2)}) collective-permute-start(bf16[32,8,256]{2,1,0:T(8,128)(2,1)S(1)} %get-tuple-element.23), channel_id=1, source_target_pairs={{0,4},{2,6},{4,0},{6,2},{1,5},{3,7},{5,1},{7,3},{8,12},{10,14},{12... | collective-permute-start | bytes 393224 | tf_op jit(solution)/shard_map/ppermute | solution.py:13
  63.1 1.7 %collective-permute-done.6 = bf16[32,8,256]{2,1,0:T(8,128)(2,1)S(1)} collective-permute-done((bf16[32,8,256]{2,1,0:T(8,128)(2,1)S(1)}, bf16[32,8,256]{2,1,0:T(8,128)(2,1)S(1)}, u32[]{:S(2)}, u32[]{:S(2)}) %collective-permute-start.6) | collective-permute-done | bytes 131104 | tf_op jit(solution)/shard_map/ppermute | solution.py:13
  64.8 3.1 %collective-permute-done.5 = bf16[32,8,256]{2,1,0:T(8,128)(2,1)S(1)} collective-permute-done((bf16[32,8,256]{2,1,0:T(8,128)(2,1)S(1)}, bf16[32,8,256]{2,1,0:T(8,128)(2,1)S(1)}, u32[]{:S(2)}, u32[]{:S(2)}) %collective-permute-start.5) | collective-permute-done | bytes 131104 | tf_op jit(solution)/shard_map/ppermute | solution.py:13
  68.0 2.1 %all-to-all-done = bf16[32,8,256]{2,1,0:T(8,128)(2,1)S(1)} async-done(((bf16[32,8,256]{2,1,0:T(8,128)(2,1)}), bf16[32,8,256]{2,1,0:T(8,128)(2,1)S(1)}, u32[]{:S(2)}, u32[]{:S(2)}) %all-to-all-start) | async-done | bytes 131104 | tf_op jit(solution)/shard_map/all_to_all | solution.py:29
  70.2 10.9 %all_to_all.20 = bf16[4,256,256]{2,1,0:T(8,128)(2,1)S(1)} all-to-all(bf16[4,256,256]{2,1,0:T(8,128)(2,1)S(1)} %broadcast_in_dim.25), channel_id=1, replica_groups=mesh['xh'=2,'z'=32,'xl'=2,'y'=4,'c'=2] {'y'}, dimensions={0} | all-to-all | bytes 1048576 | tf_op jit(solution)/shard_map/all_to_all | solution.py:81
  81.1 2.5 %collective-permute-start.10 = (bf16[4,256,256]{2,1,0:T(8,128)(2,1)S(1)}, bf16[4,256,256]{2,1,0:T(8,128)(2,1)S(1)}, u32[]{:S(2)}, u32[]{:S(2)}) collective-permute-start(bf16[4,256,256]{2,1,0:T(8,128)(2,1)S(1)} %all_to_all.20), channel_id=1, source_target_pairs={{0,520},{8,0},{512,8},{520,512},{1,521},{9,1},{513,9},{521,513},{2... | collective-permute-start | bytes 1572872 | tf_op jit(solution)/shard_map/ppermute | solution.py:13
  83.6 4.6 %collective-permute-start.9 = (bf16[4,256,256]{2,1,0:T(8,128)(2,1)S(1)}, bf16[4,256,256]{2,1,0:T(8,128)(2,1)S(1)}, u32[]{:S(2)}, u32[]{:S(2)}) collective-permute-start(bf16[4,256,256]{2,1,0:T(8,128)(2,1)S(1)} %all_to_all.20), channel_id=1, source_target_pairs={{0,512},{8,520},{512,0},{520,8},{1,513},{9,521},{513,1},{521,9},{2... | collective-permute-start | bytes 1572872 | tf_op jit(solution)/shard_map/ppermute | solution.py:13
  88.2 1.9 %collective-permute-start.8 = (bf16[4,256,256]{2,1,0:T(8,128)(2,1)S(1)}, bf16[4,256,256]{2,1,0:T(8,128)(2,1)S(1)}, u32[]{:S(2)}, u32[]{:S(2)}) collective-permute-start(bf16[4,256,256]{2,1,0:T(8,128)(2,1)S(1)} %all_to_all.20), channel_id=1, source_target_pairs={{0,8},{8,512},{512,520},{520,0},{1,9},{9,513},{513,521},{521,1},{2... | collective-permute-start | bytes 1572872 | tf_op jit(solution)/shard_map/ppermute | solution.py:13
  90.3 0.7 pad_maximum_fusion.3
  90.9 24.0 %all-to-all-start.2 = ((bf16[32,8,256]{2,1,0:T(8,128)(2,1)}), bf16[32,8,256]{2,1,0:T(8,128)(2,1)S(1)}, u32[]{:S(2)}, u32[]{:S(2)}) async-start(bf16[32,8,256]{2,1,0:T(8,128)(2,1)} %pad_maximum_fusion.3), calls=%async_computation.2 | async-start | bytes 262144 | tf_op jit(solution)/shard_map/all_to_all | solution.py:29
  116.0 1.9 %copy-done.1 = bf16[512,4096]{1,0:T(8,128)(2,1)S(1)} copy-done((bf16[512,4096]{1,0:T(8,128)(2,1)S(1)}, bf16[512,4096]{1,0:T(8,128)(2,1)}, u32[]{:S(2)}) %copy-start.1) | copy-done | bytes 4194328
  117.9 1.2 convolution_convert_fusion
  119.2 5.5 %collective-permute-start.11 = (bf16[256,256]{1,0:T(8,128)(2,1)S(1)}, bf16[256,256]{1,0:T(8,128)(2,1)S(1)}, u32[]{:S(2)}, u32[]{:S(2)}) collective-permute-start(bf16[256,256]{1,0:T(8,128)(2,1)S(1)} %get-tuple-element.29), channel_id=1, source_target_pairs={{0,1},{1,0},{2,3},{3,2},{4,5},{5,4},{6,7},{7,6},{8,9},{9,8},{10,11... | collective-permute-start | bytes 393224 | tf_op jit(solution)/shard_map/ppermute | solution.py:93
  124.8 1.0 collective-permute-done.11
  126.9 5.2 %all-to-all-start.3 = ((f32[8,8,256]{2,1,0:T(8,128)}), f32[8,8,256]{2,1,0:T(8,128)S(1)}, u32[]{:S(2)}, u32[]{:S(2)}) async-start(f32[8,8,256]{2,1,0:T(8,128)} %broadcast_in_dim.26), calls=%async_computation.3 | async-start | bytes 131072 | tf_op jit(solution)/shard_map/all_to_all | solution.py:98
  132.0 0.7 pad_maximum_fusion.2
  132.8 4.1 %all-to-all-done.3 = f32[8,8,256]{2,1,0:T(8,128)S(1)} async-done(((f32[8,8,256]{2,1,0:T(8,128)}), f32[8,8,256]{2,1,0:T(8,128)S(1)}, u32[]{:S(2)}, u32[]{:S(2)}) %all-to-all-start.3) | async-done | bytes 65568 | tf_op jit(solution)/shard_map/all_to_all | solution.py:98
  (34 shorter events, 4.1 us)
Async XLA Ops:
  0.6 20.0 %collective-permute-start = (bf16[256,4096]{1,0:T(8,128)(2,1)}, bf16[256,4096]{1,0:T(8,128)(2,1)S(1)}, u32[]{:S(2)}, u32[]{:S(2)}) collective-permute-start(bf16[256,4096]{1,0:T(8,128)(2,1)} %param.4), channel_id=1, source_target_pairs={{0,1},{1,0},{2,3},{3,2},{4,5},{5,4},{6,7},{7,6},{8,9},{9,8},{10,11... | collective-permute-start | bytes 6291464 | tf_op jit(solution)/shard_map/ppermute | solution.py:51
  16.7 4.3 %collective-permute-start.1 = (bf16[256,512]{1,0:T(8,128)(2,1)}, bf16[256,512]{1,0:T(8,128)(2,1)S(1)}, u32[]{:S(2)}, u32[]{:S(2)}) collective-permute-start(bf16[256,512]{1,0:T(8,128)(2,1)} %param.7), channel_id=1, source_target_pairs={{0,1},{1,0},{2,3},{3,2},{4,5},{5,4},{6,7},{7,6},{8,9},{9,8},{10,11... | collective-permute-start | bytes 786440 | tf_op jit(solution)/shard_map/ppermute | solution.py:52
  20.5 1.0 copy-start.3
  20.8 2.0 %copy-start = (bf16[512,4096]{1,0:T(8,128)(2,1)}, bf16[512,4096]{1,0:T(8,128)(2,1)S(1)}, u32[]{:S(2)}) copy-start(bf16[512,4096]{1,0:T(8,128)(2,1)S(1)} %constant_dynamic-update-slice_fusion) | copy-start | bytes 12582916
  22.8 8.2 %copy-start.2 = (bf16[32,4]{0,1:T(4,128)(2,1)S(1)}, bf16[32,4]{0,1:T(4,128)(2,1)}, u32[]{:S(2)}) copy-start(bf16[32,4]{0,1:T(4,128)(2,1)} %param.6) | copy-start | bytes 772
  23.8 27.4 %collective-permute-start.4 = (bf16[32,4,8,256]{3,2,1,0:T(8,128)(2,1)}, bf16[32,4,8,256]{3,2,1,0:T(8,128)(2,1)}, u32[]{:S(2)}, u32[]{:S(2)}) collective-permute-start(bf16[32,4,8,256]{3,2,1,0:T(8,128)(2,1)} %get-tuple-element.21), channel_id=1, source_target_pairs={{0,520},{8,0},{512,8},{520,512},{1,521},{9,1},{513,9},{521,513},{2... | collective-permute-start | bytes 1572872 | tf_op jit(solution)/shard_map/ppermute | solution.py:13
  25.7 27.4 %collective-permute-start.3 = (bf16[32,4,8,256]{3,2,1,0:T(8,128)(2,1)S(1)}, bf16[32,4,8,256]{3,2,1,0:T(8,128)(2,1)}, u32[]{:S(2)}, u32[]{:S(2)}) collective-permute-start(bf16[32,4,8,256]{3,2,1,0:T(8,128)(2,1)S(1)} %get-tuple-element.22), channel_id=1, source_target_pairs={{0,8},{8,512},{512,520},{520,0},{1,9},{9,513},{513,521},{521,1},{2... | collective-permute-start | bytes 1572872 | tf_op jit(solution)/shard_map/ppermute | solution.py:13
  29.0 24.1 %collective-permute-start.2 = (bf16[32,4,8,256]{3,2,1,0:T(8,128)(2,1)S(1)}, bf16[32,4,8,256]{3,2,1,0:T(8,128)(2,1)}, u32[]{:S(2)}, u32[]{:S(2)}) collective-permute-start(bf16[32,4,8,256]{3,2,1,0:T(8,128)(2,1)S(1)} %get-tuple-element.20), channel_id=1, source_target_pairs={{0,512},{8,520},{512,0},{520,8},{1,513},{9,521},{513,1},{521,9},{2... | collective-permute-start | bytes 1572872 | tf_op jit(solution)/shard_map/ppermute | solution.py:13
  32.5 37.6 %all-to-all-start = ((bf16[32,8,256]{2,1,0:T(8,128)(2,1)}), bf16[32,8,256]{2,1,0:T(8,128)(2,1)S(1)}, u32[]{:S(2)}, u32[]{:S(2)}) async-start(bf16[32,8,256]{2,1,0:T(8,128)(2,1)} %broadcast_in_dim.11), calls=%async_computation | async-start | bytes 262144 | tf_op jit(solution)/shard_map/all_to_all | solution.py:29
  54.9 8.2 %collective-permute-start.7 = (bf16[32,8,256]{2,1,0:T(8,128)(2,1)S(1)}, bf16[32,8,256]{2,1,0:T(8,128)(2,1)S(1)}, u32[]{:S(2)}, u32[]{:S(2)}) collective-permute-start(bf16[32,8,256]{2,1,0:T(8,128)(2,1)S(1)} %get-tuple-element.24), channel_id=1, source_target_pairs={{0,6},{2,0},{4,2},{6,4},{1,7},{3,1},{5,3},{7,5},{8,14},{10,8},{12,... | collective-permute-start | bytes 393224 | tf_op jit(solution)/shard_map/ppermute | solution.py:13
  57.6 7.2 %collective-permute-start.6 = (bf16[32,8,256]{2,1,0:T(8,128)(2,1)S(1)}, bf16[32,8,256]{2,1,0:T(8,128)(2,1)S(1)}, u32[]{:S(2)}, u32[]{:S(2)}) collective-permute-start(bf16[32,8,256]{2,1,0:T(8,128)(2,1)S(1)} %get-tuple-element.25), channel_id=1, source_target_pairs={{0,2},{2,4},{4,6},{6,0},{1,3},{3,5},{5,7},{7,1},{8,10},{10,12},{12... | collective-permute-start | bytes 393224 | tf_op jit(solution)/shard_map/ppermute | solution.py:13
  60.2 7.7 %collective-permute-start.5 = (bf16[32,8,256]{2,1,0:T(8,128)(2,1)S(1)}, bf16[32,8,256]{2,1,0:T(8,128)(2,1)S(1)}, u32[]{:S(2)}, u32[]{:S(2)}) collective-permute-start(bf16[32,8,256]{2,1,0:T(8,128)(2,1)S(1)} %get-tuple-element.23), channel_id=1, source_target_pairs={{0,4},{2,6},{4,0},{6,2},{1,5},{3,7},{5,1},{7,3},{8,12},{10,14},{12... | collective-permute-start | bytes 393224 | tf_op jit(solution)/shard_map/ppermute | solution.py:13
  81.1 33.9 %collective-permute-start.10 = (bf16[4,256,256]{2,1,0:T(8,128)(2,1)S(1)}, bf16[4,256,256]{2,1,0:T(8,128)(2,1)S(1)}, u32[]{:S(2)}, u32[]{:S(2)}) collective-permute-start(bf16[4,256,256]{2,1,0:T(8,128)(2,1)S(1)} %all_to_all.20), channel_id=1, source_target_pairs={{0,520},{8,0},{512,8},{520,512},{1,521},{9,1},{513,9},{521,513},{2... | collective-permute-start | bytes 1572872 | tf_op jit(solution)/shard_map/ppermute | solution.py:13
  83.6 31.4 %collective-permute-start.9 = (bf16[4,256,256]{2,1,0:T(8,128)(2,1)S(1)}, bf16[4,256,256]{2,1,0:T(8,128)(2,1)S(1)}, u32[]{:S(2)}, u32[]{:S(2)}) collective-permute-start(bf16[4,256,256]{2,1,0:T(8,128)(2,1)S(1)} %all_to_all.20), channel_id=1, source_target_pairs={{0,512},{8,520},{512,0},{520,8},{1,513},{9,521},{513,1},{521,9},{2... | collective-permute-start | bytes 1572872 | tf_op jit(solution)/shard_map/ppermute | solution.py:13
  88.2 26.8 %collective-permute-start.8 = (bf16[4,256,256]{2,1,0:T(8,128)(2,1)S(1)}, bf16[4,256,256]{2,1,0:T(8,128)(2,1)S(1)}, u32[]{:S(2)}, u32[]{:S(2)}) collective-permute-start(bf16[4,256,256]{2,1,0:T(8,128)(2,1)S(1)} %all_to_all.20), channel_id=1, source_target_pairs={{0,8},{8,512},{512,520},{520,0},{1,9},{9,513},{513,521},{521,1},{2... | collective-permute-start | bytes 1572872 | tf_op jit(solution)/shard_map/ppermute | solution.py:13
  90.9 35.3 %all-to-all-start.2 = ((bf16[32,8,256]{2,1,0:T(8,128)(2,1)}), bf16[32,8,256]{2,1,0:T(8,128)(2,1)S(1)}, u32[]{:S(2)}, u32[]{:S(2)}) async-start(bf16[32,8,256]{2,1,0:T(8,128)(2,1)} %pad_maximum_fusion.3), calls=%async_computation.2 | async-start | bytes 262144 | tf_op jit(solution)/shard_map/all_to_all | solution.py:29
  115.7 2.2 %copy-start.1 = (bf16[512,4096]{1,0:T(8,128)(2,1)S(1)}, bf16[512,4096]{1,0:T(8,128)(2,1)}, u32[]{:S(2)}) copy-start(bf16[512,4096]{1,0:T(8,128)(2,1)} %copy-done) | copy-start | bytes 12582916
  119.2 6.5 %collective-permute-start.11 = (bf16[256,256]{1,0:T(8,128)(2,1)S(1)}, bf16[256,256]{1,0:T(8,128)(2,1)S(1)}, u32[]{:S(2)}, u32[]{:S(2)}) collective-permute-start(bf16[256,256]{1,0:T(8,128)(2,1)S(1)} %get-tuple-element.29), channel_id=1, source_target_pairs={{0,1},{1,0},{2,3},{3,2},{4,5},{5,4},{6,7},{7,6},{8,9},{9,8},{10,11... | collective-permute-start | bytes 393224 | tf_op jit(solution)/shard_map/ppermute | solution.py:93
  126.9 10.0 %all-to-all-start.3 = ((f32[8,8,256]{2,1,0:T(8,128)}), f32[8,8,256]{2,1,0:T(8,128)S(1)}, u32[]{:S(2)}, u32[]{:S(2)}) async-start(f32[8,8,256]{2,1,0:T(8,128)} %broadcast_in_dim.26), calls=%async_computation.3 | async-start | bytes 131072 | tf_op jit(solution)/shard_map/all_to_all | solution.py:98

commit v10 on v9

--- a/solution.py
+++ b/solution.py
@@ -65,7 +65,7 @@
     grad = lax.dot_general(acts, cots, dims, preferred_element_type=f32)
     grad = (grad * factor).astype(bf16)
     grad = grad.reshape(2, n_z, 2, 4, rows, half)
-    first = 3 * n_z // 4
+    first = 11 * n_z // 16
     col = over_z(spread, first)
 
     def to_x(k):
@@ -73,8 +73,13 @@
         return lax.dynamic_slice(grad, start, (1, n_z, 1, 4, rows, half)).reshape(n_z, 4, rows, half)
 
     line = spread_sum(to_x, X)
-    plane = spread_sum(lambda k: lax.dynamic_index_in_dim(line, k, 1, keepdims=False), "y")
-    col, plane = lax.optimization_barrier((col, plane))
+    y_piece = lambda k: lax.dynamic_index_in_dim(line, k, 1, keepdims=False)
+    parts = [around(y_piece((y + shift) % 4), "y", shift) for shift in (2, 1, 3)]
+    col, parts[0], parts[1] = lax.optimization_barrier((col, parts[0], parts[1]))
+    total = y_piece(y).astype(f32)
+    for part in parts:
+        total += part.astype(f32)
+    plane = total.astype(bf16)
     col = jnp.roll(col, first, axis=0)
 
     slab = jnp.broadcast_to(col.reshape(1, column, half), (4, column, half))

time: 138 us -> 139 us (level)
  blocking collectives: 10.9 us -> 0 us
  starting transfers between devices: 95.7 us -> 103 us
  waiting for transfers between devices: 14.8 us -> 16.9 us
    all_to_all x1 -> x0, blocking collectives: 10.9 us -> none  [body(): slab = lax.all_to_all(slab, 'y', split_axis=0, concat_axis=0, tiled=True)]
    all_to_all x2, waiting for transfers between devices: 2.59 us -> 7.04 us  [over_z(): lax.all_to_all(value, 'z', split_axis=0, concat_axis=0, axis_index_groups...]
    all_to_all x0 -> x1, starting transfers between devices: none -> 4.18 us  [body(): slab = lax.all_to_all(slab, 'y', split_axis=0, concat_axis=0, tiled=True)]
    ppermute x9, waiting for transfers between devices: 6.75 us -> 4.77 us  [around(): return lax.ppermute(value, axes, [(i, (i + shift) % 4) for i in range(4)])]
    ppermute x9, starting transfers between devices: 24.4 us -> 26.2 us  [around(): return lax.ppermute(value, axes, [(i, (i + shift) % 4) for i in range(4)])]
    unnamed x10 -> x8, local copies, waits for them, and re-layouts: 4.67 us -> 5.02 us
  transfers between devices with their start and end apart: 15 -> 16, of which waited for: 9 -> 6; matrix products, arithmetic and copies ran while one was open for 6% -> 7% of each run, Pallas kernels for 0% -> 0%
where the time goes in v10:
time: 139 us; the launch traced here: 138 us
  starting transfers between devices  103 us (74%)
  waiting for transfers between devices  16.9 us (12%)
  local copies, waits for them, and re-layouts  8.85 us (6%)
  other arithmetic  5.3 us (4%)
  matrix products  2.55 us (2%)
    all_to_all x2, starting transfers between devices, over_z(): lax.all_to_all(value, 'z', split_axis=0, concat_axis=0, axis_index_groups...  43.5 us
    ppermute x9, starting transfers between devices, around(): return lax.ppermute(value, axes, [(i, (i + shift) % 4) for i in range(4)])  26.2 us
    ppermute x1, starting transfers between devices, body(): other_act = lax.ppermute(activations, 'c', SWAP)  16.1 us
    all_to_all x2, waiting for transfers between devices, over_z(): lax.all_to_all(value, 'z', split_axis=0, concat_axis=0, axis_index_groups...  7.04 us
    ppermute x1, starting transfers between devices, body(): got = lax.ppermute(proj[tok:], 'c', SWAP)  5.86 us
    all_to_all x1, starting transfers between devices, body(): lax.all_to_all(pieces, ('y', 'c'), split_axis=0, concat_axis=0, tiled=True)  5.65 us
    unnamed x8, local copies, waits for them, and re-layouts  5.02 us
    ppermute x9, waiting for transfers between devices, around(): return lax.ppermute(value, axes, [(i, (i + shift) % 4) for i in range(4)])  4.77 us
  transfers between devices with their start and end apart: 16, of which 6 were waited for; matrix products, arithmetic and copies ran while one was open for 7% of the time, Pallas kernels for 0%

profile of v10, /device:TPU:1, one launch (start us, length us, event | category | flops | bytes accessed | tf_op | source)
XLA Modules:
  0.0 138.2 jit_solution(7180833440426405812)
XLA Ops:
  0.6 16.1 %collective-permute-start = (bf16[256,4096]{1,0:T(8,128)(2,1)}, bf16[256,4096]{1,0:T(8,128)(2,1)S(1)}, u32[]{:S(2)}, u32[]{:S(2)}) collective-permute-start(bf16[256,4096]{1,0:T(8,128)(2,1)} %param.4), channel_id=1, source_target_pairs={{0,1},{1,0},{2,3},{3,2},{4,5},{5,4},{6,7},{7,6},{8,9},{9,8},{10,11... | collective-permute-start | bytes 6291464 | tf_op jit(solution)/shard_map/ppermute | solution.py:51
  16.7 1.9 %collective-permute-start.1 = (bf16[256,512]{1,0:T(8,128)(2,1)}, bf16[256,512]{1,0:T(8,128)(2,1)S(1)}, u32[]{:S(2)}, u32[]{:S(2)}) collective-permute-start(bf16[256,512]{1,0:T(8,128)(2,1)} %param.7), channel_id=1, source_target_pairs={{0,1},{1,0},{2,3},{3,2},{4,5},{5,4},{6,7},{7,6},{8,9},{9,8},{10,11... | collective-permute-start | bytes 786440 | tf_op jit(solution)/shard_map/ppermute | solution.py:52
  18.8 0.8 dynamic-slice_convert_fusion
  19.5 1.7 %constant_dynamic-update-slice_fusion.1 = bf16[512,4096]{1,0:T(8,128)(2,1)S(1)} fusion(bf16[256,4096]{1,0:T(8,128)(2,1)} %param.4), kind=kLoop, calls=%fused_computation.31 | loop fusion | bytes 4194304
  21.5 0.8 copy-done.2
  22.2 1.3 fusion
  23.5 1.0 dynamic-slice_bitcast_fusion.2
  24.5 1.9 %collective-permute-start.4 = (bf16[32,4,8,256]{3,2,1,0:T(8,128)(2,1)}, bf16[32,4,8,256]{3,2,1,0:T(8,128)(2,1)}, u32[]{:S(2)}, u32[]{:S(2)}) collective-permute-start(bf16[32,4,8,256]{3,2,1,0:T(8,128)(2,1)} %get-tuple-element.23), channel_id=1, source_target_pairs={{0,520},{8,0},{512,8},{520,512},{1,521},{9,1},{513,9},{521,513},{2... | collective-permute-start | bytes 1572872 | tf_op jit(solution)/shard_map/ppermute | solution.py:13
  26.4 3.4 %collective-permute-start.3 = (bf16[32,4,8,256]{3,2,1,0:T(8,128)(2,1)S(1)}, bf16[32,4,8,256]{3,2,1,0:T(8,128)(2,1)}, u32[]{:S(2)}, u32[]{:S(2)}) collective-permute-start(bf16[32,4,8,256]{3,2,1,0:T(8,128)(2,1)S(1)} %get-tuple-element.24), channel_id=1, source_target_pairs={{0,8},{8,512},{512,520},{520,0},{1,9},{9,513},{513,521},{521,1},{2... | collective-permute-start | bytes 1572872 | tf_op jit(solution)/shard_map/ppermute | solution.py:13
  29.8 1.9 %collective-permute-start.2 = (bf16[32,4,8,256]{3,2,1,0:T(8,128)(2,1)S(1)}, bf16[32,4,8,256]{3,2,1,0:T(8,128)(2,1)}, u32[]{:S(2)}, u32[]{:S(2)}) collective-permute-start(bf16[32,4,8,256]{3,2,1,0:T(8,128)(2,1)S(1)} %get-tuple-element.22), channel_id=1, source_target_pairs={{0,512},{8,520},{512,0},{520,8},{1,513},{9,521},{513,1},{521,9},{2... | collective-permute-start | bytes 1572872 | tf_op jit(solution)/shard_map/ppermute | solution.py:13
  31.7 0.8 fusion.9
  33.2 18.8 %all-to-all-start = ((bf16[32,8,256]{2,1,0:T(8,128)(2,1)}), bf16[32,8,256]{2,1,0:T(8,128)(2,1)S(1)}, u32[]{:S(2)}, u32[]{:S(2)}) async-start(bf16[32,8,256]{2,1,0:T(8,128)(2,1)} %broadcast_in_dim.11), calls=%async_computation | async-start | bytes 262144 | tf_op jit(solution)/shard_map/all_to_all | solution.py:29
  52.1 1.8 %collective-permute-done.3 = bf16[32,4,8,256]{3,2,1,0:T(8,128)(2,1)} collective-permute-done((bf16[32,4,8,256]{3,2,1,0:T(8,128)(2,1)S(1)}, bf16[32,4,8,256]{3,2,1,0:T(8,128)(2,1)}, u32[]{:S(2)}, u32[]{:S(2)}) %collective-permute-start.3) | collective-permute-done | bytes 524320 | tf_op jit(solution)/shard_map/ppermute | solution.py:13
  53.9 1.7 %fusion.3 = bf16[32,4,8,256]{3,2,1,0:T(8,128)(2,1)S(1)} fusion(bf16[32,4,8,256]{3,2,1,0:T(8,128)(2,1)} %collective-permute-done.4, bf16[32,4,8,256]{3,2,1,0:T(8,128)(2,1)} %collective-permute-done.3, bf16[32,4,8,256]{3,2,1,0:T(8,128)(2,1)} %collective-permute-done.2, bf16[2,32,2,4,8,256]{5,4,3,2,1,0:T(8,128)(2,1)S(1)} %bitcast.43, s32[]{:T(128)S(6)} %select_n.150, ...), kind=kLoop, calls=%fused_computation.8 | loop fusion | flops 2097152 | bytes 2621448 | tf_op jit(solution)/shard_map/convert_element_type | solution.py:23
  55.7 3.0 %collective-permute-start.5 = (bf16[32,8,256]{2,1,0:T(8,128)(2,1)S(1)}, bf16[32,8,256]{2,1,0:T(8,128)(2,1)S(1)}, u32[]{:S(2)}, u32[]{:S(2)}) collective-permute-start(bf16[32,8,256]{2,1,0:T(8,128)(2,1)S(1)} %get-tuple-element.27), channel_id=1, source_target_pairs={{0,4},{2,6},{4,0},{6,2},{1,5},{3,7},{5,1},{7,3},{8,12},{10,14},{12... | collective-permute-start | bytes 393224 | tf_op jit(solution)/shard_map/ppermute | solution.py:13
  58.7 2.3 %collective-permute-start.6 = (bf16[32,8,256]{2,1,0:T(8,128)(2,1)S(1)}, bf16[32,8,256]{2,1,0:T(8,128)(2,1)S(1)}, u32[]{:S(2)}, u32[]{:S(2)}) collective-permute-start(bf16[32,8,256]{2,1,0:T(8,128)(2,1)S(1)} %get-tuple-element.26), channel_id=1, source_target_pairs={{0,2},{2,4},{4,6},{6,0},{1,3},{3,5},{5,7},{7,1},{8,10},{10,12},{12... | collective-permute-start | bytes 393224 | tf_op jit(solution)/shard_map/ppermute | solution.py:13
  61.0 7.0 %all-to-all-done = bf16[32,8,256]{2,1,0:T(8,128)(2,1)S(1)} async-done(((bf16[32,8,256]{2,1,0:T(8,128)(2,1)}), bf16[32,8,256]{2,1,0:T(8,128)(2,1)S(1)}, u32[]{:S(2)}, u32[]{:S(2)}) %all-to-all-start) | async-done | bytes 131104 | tf_op jit(solution)/shard_map/all_to_all | solution.py:29
  68.1 0.8 broadcast_in_dim.25
  68.9 4.2 %all-to-all-start.1 = ((bf16[4,256,256]{2,1,0:T(8,128)(2,1)}), bf16[4,256,256]{2,1,0:T(8,128)(2,1)S(1)}, u32[]{:S(2)}, u32[]{:S(2)}) async-start(bf16[4,256,256]{2,1,0:T(8,128)(2,1)} %broadcast_in_dim.25), calls=%async_computation.1 | async-start | bytes 1048576 | tf_op jit(solution)/shard_map/all_to_all | solution.py:86
  73.1 4.6 %collective-permute-start.7 = (bf16[32,8,256]{2,1,0:T(8,128)(2,1)S(1)}, bf16[32,8,256]{2,1,0:T(8,128)(2,1)S(1)}, u32[]{:S(2)}, u32[]{:S(2)}) collective-permute-start(bf16[32,8,256]{2,1,0:T(8,128)(2,1)S(1)} %get-tuple-element.25), channel_id=1, source_target_pairs={{0,6},{2,0},{4,2},{6,4},{1,7},{3,1},{5,3},{7,5},{8,14},{10,8},{12,... | collective-permute-start | bytes 393224 | tf_op jit(solution)/shard_map/ppermute | solution.py:13
  77.7 2.9 %collective-permute-done.7 = bf16[32,8,256]{2,1,0:T(8,128)(2,1)S(1)} collective-permute-done((bf16[32,8,256]{2,1,0:T(8,128)(2,1)S(1)}, bf16[32,8,256]{2,1,0:T(8,128)(2,1)S(1)}, u32[]{:S(2)}, u32[]{:S(2)}) %collective-permute-start.7) | collective-permute-done | bytes 131104 | tf_op jit(solution)/shard_map/ppermute | solution.py:13
  80.7 2.9 %collective-permute-start.10 = (bf16[4,256,256]{2,1,0:T(8,128)(2,1)S(1)}, bf16[4,256,256]{2,1,0:T(8,128)(2,1)S(1)}, u32[]{:S(2)}, u32[]{:S(2)}) collective-permute-start(bf16[4,256,256]{2,1,0:T(8,128)(2,1)S(1)} %all-to-all-done.1), channel_id=1, source_target_pairs={{0,520},{8,0},{512,8},{520,512},{1,521},{9,1},{513,9},{521,513},{2... | collective-permute-start | bytes 1572872 | tf_op jit(solution)/shard_map/ppermute | solution.py:13
  83.6 4.2 %collective-permute-start.9 = (bf16[4,256,256]{2,1,0:T(8,128)(2,1)S(1)}, bf16[4,256,256]{2,1,0:T(8,128)(2,1)S(1)}, u32[]{:S(2)}, u32[]{:S(2)}) collective-permute-start(bf16[4,256,256]{2,1,0:T(8,128)(2,1)S(1)} %all-to-all-done.1), channel_id=1, source_target_pairs={{0,512},{8,520},{512,0},{520,8},{1,513},{9,521},{513,1},{521,9},{2... | collective-permute-start | bytes 1572872 | tf_op jit(solution)/shard_map/ppermute | solution.py:13
  87.8 1.9 %collective-permute-start.8 = (bf16[4,256,256]{2,1,0:T(8,128)(2,1)S(1)}, bf16[4,256,256]{2,1,0:T(8,128)(2,1)S(1)}, u32[]{:S(2)}, u32[]{:S(2)}) collective-permute-start(bf16[4,256,256]{2,1,0:T(8,128)(2,1)S(1)} %all-to-all-done.1), channel_id=1, source_target_pairs={{0,8},{8,512},{512,520},{520,0},{1,9},{9,513},{513,521},{521,1},{2... | collective-permute-start | bytes 1572872 | tf_op jit(solution)/shard_map/ppermute | solution.py:13
  90.5 24.7 %all-to-all-start.2 = ((bf16[32,8,256]{2,1,0:T(8,128)(2,1)}), bf16[32,8,256]{2,1,0:T(8,128)(2,1)S(1)}, u32[]{:S(2)}, u32[]{:S(2)}) async-start(bf16[32,8,256]{2,1,0:T(8,128)(2,1)} %pad_maximum_fusion.3), calls=%async_computation.2 | async-start | bytes 262144 | tf_op jit(solution)/shard_map/all_to_all | solution.py:29
  116.3 1.9 %copy-done.1 = bf16[512,4096]{1,0:T(8,128)(2,1)S(1)} copy-done((bf16[512,4096]{1,0:T(8,128)(2,1)S(1)}, bf16[512,4096]{1,0:T(8,128)(2,1)}, u32[]{:S(2)}) %copy-start.1) | copy-done | bytes 4194328
  118.2 1.2 convolution_convert_fusion
  119.5 5.9 %collective-permute-start.11 = (bf16[256,256]{1,0:T(8,128)(2,1)S(1)}, bf16[256,256]{1,0:T(8,128)(2,1)S(1)}, u32[]{:S(2)}, u32[]{:S(2)}) collective-permute-start(bf16[256,256]{1,0:T(8,128)(2,1)S(1)} %get-tuple-element.31), channel_id=1, source_target_pairs={{0,1},{1,0},{2,3},{3,2},{4,5},{5,4},{6,7},{7,6},{8,9},{9,8},{10,11... | collective-permute-start | bytes 393224 | tf_op jit(solution)/shard_map/ppermute | solution.py:98
  125.4 1.0 collective-permute-done.11
  127.1 5.6 %all-to-all-start.3 = ((f32[8,8,256]{2,1,0:T(8,128)}), f32[8,8,256]{2,1,0:T(8,128)S(1)}, u32[]{:S(2)}, u32[]{:S(2)}) async-start(f32[8,8,256]{2,1,0:T(8,128)} %broadcast_in_dim.26), calls=%async_computation.3 | async-start | bytes 131072 | tf_op jit(solution)/shard_map/all_to_all | solution.py:103
  132.7 0.7 pad_maximum_fusion.2
  133.5 4.1 %all-to-all-done.3 = f32[8,8,256]{2,1,0:T(8,128)S(1)} async-done(((f32[8,8,256]{2,1,0:T(8,128)}), f32[8,8,256]{2,1,0:T(8,128)S(1)}, u32[]{:S(2)}, u32[]{:S(2)}) %all-to-all-start.3) | async-done | bytes 65568 | tf_op jit(solution)/shard_map/all_to_all | solution.py:103
  (33 shorter events, 4.1 us)
Async XLA Ops:
  0.6 20.7 %collective-permute-start = (bf16[256,4096]{1,0:T(8,128)(2,1)}, bf16[256,4096]{1,0:T(8,128)(2,1)S(1)}, u32[]{:S(2)}, u32[]{:S(2)}) collective-permute-start(bf16[256,4096]{1,0:T(8,128)(2,1)} %param.4), channel_id=1, source_target_pairs={{0,1},{1,0},{2,3},{3,2},{4,5},{5,4},{6,7},{7,6},{8,9},{9,8},{10,11... | collective-permute-start | bytes 6291464 | tf_op jit(solution)/shard_map/ppermute | solution.py:51
  16.7 4.7 %collective-permute-start.1 = (bf16[256,512]{1,0:T(8,128)(2,1)}, bf16[256,512]{1,0:T(8,128)(2,1)S(1)}, u32[]{:S(2)}, u32[]{:S(2)}) collective-permute-start(bf16[256,512]{1,0:T(8,128)(2,1)} %param.7), channel_id=1, source_target_pairs={{0,1},{1,0},{2,3},{3,2},{4,5},{5,4},{6,7},{7,6},{8,9},{9,8},{10,11... | collective-permute-start | bytes 786440 | tf_op jit(solution)/shard_map/ppermute | solution.py:52
  21.3 1.0 copy-start.2
  21.4 2.1 %copy-start = (bf16[512,4096]{1,0:T(8,128)(2,1)}, bf16[512,4096]{1,0:T(8,128)(2,1)S(1)}, u32[]{:S(2)}) copy-start(bf16[512,4096]{1,0:T(8,128)(2,1)S(1)} %constant_dynamic-update-slice_fusion) | copy-start | bytes 12582916
  24.5 27.5 %collective-permute-start.4 = (bf16[32,4,8,256]{3,2,1,0:T(8,128)(2,1)}, bf16[32,4,8,256]{3,2,1,0:T(8,128)(2,1)}, u32[]{:S(2)}, u32[]{:S(2)}) collective-permute-start(bf16[32,4,8,256]{3,2,1,0:T(8,128)(2,1)} %get-tuple-element.23), channel_id=1, source_target_pairs={{0,520},{8,0},{512,8},{520,512},{1,521},{9,1},{513,9},{521,513},{2... | collective-permute-start | bytes 1572872 | tf_op jit(solution)/shard_map/ppermute | solution.py:13
  26.4 27.4 %collective-permute-start.3 = (bf16[32,4,8,256]{3,2,1,0:T(8,128)(2,1)S(1)}, bf16[32,4,8,256]{3,2,1,0:T(8,128)(2,1)}, u32[]{:S(2)}, u32[]{:S(2)}) collective-permute-start(bf16[32,4,8,256]{3,2,1,0:T(8,128)(2,1)S(1)} %get-tuple-element.24), channel_id=1, source_target_pairs={{0,8},{8,512},{512,520},{520,0},{1,9},{9,513},{513,521},{521,1},{2... | collective-permute-start | bytes 1572872 | tf_op jit(solution)/shard_map/ppermute | solution.py:13
  29.8 24.1 %collective-permute-start.2 = (bf16[32,4,8,256]{3,2,1,0:T(8,128)(2,1)S(1)}, bf16[32,4,8,256]{3,2,1,0:T(8,128)(2,1)}, u32[]{:S(2)}, u32[]{:S(2)}) collective-permute-start(bf16[32,4,8,256]{3,2,1,0:T(8,128)(2,1)S(1)} %get-tuple-element.22), channel_id=1, source_target_pairs={{0,512},{8,520},{512,0},{520,8},{1,513},{9,521},{513,1},{521,9},{2... | collective-permute-start | bytes 1572872 | tf_op jit(solution)/shard_map/ppermute | solution.py:13
  33.2 34.8 %all-to-all-start = ((bf16[32,8,256]{2,1,0:T(8,128)(2,1)}), bf16[32,8,256]{2,1,0:T(8,128)(2,1)S(1)}, u32[]{:S(2)}, u32[]{:S(2)}) async-start(bf16[32,8,256]{2,1,0:T(8,128)(2,1)} %broadcast_in_dim.11), calls=%async_computation | async-start | bytes 262144 | tf_op jit(solution)/shard_map/all_to_all | solution.py:29
  55.7 12.3 %collective-permute-start.5 = (bf16[32,8,256]{2,1,0:T(8,128)(2,1)S(1)}, bf16[32,8,256]{2,1,0:T(8,128)(2,1)S(1)}, u32[]{:S(2)}, u32[]{:S(2)}) collective-permute-start(bf16[32,8,256]{2,1,0:T(8,128)(2,1)S(1)} %get-tuple-element.27), channel_id=1, source_target_pairs={{0,4},{2,6},{4,0},{6,2},{1,5},{3,7},{5,1},{7,3},{8,12},{10,14},{12... | collective-permute-start | bytes 393224 | tf_op jit(solution)/shard_map/ppermute | solution.py:13
  58.7 9.3 %collective-permute-start.6 = (bf16[32,8,256]{2,1,0:T(8,128)(2,1)S(1)}, bf16[32,8,256]{2,1,0:T(8,128)(2,1)S(1)}, u32[]{:S(2)}, u32[]{:S(2)}) collective-permute-start(bf16[32,8,256]{2,1,0:T(8,128)(2,1)S(1)} %get-tuple-element.26), channel_id=1, source_target_pairs={{0,2},{2,4},{4,6},{6,0},{1,3},{3,5},{5,7},{7,1},{8,10},{10,12},{12... | collective-permute-start | bytes 393224 | tf_op jit(solution)/shard_map/ppermute | solution.py:13
  68.9 11.8 %all-to-all-start.1 = ((bf16[4,256,256]{2,1,0:T(8,128)(2,1)}), bf16[4,256,256]{2,1,0:T(8,128)(2,1)S(1)}, u32[]{:S(2)}, u32[]{:S(2)}) async-start(bf16[4,256,256]{2,1,0:T(8,128)(2,1)} %broadcast_in_dim.25), calls=%async_computation.1 | async-start | bytes 1048576 | tf_op jit(solution)/shard_map/all_to_all | solution.py:86
  73.1 7.5 %collective-permute-start.7 = (bf16[32,8,256]{2,1,0:T(8,128)(2,1)S(1)}, bf16[32,8,256]{2,1,0:T(8,128)(2,1)S(1)}, u32[]{:S(2)}, u32[]{:S(2)}) collective-permute-start(bf16[32,8,256]{2,1,0:T(8,128)(2,1)S(1)} %get-tuple-element.25), channel_id=1, source_target_pairs={{0,6},{2,0},{4,2},{6,4},{1,7},{3,1},{5,3},{7,5},{8,14},{10,8},{12,... | collective-permute-start | bytes 393224 | tf_op jit(solution)/shard_map/ppermute | solution.py:13
  80.7 34.6 %collective-permute-start.10 = (bf16[4,256,256]{2,1,0:T(8,128)(2,1)S(1)}, bf16[4,256,256]{2,1,0:T(8,128)(2,1)S(1)}, u32[]{:S(2)}, u32[]{:S(2)}) collective-permute-start(bf16[4,256,256]{2,1,0:T(8,128)(2,1)S(1)} %all-to-all-done.1), channel_id=1, source_target_pairs={{0,520},{8,0},{512,8},{520,512},{1,521},{9,1},{513,9},{521,513},{2... | collective-permute-start | bytes 1572872 | tf_op jit(solution)/shard_map/ppermute | solution.py:13
  83.6 31.7 %collective-permute-start.9 = (bf16[4,256,256]{2,1,0:T(8,128)(2,1)S(1)}, bf16[4,256,256]{2,1,0:T(8,128)(2,1)S(1)}, u32[]{:S(2)}, u32[]{:S(2)}) collective-permute-start(bf16[4,256,256]{2,1,0:T(8,128)(2,1)S(1)} %all-to-all-done.1), channel_id=1, source_target_pairs={{0,512},{8,520},{512,0},{520,8},{1,513},{9,521},{513,1},{521,9},{2... | collective-permute-start | bytes 1572872 | tf_op jit(solution)/shard_map/ppermute | solution.py:13
  87.8 27.4 %collective-permute-start.8 = (bf16[4,256,256]{2,1,0:T(8,128)(2,1)S(1)}, bf16[4,256,256]{2,1,0:T(8,128)(2,1)S(1)}, u32[]{:S(2)}, u32[]{:S(2)}) collective-permute-start(bf16[4,256,256]{2,1,0:T(8,128)(2,1)S(1)} %all-to-all-done.1), channel_id=1, source_target_pairs={{0,8},{8,512},{512,520},{520,0},{1,9},{9,513},{513,521},{521,1},{2... | collective-permute-start | bytes 1572872 | tf_op jit(solution)/shard_map/ppermute | solution.py:13
  90.5 35.9 %all-to-all-start.2 = ((bf16[32,8,256]{2,1,0:T(8,128)(2,1)}), bf16[32,8,256]{2,1,0:T(8,128)(2,1)S(1)}, u32[]{:S(2)}, u32[]{:S(2)}) async-start(bf16[32,8,256]{2,1,0:T(8,128)(2,1)} %pad_maximum_fusion.3), calls=%async_computation.2 | async-start | bytes 262144 | tf_op jit(solution)/shard_map/all_to_all | solution.py:29
  116.0 2.2 %copy-start.1 = (bf16[512,4096]{1,0:T(8,128)(2,1)S(1)}, bf16[512,4096]{1,0:T(8,128)(2,1)}, u32[]{:S(2)}) copy-start(bf16[512,4096]{1,0:T(8,128)(2,1)} %copy-done) | copy-start | bytes 12582916
  119.5 6.8 %collective-permute-start.11 = (bf16[256,256]{1,0:T(8,128)(2,1)S(1)}, bf16[256,256]{1,0:T(8,128)(2,1)S(1)}, u32[]{:S(2)}, u32[]{:S(2)}) collective-permute-start(bf16[256,256]{1,0:T(8,128)(2,1)S(1)} %get-tuple-element.31), channel_id=1, source_target_pairs={{0,1},{1,0},{2,3},{3,2},{4,5},{5,4},{6,7},{7,6},{8,9},{9,8},{10,11... | collective-permute-start | bytes 393224 | tf_op jit(solution)/shard_map/ppermute | solution.py:98
  127.1 10.5 %all-to-all-start.3 = ((f32[8,8,256]{2,1,0:T(8,128)}), f32[8,8,256]{2,1,0:T(8,128)S(1)}, u32[]{:S(2)}, u32[]{:S(2)}) async-start(f32[8,8,256]{2,1,0:T(8,128)} %broadcast_in_dim.26), calls=%async_computation.3 | async-start | bytes 131072 | tf_op jit(solution)/shard_map/all_to_all | solution.py:103

commit v11 on v9

--- a/solution.py
+++ b/solution.py
@@ -65,7 +65,7 @@
     grad = lax.dot_general(acts, cots, dims, preferred_element_type=f32)
     grad = (grad * factor).astype(bf16)
     grad = grad.reshape(2, n_z, 2, 4, rows, half)
-    first = 3 * n_z // 4
+    first = 11 * n_z // 16
     col = over_z(spread, first)
 
     def to_x(k):

time: 138 us -> 137 us (level)
  waiting for transfers between devices: 14.8 us -> 12 us
  starting transfers between devices: 95.7 us -> 97.3 us
    all_to_all x2, waiting for transfers between devices: 2.59 us -> 0.01 us  [over_z(): lax.all_to_all(value, 'z', split_axis=0, concat_axis=0, axis_index_groups...]
    ppermute x1, starting transfers between devices: 5.53 us -> 7.57 us  [body(): got = lax.ppermute(proj[tok:], 'c', SWAP)]
  transfers between devices with their start and end apart: 15 -> 15, of which waited for: 9 -> 7; matrix products, arithmetic and copies ran while one was open for 6% -> 7% of each run, Pallas kernels for 0% -> 0%
where the time goes in v11:
time: 137 us; the launch traced here: 135 us
  starting transfers between devices  97.3 us (71%)
  waiting for transfers between devices  12 us (9%)
  blocking collectives  10 us (7%)
  local copies, waits for them, and re-layouts  7.69 us (6%)
  other arithmetic  4.62 us (3%)
  matrix products  2.55 us (2%)
    all_to_all x2, starting transfers between devices, over_z(): lax.all_to_all(value, 'z', split_axis=0, concat_axis=0, axis_index_groups...  43.3 us
    ppermute x9, starting transfers between devices, around(): return lax.ppermute(value, axes, [(i, (i + shift) % 4) for i in range(4)])  24.6 us
    ppermute x1, starting transfers between devices, body(): other_act = lax.ppermute(activations, 'c', SWAP)  16.1 us
    all_to_all x1, blocking collectives, body(): slab = lax.all_to_all(slab, 'y', split_axis=0, concat_axis=0, tiled=True)  10 us
    ppermute x1, starting transfers between devices, body(): got = lax.ppermute(proj[tok:], 'c', SWAP)  7.57 us
    ppermute x9, waiting for transfers between devices, around(): return lax.ppermute(value, axes, [(i, (i + shift) % 4) for i in range(4)])  6.53 us
    unnamed x10, local copies, waits for them, and re-layouts  4.67 us
    all_to_all x1, waiting for transfers between devices, body(): lax.all_to_all(pieces, ('y', 'c'), split_axis=0, concat_axis=0, tiled=True)  4.12 us
  transfers between devices with their start and end apart: 15, of which 7 were waited for; matrix products, arithmetic and copies ran while one was open for 7% of the time, Pallas kernels for 0%

profile of v11, /device:TPU:1, one launch (start us, length us, event | category | flops | bytes accessed | tf_op | source)
XLA Modules:
  0.0 135.4 jit_solution(13321269684857635353)
XLA Ops:
  0.6 16.1 %collective-permute-start = (bf16[256,4096]{1,0:T(8,128)(2,1)}, bf16[256,4096]{1,0:T(8,128)(2,1)S(1)}, u32[]{:S(2)}, u32[]{:S(2)}) collective-permute-start(bf16[256,4096]{1,0:T(8,128)(2,1)} %param.4), channel_id=1, source_target_pairs={{0,1},{1,0},{2,3},{3,2},{4,5},{5,4},{6,7},{7,6},{8,9},{9,8},{10,11... | collective-permute-start | bytes 6291464 | tf_op jit(solution)/shard_map/ppermute | solution.py:51
  16.7 1.9 %collective-permute-start.1 = (bf16[256,512]{1,0:T(8,128)(2,1)}, bf16[256,512]{1,0:T(8,128)(2,1)S(1)}, u32[]{:S(2)}, u32[]{:S(2)}) collective-permute-start(bf16[256,512]{1,0:T(8,128)(2,1)} %param.7), channel_id=1, source_target_pairs={{0,1},{1,0},{2,3},{3,2},{4,5},{5,4},{6,7},{7,6},{8,9},{9,8},{10,11... | collective-permute-start | bytes 786440 | tf_op jit(solution)/shard_map/ppermute | solution.py:52
  18.8 1.7 %constant_dynamic-update-slice_fusion.1 = bf16[512,4096]{1,0:T(8,128)(2,1)S(1)} fusion(bf16[256,4096]{1,0:T(8,128)(2,1)} %param.4), kind=kLoop, calls=%fused_computation.31 | loop fusion | bytes 4194304
  21.5 1.3 fusion
  22.8 1.0 dynamic-slice_bitcast_fusion.2
  23.8 1.9 %collective-permute-start.4 = (bf16[32,4,8,256]{3,2,1,0:T(8,128)(2,1)}, bf16[32,4,8,256]{3,2,1,0:T(8,128)(2,1)}, u32[]{:S(2)}, u32[]{:S(2)}) collective-permute-start(bf16[32,4,8,256]{3,2,1,0:T(8,128)(2,1)} %get-tuple-element.21), channel_id=1, source_target_pairs={{0,520},{8,0},{512,8},{520,512},{1,521},{9,1},{513,9},{521,513},{2... | collective-permute-start | bytes 1572872 | tf_op jit(solution)/shard_map/ppermute | solution.py:13
  25.7 3.4 %collective-permute-start.3 = (bf16[32,4,8,256]{3,2,1,0:T(8,128)(2,1)S(1)}, bf16[32,4,8,256]{3,2,1,0:T(8,128)(2,1)}, u32[]{:S(2)}, u32[]{:S(2)}) collective-permute-start(bf16[32,4,8,256]{3,2,1,0:T(8,128)(2,1)S(1)} %get-tuple-element.22), channel_id=1, source_target_pairs={{0,8},{8,512},{512,520},{520,0},{1,9},{9,513},{513,521},{521,1},{2... | collective-permute-start | bytes 1572872 | tf_op jit(solution)/shard_map/ppermute | solution.py:13
  29.0 1.9 %collective-permute-start.2 = (bf16[32,4,8,256]{3,2,1,0:T(8,128)(2,1)S(1)}, bf16[32,4,8,256]{3,2,1,0:T(8,128)(2,1)}, u32[]{:S(2)}, u32[]{:S(2)}) collective-permute-start(bf16[32,4,8,256]{3,2,1,0:T(8,128)(2,1)S(1)} %get-tuple-element.20), channel_id=1, source_target_pairs={{0,512},{8,520},{512,0},{520,8},{1,513},{9,521},{513,1},{521,9},{2... | collective-permute-start | bytes 1572872 | tf_op jit(solution)/shard_map/ppermute | solution.py:13
  31.1 0.8 fusion.9
  31.8 0.7 broadcast_in_dim.11
  32.5 18.8 %all-to-all-start = ((bf16[32,8,256]{2,1,0:T(8,128)(2,1)}), bf16[32,8,256]{2,1,0:T(8,128)(2,1)S(1)}, u32[]{:S(2)}, u32[]{:S(2)}) async-start(bf16[32,8,256]{2,1,0:T(8,128)(2,1)} %broadcast_in_dim.11), calls=%async_computation | async-start | bytes 262144 | tf_op jit(solution)/shard_map/all_to_all | solution.py:29
  51.4 1.7 %collective-permute-done.3 = bf16[32,4,8,256]{3,2,1,0:T(8,128)(2,1)} collective-permute-done((bf16[32,4,8,256]{3,2,1,0:T(8,128)(2,1)S(1)}, bf16[32,4,8,256]{3,2,1,0:T(8,128)(2,1)}, u32[]{:S(2)}, u32[]{:S(2)}) %collective-permute-start.3) | collective-permute-done | bytes 524320 | tf_op jit(solution)/shard_map/ppermute | solution.py:13
  53.1 1.7 %fusion.3 = bf16[32,4,8,256]{3,2,1,0:T(8,128)(2,1)S(1)} fusion(bf16[32,4,8,256]{3,2,1,0:T(8,128)(2,1)} %collective-permute-done.4, bf16[32,4,8,256]{3,2,1,0:T(8,128)(2,1)} %collective-permute-done.3, bf16[32,4,8,256]{3,2,1,0:T(8,128)(2,1)} %collective-permute-done.2, bf16[2,32,2,4,8,256]{5,4,3,2,1,0:T(8,128)(2,1)S(1)} %bitcast.43, s32[]{:T(128)S(6)} %select_n.150, ...), kind=kLoop, calls=%fused_computation.8 | loop fusion | flops 2097152 | bytes 2621448 | tf_op jit(solution)/shard_map/convert_element_type | solution.py:23
  54.9 2.9 %collective-permute-start.7 = (bf16[32,8,256]{2,1,0:T(8,128)(2,1)S(1)}, bf16[32,8,256]{2,1,0:T(8,128)(2,1)S(1)}, u32[]{:S(2)}, u32[]{:S(2)}) collective-permute-start(bf16[32,8,256]{2,1,0:T(8,128)(2,1)S(1)} %get-tuple-element.24), channel_id=1, source_target_pairs={{0,6},{2,0},{4,2},{6,4},{1,7},{3,1},{5,3},{7,5},{8,14},{10,8},{12,... | collective-permute-start | bytes 393224 | tf_op jit(solution)/shard_map/ppermute | solution.py:13
  57.9 2.3 %collective-permute-start.6 = (bf16[32,8,256]{2,1,0:T(8,128)(2,1)S(1)}, bf16[32,8,256]{2,1,0:T(8,128)(2,1)S(1)}, u32[]{:S(2)}, u32[]{:S(2)}) collective-permute-start(bf16[32,8,256]{2,1,0:T(8,128)(2,1)S(1)} %get-tuple-element.25), channel_id=1, source_target_pairs={{0,2},{2,4},{4,6},{6,0},{1,3},{3,5},{5,7},{7,1},{8,10},{10,12},{12... | collective-permute-start | bytes 393224 | tf_op jit(solution)/shard_map/ppermute | solution.py:13
  60.2 3.1 %collective-permute-start.5 = (bf16[32,8,256]{2,1,0:T(8,128)(2,1)S(1)}, bf16[32,8,256]{2,1,0:T(8,128)(2,1)S(1)}, u32[]{:S(2)}, u32[]{:S(2)}) collective-permute-start(bf16[32,8,256]{2,1,0:T(8,128)(2,1)S(1)} %get-tuple-element.23), channel_id=1, source_target_pairs={{0,4},{2,6},{4,0},{6,2},{1,5},{3,7},{5,1},{7,3},{8,12},{10,14},{12... | collective-permute-start | bytes 393224 | tf_op jit(solution)/shard_map/ppermute | solution.py:13
  63.3 1.7 %collective-permute-done.6 = bf16[32,8,256]{2,1,0:T(8,128)(2,1)S(1)} collective-permute-done((bf16[32,8,256]{2,1,0:T(8,128)(2,1)S(1)}, bf16[32,8,256]{2,1,0:T(8,128)(2,1)S(1)}, u32[]{:S(2)}, u32[]{:S(2)}) %collective-permute-start.6) | collective-permute-done | bytes 131104 | tf_op jit(solution)/shard_map/ppermute | solution.py:13
  65.1 3.1 %collective-permute-done.5 = bf16[32,8,256]{2,1,0:T(8,128)(2,1)S(1)} collective-permute-done((bf16[32,8,256]{2,1,0:T(8,128)(2,1)S(1)}, bf16[32,8,256]{2,1,0:T(8,128)(2,1)S(1)}, u32[]{:S(2)}, u32[]{:S(2)}) %collective-permute-start.5) | collective-permute-done | bytes 131104 | tf_op jit(solution)/shard_map/ppermute | solution.py:13
  68.3 10.0 %all_to_all.20 = bf16[4,256,256]{2,1,0:T(8,128)(2,1)S(1)} all-to-all(bf16[4,256,256]{2,1,0:T(8,128)(2,1)S(1)} %broadcast_in_dim.25), channel_id=1, replica_groups=mesh['xh'=2,'z'=32,'xl'=2,'y'=4,'c'=2] {'y'}, dimensions={0} | all-to-all | bytes 1048576 | tf_op jit(solution)/shard_map/all_to_all | solution.py:81
  78.3 2.7 %collective-permute-start.10 = (bf16[4,256,256]{2,1,0:T(8,128)(2,1)S(1)}, bf16[4,256,256]{2,1,0:T(8,128)(2,1)S(1)}, u32[]{:S(2)}, u32[]{:S(2)}) collective-permute-start(bf16[4,256,256]{2,1,0:T(8,128)(2,1)S(1)} %all_to_all.20), channel_id=1, source_target_pairs={{0,520},{8,0},{512,8},{520,512},{1,521},{9,1},{513,9},{521,513},{2... | collective-permute-start | bytes 1572872 | tf_op jit(solution)/shard_map/ppermute | solution.py:13
  81.0 4.5 %collective-permute-start.9 = (bf16[4,256,256]{2,1,0:T(8,128)(2,1)S(1)}, bf16[4,256,256]{2,1,0:T(8,128)(2,1)S(1)}, u32[]{:S(2)}, u32[]{:S(2)}) collective-permute-start(bf16[4,256,256]{2,1,0:T(8,128)(2,1)S(1)} %all_to_all.20), channel_id=1, source_target_pairs={{0,512},{8,520},{512,0},{520,8},{1,513},{9,521},{513,1},{521,9},{2... | collective-permute-start | bytes 1572872 | tf_op jit(solution)/shard_map/ppermute | solution.py:13
  85.5 1.9 %collective-permute-start.8 = (bf16[4,256,256]{2,1,0:T(8,128)(2,1)S(1)}, bf16[4,256,256]{2,1,0:T(8,128)(2,1)S(1)}, u32[]{:S(2)}, u32[]{:S(2)}) collective-permute-start(bf16[4,256,256]{2,1,0:T(8,128)(2,1)S(1)} %all_to_all.20), channel_id=1, source_target_pairs={{0,8},{8,512},{512,520},{520,0},{1,9},{9,513},{513,521},{521,1},{2... | collective-permute-start | bytes 1572872 | tf_op jit(solution)/shard_map/ppermute | solution.py:13
  87.5 0.7 pad_maximum_fusion.3
  88.2 24.5 %all-to-all-start.2 = ((bf16[32,8,256]{2,1,0:T(8,128)(2,1)}), bf16[32,8,256]{2,1,0:T(8,128)(2,1)S(1)}, u32[]{:S(2)}, u32[]{:S(2)}) async-start(bf16[32,8,256]{2,1,0:T(8,128)(2,1)} %pad_maximum_fusion.3), calls=%async_computation.2 | async-start | bytes 262144 | tf_op jit(solution)/shard_map/all_to_all | solution.py:29
  113.7 1.9 %copy-done.1 = bf16[512,4096]{1,0:T(8,128)(2,1)S(1)} copy-done((bf16[512,4096]{1,0:T(8,128)(2,1)S(1)}, bf16[512,4096]{1,0:T(8,128)(2,1)}, u32[]{:S(2)}) %copy-start.1) | copy-done | bytes 4194328
  115.6 1.2 convolution_convert_fusion
  116.9 7.6 %collective-permute-start.11 = (bf16[256,256]{1,0:T(8,128)(2,1)S(1)}, bf16[256,256]{1,0:T(8,128)(2,1)S(1)}, u32[]{:S(2)}, u32[]{:S(2)}) collective-permute-start(bf16[256,256]{1,0:T(8,128)(2,1)S(1)} %get-tuple-element.29), channel_id=1, source_target_pairs={{0,1},{1,0},{2,3},{3,2},{4,5},{5,4},{6,7},{7,6},{8,9},{9,8},{10,11... | collective-permute-start | bytes 393224 | tf_op jit(solution)/shard_map/ppermute | solution.py:93
  124.5 1.0 collective-permute-done.11
  125.5 0.6 broadcast_in_dim.26
  126.1 3.8 %all-to-all-start.3 = ((f32[8,8,256]{2,1,0:T(8,128)}), f32[8,8,256]{2,1,0:T(8,128)S(1)}, u32[]{:S(2)}, u32[]{:S(2)}) async-start(f32[8,8,256]{2,1,0:T(8,128)} %broadcast_in_dim.26), calls=%async_computation.3 | async-start | bytes 131072 | tf_op jit(solution)/shard_map/all_to_all | solution.py:98
  130.0 0.7 pad_maximum_fusion.2
  130.7 4.1 %all-to-all-done.3 = f32[8,8,256]{2,1,0:T(8,128)S(1)} async-done(((f32[8,8,256]{2,1,0:T(8,128)}), f32[8,8,256]{2,1,0:T(8,128)S(1)}, u32[]{:S(2)}, u32[]{:S(2)}) %all-to-all-start.3) | async-done | bytes 65568 | tf_op jit(solution)/shard_map/all_to_all | solution.py:98
  (34 shorter events, 3.0 us)
Async XLA Ops:
  0.6 20.0 %collective-permute-start = (bf16[256,4096]{1,0:T(8,128)(2,1)}, bf16[256,4096]{1,0:T(8,128)(2,1)S(1)}, u32[]{:S(2)}, u32[]{:S(2)}) collective-permute-start(bf16[256,4096]{1,0:T(8,128)(2,1)} %param.4), channel_id=1, source_target_pairs={{0,1},{1,0},{2,3},{3,2},{4,5},{5,4},{6,7},{7,6},{8,9},{9,8},{10,11... | collective-permute-start | bytes 6291464 | tf_op jit(solution)/shard_map/ppermute | solution.py:51
  16.7 4.3 %collective-permute-start.1 = (bf16[256,512]{1,0:T(8,128)(2,1)}, bf16[256,512]{1,0:T(8,128)(2,1)S(1)}, u32[]{:S(2)}, u32[]{:S(2)}) collective-permute-start(bf16[256,512]{1,0:T(8,128)(2,1)} %param.7), channel_id=1, source_target_pairs={{0,1},{1,0},{2,3},{3,2},{4,5},{5,4},{6,7},{7,6},{8,9},{9,8},{10,11... | collective-permute-start | bytes 786440 | tf_op jit(solution)/shard_map/ppermute | solution.py:52
  20.5 1.0 copy-start.3
  20.8 2.0 %copy-start = (bf16[512,4096]{1,0:T(8,128)(2,1)}, bf16[512,4096]{1,0:T(8,128)(2,1)S(1)}, u32[]{:S(2)}) copy-start(bf16[512,4096]{1,0:T(8,128)(2,1)S(1)} %constant_dynamic-update-slice_fusion) | copy-start | bytes 12582916
  22.8 8.2 %copy-start.2 = (bf16[32,4]{0,1:T(4,128)(2,1)S(1)}, bf16[32,4]{0,1:T(4,128)(2,1)}, u32[]{:S(2)}) copy-start(bf16[32,4]{0,1:T(4,128)(2,1)} %param.6) | copy-start | bytes 772
  23.8 27.6 %collective-permute-start.4 = (bf16[32,4,8,256]{3,2,1,0:T(8,128)(2,1)}, bf16[32,4,8,256]{3,2,1,0:T(8,128)(2,1)}, u32[]{:S(2)}, u32[]{:S(2)}) collective-permute-start(bf16[32,4,8,256]{3,2,1,0:T(8,128)(2,1)} %get-tuple-element.21), channel_id=1, source_target_pairs={{0,520},{8,0},{512,8},{520,512},{1,521},{9,1},{513,9},{521,513},{2... | collective-permute-start | bytes 1572872 | tf_op jit(solution)/shard_map/ppermute | solution.py:13
  25.7 27.4 %collective-permute-start.3 = (bf16[32,4,8,256]{3,2,1,0:T(8,128)(2,1)S(1)}, bf16[32,4,8,256]{3,2,1,0:T(8,128)(2,1)}, u32[]{:S(2)}, u32[]{:S(2)}) collective-permute-start(bf16[32,4,8,256]{3,2,1,0:T(8,128)(2,1)S(1)} %get-tuple-element.22), channel_id=1, source_target_pairs={{0,8},{8,512},{512,520},{520,0},{1,9},{9,513},{513,521},{521,1},{2... | collective-permute-start | bytes 1572872 | tf_op jit(solution)/shard_map/ppermute | solution.py:13
  29.0 24.1 %collective-permute-start.2 = (bf16[32,4,8,256]{3,2,1,0:T(8,128)(2,1)S(1)}, bf16[32,4,8,256]{3,2,1,0:T(8,128)(2,1)}, u32[]{:S(2)}, u32[]{:S(2)}) collective-permute-start(bf16[32,4,8,256]{3,2,1,0:T(8,128)(2,1)S(1)} %get-tuple-element.20), channel_id=1, source_target_pairs={{0,512},{8,520},{512,0},{520,8},{1,513},{9,521},{513,1},{521,9},{2... | collective-permute-start | bytes 1572872 | tf_op jit(solution)/shard_map/ppermute | solution.py:13
  32.5 35.7 %all-to-all-start = ((bf16[32,8,256]{2,1,0:T(8,128)(2,1)}), bf16[32,8,256]{2,1,0:T(8,128)(2,1)S(1)}, u32[]{:S(2)}, u32[]{:S(2)}) async-start(bf16[32,8,256]{2,1,0:T(8,128)(2,1)} %broadcast_in_dim.11), calls=%async_computation | async-start | bytes 262144 | tf_op jit(solution)/shard_map/all_to_all | solution.py:29
  54.9 8.4 %collective-permute-start.7 = (bf16[32,8,256]{2,1,0:T(8,128)(2,1)S(1)}, bf16[32,8,256]{2,1,0:T(8,128)(2,1)S(1)}, u32[]{:S(2)}, u32[]{:S(2)}) collective-permute-start(bf16[32,8,256]{2,1,0:T(8,128)(2,1)S(1)} %get-tuple-element.24), channel_id=1, source_target_pairs={{0,6},{2,0},{4,2},{6,4},{1,7},{3,1},{5,3},{7,5},{8,14},{10,8},{12,... | collective-permute-start | bytes 393224 | tf_op jit(solution)/shard_map/ppermute | solution.py:13
  57.9 7.2 %collective-permute-start.6 = (bf16[32,8,256]{2,1,0:T(8,128)(2,1)S(1)}, bf16[32,8,256]{2,1,0:T(8,128)(2,1)S(1)}, u32[]{:S(2)}, u32[]{:S(2)}) collective-permute-start(bf16[32,8,256]{2,1,0:T(8,128)(2,1)S(1)} %get-tuple-element.25), channel_id=1, source_target_pairs={{0,2},{2,4},{4,6},{6,0},{1,3},{3,5},{5,7},{7,1},{8,10},{10,12},{12... | collective-permute-start | bytes 393224 | tf_op jit(solution)/shard_map/ppermute | solution.py:13
  60.2 7.9 %collective-permute-start.5 = (bf16[32,8,256]{2,1,0:T(8,128)(2,1)S(1)}, bf16[32,8,256]{2,1,0:T(8,128)(2,1)S(1)}, u32[]{:S(2)}, u32[]{:S(2)}) collective-permute-start(bf16[32,8,256]{2,1,0:T(8,128)(2,1)S(1)} %get-tuple-element.23), channel_id=1, source_target_pairs={{0,4},{2,6},{4,0},{6,2},{1,5},{3,7},{5,1},{7,3},{8,12},{10,14},{12... | collective-permute-start | bytes 393224 | tf_op jit(solution)/shard_map/ppermute | solution.py:13
  78.3 34.3 %collective-permute-start.10 = (bf16[4,256,256]{2,1,0:T(8,128)(2,1)S(1)}, bf16[4,256,256]{2,1,0:T(8,128)(2,1)S(1)}, u32[]{:S(2)}, u32[]{:S(2)}) collective-permute-start(bf16[4,256,256]{2,1,0:T(8,128)(2,1)S(1)} %all_to_all.20), channel_id=1, source_target_pairs={{0,520},{8,0},{512,8},{520,512},{1,521},{9,1},{513,9},{521,513},{2... | collective-permute-start | bytes 1572872 | tf_op jit(solution)/shard_map/ppermute | solution.py:13
  81.0 31.6 %collective-permute-start.9 = (bf16[4,256,256]{2,1,0:T(8,128)(2,1)S(1)}, bf16[4,256,256]{2,1,0:T(8,128)(2,1)S(1)}, u32[]{:S(2)}, u32[]{:S(2)}) collective-permute-start(bf16[4,256,256]{2,1,0:T(8,128)(2,1)S(1)} %all_to_all.20), channel_id=1, source_target_pairs={{0,512},{8,520},{512,0},{520,8},{1,513},{9,521},{513,1},{521,9},{2... | collective-permute-start | bytes 1572872 | tf_op jit(solution)/shard_map/ppermute | solution.py:13
  85.5 27.2 %collective-permute-start.8 = (bf16[4,256,256]{2,1,0:T(8,128)(2,1)S(1)}, bf16[4,256,256]{2,1,0:T(8,128)(2,1)S(1)}, u32[]{:S(2)}, u32[]{:S(2)}) collective-permute-start(bf16[4,256,256]{2,1,0:T(8,128)(2,1)S(1)} %all_to_all.20), channel_id=1, source_target_pairs={{0,8},{8,512},{512,520},{520,0},{1,9},{9,513},{513,521},{521,1},{2... | collective-permute-start | bytes 1572872 | tf_op jit(solution)/shard_map/ppermute | solution.py:13
  88.2 37.3 %all-to-all-start.2 = ((bf16[32,8,256]{2,1,0:T(8,128)(2,1)}), bf16[32,8,256]{2,1,0:T(8,128)(2,1)S(1)}, u32[]{:S(2)}, u32[]{:S(2)}) async-start(bf16[32,8,256]{2,1,0:T(8,128)(2,1)} %pad_maximum_fusion.3), calls=%async_computation.2 | async-start | bytes 262144 | tf_op jit(solution)/shard_map/all_to_all | solution.py:29
  113.4 2.2 %copy-start.1 = (bf16[512,4096]{1,0:T(8,128)(2,1)S(1)}, bf16[512,4096]{1,0:T(8,128)(2,1)}, u32[]{:S(2)}) copy-start(bf16[512,4096]{1,0:T(8,128)(2,1)} %copy-done) | copy-start | bytes 12582916
  116.9 8.5 %collective-permute-start.11 = (bf16[256,256]{1,0:T(8,128)(2,1)S(1)}, bf16[256,256]{1,0:T(8,128)(2,1)S(1)}, u32[]{:S(2)}, u32[]{:S(2)}) collective-permute-start(bf16[256,256]{1,0:T(8,128)(2,1)S(1)} %get-tuple-element.29), channel_id=1, source_target_pairs={{0,1},{1,0},{2,3},{3,2},{4,5},{5,4},{6,7},{7,6},{8,9},{9,8},{10,11... | collective-permute-start | bytes 393224 | tf_op jit(solution)/shard_map/ppermute | solution.py:93
  126.1 8.7 %all-to-all-start.3 = ((f32[8,8,256]{2,1,0:T(8,128)}), f32[8,8,256]{2,1,0:T(8,128)S(1)}, u32[]{:S(2)}, u32[]{:S(2)}) async-start(f32[8,8,256]{2,1,0:T(8,128)} %broadcast_in_dim.26), calls=%async_computation.3 | async-start | bytes 131072 | tf_op jit(solution)/shard_map/all_to_all | solution.py:98

commit v12 on v11

--- a/solution.py
+++ b/solution.py
@@ -79,9 +79,10 @@
 
     slab = jnp.broadcast_to(col.reshape(1, column, half), (4, column, half))
     slab = lax.all_to_all(slab, "y", split_axis=0, concat_axis=0, tiled=True)
+    plane = jnp.roll(plane, n_z // 2, axis=0)
     slab, plane = lax.optimization_barrier((slab, plane))
     held = [around(slab, X, shift) for shift in (2, 1, 3)]
-    moved = over_z(jnp.roll(plane, n_z // 2, axis=0), n_z // 2)
+    moved = over_z(plane, n_z // 2)
 
     two, one, three = held
     stack = jnp.stack([slab, one, two, three])

time: 137 us -> 137 us (level)
  blocking collectives: 10 us -> 0 us
  waiting for transfers between devices: 12 us -> 18.2 us
  starting transfers between devices: 97.3 us -> 101 us
    all_to_all x1 -> x0, blocking collectives: 10 us -> none  [body(): slab = lax.all_to_all(slab, 'y', split_axis=0, concat_axis=0, tiled=True)]
    all_to_all x0 -> x1, waiting for transfers between devices: none -> 6.21 us  [body(): slab = lax.all_to_all(slab, 'y', split_axis=0, concat_axis=0, tiled=True)]
    all_to_all x0 -> x1, starting transfers between devices: none -> 3.47 us  [body(): slab = lax.all_to_all(slab, 'y', split_axis=0, concat_axis=0, tiled=True)]
  transfers between devices with their start and end apart: 15 -> 16, of which waited for: 7 -> 8; matrix products, arithmetic and copies ran while one was open for 7% -> 7% of each run, Pallas kernels for 0% -> 0%
where the time goes in v12:
time: 137 us; the launch traced here: 136 us
  starting transfers between devices  101 us (74%)
  waiting for transfers between devices  18.2 us (13%)
  local copies, waits for them, and re-layouts  8.49 us (6%)
  other arithmetic  4.62 us (3%)
  matrix products  2.55 us (2%)
    all_to_all x2, starting transfers between devices, over_z(): lax.all_to_all(value, 'z', split_axis=0, concat_axis=0, axis_index_groups...  42.9 us
    ppermute x9, starting transfers between devices, around(): return lax.ppermute(value, axes, [(i, (i + shift) % 4) for i in range(4)])  24.6 us
    ppermute x1, starting transfers between devices, body(): other_act = lax.ppermute(activations, 'c', SWAP)  16.1 us
    ppermute x1, starting transfers between devices, body(): got = lax.ppermute(proj[tok:], 'c', SWAP)  7.83 us
    ppermute x9, waiting for transfers between devices, around(): return lax.ppermute(value, axes, [(i, (i + shift) % 4) for i in range(4)])  6.53 us
    all_to_all x1, waiting for transfers between devices, body(): slab = lax.all_to_all(slab, 'y', split_axis=0, concat_axis=0, tiled=True)  6.21 us
    unnamed x10, local copies, waits for them, and re-layouts  4.67 us
    all_to_all x1, waiting for transfers between devices, body(): lax.all_to_all(pieces, ('y', 'c'), split_axis=0, concat_axis=0, tiled=True)  4.12 us
  transfers between devices with their start and end apart: 16, of which 8 were waited for; matrix products, arithmetic and copies ran while one was open for 7% of the time, Pallas kernels for 0%

profile of v12, /device:TPU:1, one launch (start us, length us, event | category | flops | bytes accessed | tf_op | source)
XLA Modules:
  0.0 135.8 jit_solution(14266539710999001577)
XLA Ops:
  0.6 16.1 %collective-permute-start = (bf16[256,4096]{1,0:T(8,128)(2,1)}, bf16[256,4096]{1,0:T(8,128)(2,1)S(1)}, u32[]{:S(2)}, u32[]{:S(2)}) collective-permute-start(bf16[256,4096]{1,0:T(8,128)(2,1)} %param.4), channel_id=1, source_target_pairs={{0,1},{1,0},{2,3},{3,2},{4,5},{5,4},{6,7},{7,6},{8,9},{9,8},{10,11... | collective-permute-start | bytes 6291464 | tf_op jit(solution)/shard_map/ppermute | solution.py:51
  16.7 1.9 %collective-permute-start.1 = (bf16[256,512]{1,0:T(8,128)(2,1)}, bf16[256,512]{1,0:T(8,128)(2,1)S(1)}, u32[]{:S(2)}, u32[]{:S(2)}) collective-permute-start(bf16[256,512]{1,0:T(8,128)(2,1)} %param.7), channel_id=1, source_target_pairs={{0,1},{1,0},{2,3},{3,2},{4,5},{5,4},{6,7},{7,6},{8,9},{9,8},{10,11... | collective-permute-start | bytes 786440 | tf_op jit(solution)/shard_map/ppermute | solution.py:52
  18.8 1.7 %constant_dynamic-update-slice_fusion.1 = bf16[512,4096]{1,0:T(8,128)(2,1)S(1)} fusion(bf16[256,4096]{1,0:T(8,128)(2,1)} %param.4), kind=kLoop, calls=%fused_computation.31 | loop fusion | bytes 4194304
  21.5 1.3 fusion
  22.8 1.0 dynamic-slice_bitcast_fusion.2
  23.8 1.9 %collective-permute-start.4 = (bf16[32,4,8,256]{3,2,1,0:T(8,128)(2,1)}, bf16[32,4,8,256]{3,2,1,0:T(8,128)(2,1)}, u32[]{:S(2)}, u32[]{:S(2)}) collective-permute-start(bf16[32,4,8,256]{3,2,1,0:T(8,128)(2,1)} %get-tuple-element.21), channel_id=1, source_target_pairs={{0,520},{8,0},{512,8},{520,512},{1,521},{9,1},{513,9},{521,513},{2... | collective-permute-start | bytes 1572872 | tf_op jit(solution)/shard_map/ppermute | solution.py:13
  25.7 3.4 %collective-permute-start.3 = (bf16[32,4,8,256]{3,2,1,0:T(8,128)(2,1)S(1)}, bf16[32,4,8,256]{3,2,1,0:T(8,128)(2,1)}, u32[]{:S(2)}, u32[]{:S(2)}) collective-permute-start(bf16[32,4,8,256]{3,2,1,0:T(8,128)(2,1)S(1)} %get-tuple-element.22), channel_id=1, source_target_pairs={{0,8},{8,512},{512,520},{520,0},{1,9},{9,513},{513,521},{521,1},{2... | collective-permute-start | bytes 1572872 | tf_op jit(solution)/shard_map/ppermute | solution.py:13
  29.0 1.9 %collective-permute-start.2 = (bf16[32,4,8,256]{3,2,1,0:T(8,128)(2,1)S(1)}, bf16[32,4,8,256]{3,2,1,0:T(8,128)(2,1)}, u32[]{:S(2)}, u32[]{:S(2)}) collective-permute-start(bf16[32,4,8,256]{3,2,1,0:T(8,128)(2,1)S(1)} %get-tuple-element.20), channel_id=1, source_target_pairs={{0,512},{8,520},{512,0},{520,8},{1,513},{9,521},{513,1},{521,9},{2... | collective-permute-start | bytes 1572872 | tf_op jit(solution)/shard_map/ppermute | solution.py:13
  31.1 0.8 fusion.9
  32.5 18.8 %all-to-all-start = ((bf16[32,8,256]{2,1,0:T(8,128)(2,1)}), bf16[32,8,256]{2,1,0:T(8,128)(2,1)S(1)}, u32[]{:S(2)}, u32[]{:S(2)}) async-start(bf16[32,8,256]{2,1,0:T(8,128)(2,1)} %broadcast_in_dim.11), calls=%async_computation | async-start | bytes 262144 | tf_op jit(solution)/shard_map/all_to_all | solution.py:29
  51.4 1.7 %collective-permute-done.3 = bf16[32,4,8,256]{3,2,1,0:T(8,128)(2,1)} collective-permute-done((bf16[32,4,8,256]{3,2,1,0:T(8,128)(2,1)S(1)}, bf16[32,4,8,256]{3,2,1,0:T(8,128)(2,1)}, u32[]{:S(2)}, u32[]{:S(2)}) %collective-permute-start.3) | collective-permute-done | bytes 524320 | tf_op jit(solution)/shard_map/ppermute | solution.py:13
  53.1 1.7 %fusion.3 = bf16[32,4,8,256]{3,2,1,0:T(8,128)(2,1)S(1)} fusion(bf16[32,4,8,256]{3,2,1,0:T(8,128)(2,1)} %collective-permute-done.4, bf16[32,4,8,256]{3,2,1,0:T(8,128)(2,1)} %collective-permute-done.3, bf16[32,4,8,256]{3,2,1,0:T(8,128)(2,1)} %collective-permute-done.2, bf16[2,32,2,4,8,256]{5,4,3,2,1,0:T(8,128)(2,1)S(1)} %bitcast.43, s32[]{:T(128)S(6)} %select_n.150, ...), kind=kLoop, calls=%fused_computation.8 | loop fusion | flops 2097152 | bytes 2621448 | tf_op jit(solution)/shard_map/convert_element_type | solution.py:23
  54.9 2.9 %collective-permute-start.7 = (bf16[32,8,256]{2,1,0:T(8,128)(2,1)S(1)}, bf16[32,8,256]{2,1,0:T(8,128)(2,1)S(1)}, u32[]{:S(2)}, u32[]{:S(2)}) collective-permute-start(bf16[32,8,256]{2,1,0:T(8,128)(2,1)S(1)} %get-tuple-element.24), channel_id=1, source_target_pairs={{0,6},{2,0},{4,2},{6,4},{1,7},{3,1},{5,3},{7,5},{8,14},{10,8},{12,... | collective-permute-start | bytes 393224 | tf_op jit(solution)/shard_map/ppermute | solution.py:13
  57.9 2.3 %collective-permute-start.6 = (bf16[32,8,256]{2,1,0:T(8,128)(2,1)S(1)}, bf16[32,8,256]{2,1,0:T(8,128)(2,1)S(1)}, u32[]{:S(2)}, u32[]{:S(2)}) collective-permute-start(bf16[32,8,256]{2,1,0:T(8,128)(2,1)S(1)} %get-tuple-element.25), channel_id=1, source_target_pairs={{0,2},{2,4},{4,6},{6,0},{1,3},{3,5},{5,7},{7,1},{8,10},{10,12},{12... | collective-permute-start | bytes 393224 | tf_op jit(solution)/shard_map/ppermute | solution.py:13
  60.2 3.1 %collective-permute-start.5 = (bf16[32,8,256]{2,1,0:T(8,128)(2,1)S(1)}, bf16[32,8,256]{2,1,0:T(8,128)(2,1)S(1)}, u32[]{:S(2)}, u32[]{:S(2)}) collective-permute-start(bf16[32,8,256]{2,1,0:T(8,128)(2,1)S(1)} %get-tuple-element.23), channel_id=1, source_target_pairs={{0,4},{2,6},{4,0},{6,2},{1,5},{3,7},{5,1},{7,3},{8,12},{10,14},{12... | collective-permute-start | bytes 393224 | tf_op jit(solution)/shard_map/ppermute | solution.py:13
  63.3 1.7 %collective-permute-done.6 = bf16[32,8,256]{2,1,0:T(8,128)(2,1)S(1)} collective-permute-done((bf16[32,8,256]{2,1,0:T(8,128)(2,1)S(1)}, bf16[32,8,256]{2,1,0:T(8,128)(2,1)S(1)}, u32[]{:S(2)}, u32[]{:S(2)}) %collective-permute-start.6) | collective-permute-done | bytes 131104 | tf_op jit(solution)/shard_map/ppermute | solution.py:13
  65.1 3.1 %collective-permute-done.5 = bf16[32,8,256]{2,1,0:T(8,128)(2,1)S(1)} collective-permute-done((bf16[32,8,256]{2,1,0:T(8,128)(2,1)S(1)}, bf16[32,8,256]{2,1,0:T(8,128)(2,1)S(1)}, u32[]{:S(2)}, u32[]{:S(2)}) %collective-permute-start.5) | collective-permute-done | bytes 131104 | tf_op jit(solution)/shard_map/ppermute | solution.py:13
  68.3 0.8 broadcast_in_dim.25
  69.1 3.5 %all-to-all-start.1 = ((bf16[4,256,256]{2,1,0:T(8,128)(2,1)}), bf16[4,256,256]{2,1,0:T(8,128)(2,1)S(1)}, u32[]{:S(2)}, u32[]{:S(2)}) async-start(bf16[4,256,256]{2,1,0:T(8,128)(2,1)} %broadcast_in_dim.25), calls=%async_computation.1 | async-start | bytes 1048576 | tf_op jit(solution)/shard_map/all_to_all | solution.py:81
  72.6 0.7 pad_maximum_fusion.3
  73.3 6.2 %all-to-all-done.1 = bf16[4,256,256]{2,1,0:T(8,128)(2,1)S(1)} async-done(((bf16[4,256,256]{2,1,0:T(8,128)(2,1)}), bf16[4,256,256]{2,1,0:T(8,128)(2,1)S(1)}, u32[]{:S(2)}, u32[]{:S(2)}) %all-to-all-start.1) | async-done | bytes 524320 | tf_op jit(solution)/shard_map/all_to_all | solution.py:81
  79.5 2.7 %collective-permute-start.10 = (bf16[4,256,256]{2,1,0:T(8,128)(2,1)S(1)}, bf16[4,256,256]{2,1,0:T(8,128)(2,1)S(1)}, u32[]{:S(2)}, u32[]{:S(2)}) collective-permute-start(bf16[4,256,256]{2,1,0:T(8,128)(2,1)S(1)} %all-to-all-done.1), channel_id=1, source_target_pairs={{0,520},{8,0},{512,8},{520,512},{1,521},{9,1},{513,9},{521,513},{2... | collective-permute-start | bytes 1572872 | tf_op jit(solution)/shard_map/ppermute | solution.py:13
  82.2 4.4 %collective-permute-start.9 = (bf16[4,256,256]{2,1,0:T(8,128)(2,1)S(1)}, bf16[4,256,256]{2,1,0:T(8,128)(2,1)S(1)}, u32[]{:S(2)}, u32[]{:S(2)}) collective-permute-start(bf16[4,256,256]{2,1,0:T(8,128)(2,1)S(1)} %all-to-all-done.1), channel_id=1, source_target_pairs={{0,512},{8,520},{512,0},{520,8},{1,513},{9,521},{513,1},{521,9},{2... | collective-permute-start | bytes 1572872 | tf_op jit(solution)/shard_map/ppermute | solution.py:13
  86.6 1.9 %collective-permute-start.8 = (bf16[4,256,256]{2,1,0:T(8,128)(2,1)S(1)}, bf16[4,256,256]{2,1,0:T(8,128)(2,1)S(1)}, u32[]{:S(2)}, u32[]{:S(2)}) collective-permute-start(bf16[4,256,256]{2,1,0:T(8,128)(2,1)S(1)} %all-to-all-done.1), channel_id=1, source_target_pairs={{0,8},{8,512},{512,520},{520,0},{1,9},{9,513},{513,521},{521,1},{2... | collective-permute-start | bytes 1572872 | tf_op jit(solution)/shard_map/ppermute | solution.py:13
  88.6 24.1 %all-to-all-start.2 = ((bf16[32,8,256]{2,1,0:T(8,128)(2,1)}), bf16[32,8,256]{2,1,0:T(8,128)(2,1)S(1)}, u32[]{:S(2)}, u32[]{:S(2)}) async-start(bf16[32,8,256]{2,1,0:T(8,128)(2,1)} %pad_maximum_fusion.3), calls=%async_computation.2 | async-start | bytes 262144 | tf_op jit(solution)/shard_map/all_to_all | solution.py:29
  113.8 1.9 %copy-done.1 = bf16[512,4096]{1,0:T(8,128)(2,1)S(1)} copy-done((bf16[512,4096]{1,0:T(8,128)(2,1)S(1)}, bf16[512,4096]{1,0:T(8,128)(2,1)}, u32[]{:S(2)}) %copy-start.1) | copy-done | bytes 4194328
  115.7 1.2 convolution_convert_fusion
  116.9 7.8 %collective-permute-start.11 = (bf16[256,256]{1,0:T(8,128)(2,1)S(1)}, bf16[256,256]{1,0:T(8,128)(2,1)S(1)}, u32[]{:S(2)}, u32[]{:S(2)}) collective-permute-start(bf16[256,256]{1,0:T(8,128)(2,1)S(1)} %get-tuple-element.29), channel_id=1, source_target_pairs={{0,1},{1,0},{2,3},{3,2},{4,5},{5,4},{6,7},{7,6},{8,9},{9,8},{10,11... | collective-permute-start | bytes 393224 | tf_op jit(solution)/shard_map/ppermute | solution.py:94
  124.8 1.0 collective-permute-done.11
  126.4 3.9 %all-to-all-start.3 = ((f32[8,8,256]{2,1,0:T(8,128)}), f32[8,8,256]{2,1,0:T(8,128)S(1)}, u32[]{:S(2)}, u32[]{:S(2)}) async-start(f32[8,8,256]{2,1,0:T(8,128)} %broadcast_in_dim.26), calls=%async_computation.3 | async-start | bytes 131072 | tf_op jit(solution)/shard_map/all_to_all | solution.py:99
  130.3 0.7 pad_maximum_fusion.2
  131.0 4.1 %all-to-all-done.3 = f32[8,8,256]{2,1,0:T(8,128)S(1)} async-done(((f32[8,8,256]{2,1,0:T(8,128)}), f32[8,8,256]{2,1,0:T(8,128)S(1)}, u32[]{:S(2)}, u32[]{:S(2)}) %all-to-all-start.3) | async-done | bytes 65568 | tf_op jit(solution)/shard_map/all_to_all | solution.py:99
  (35 shorter events, 4.2 us)
Async XLA Ops:
  0.6 20.0 %collective-permute-start = (bf16[256,4096]{1,0:T(8,128)(2,1)}, bf16[256,4096]{1,0:T(8,128)(2,1)S(1)}, u32[]{:S(2)}, u32[]{:S(2)}) collective-permute-start(bf16[256,4096]{1,0:T(8,128)(2,1)} %param.4), channel_id=1, source_target_pairs={{0,1},{1,0},{2,3},{3,2},{4,5},{5,4},{6,7},{7,6},{8,9},{9,8},{10,11... | collective-permute-start | bytes 6291464 | tf_op jit(solution)/shard_map/ppermute | solution.py:51
  16.7 4.3 %collective-permute-start.1 = (bf16[256,512]{1,0:T(8,128)(2,1)}, bf16[256,512]{1,0:T(8,128)(2,1)S(1)}, u32[]{:S(2)}, u32[]{:S(2)}) collective-permute-start(bf16[256,512]{1,0:T(8,128)(2,1)} %param.7), channel_id=1, source_target_pairs={{0,1},{1,0},{2,3},{3,2},{4,5},{5,4},{6,7},{7,6},{8,9},{9,8},{10,11... | collective-permute-start | bytes 786440 | tf_op jit(solution)/shard_map/ppermute | solution.py:52
  20.5 1.0 copy-start.3
  20.8 2.0 %copy-start = (bf16[512,4096]{1,0:T(8,128)(2,1)}, bf16[512,4096]{1,0:T(8,128)(2,1)S(1)}, u32[]{:S(2)}) copy-start(bf16[512,4096]{1,0:T(8,128)(2,1)S(1)} %constant_dynamic-update-slice_fusion) | copy-start | bytes 12582916
  22.8 8.2 %copy-start.2 = (bf16[32,4]{0,1:T(4,128)(2,1)S(1)}, bf16[32,4]{0,1:T(4,128)(2,1)}, u32[]{:S(2)}) copy-start(bf16[32,4]{0,1:T(4,128)(2,1)} %param.6) | copy-start | bytes 772
  23.8 27.6 %collective-permute-start.4 = (bf16[32,4,8,256]{3,2,1,0:T(8,128)(2,1)}, bf16[32,4,8,256]{3,2,1,0:T(8,128)(2,1)}, u32[]{:S(2)}, u32[]{:S(2)}) collective-permute-start(bf16[32,4,8,256]{3,2,1,0:T(8,128)(2,1)} %get-tuple-element.21), channel_id=1, source_target_pairs={{0,520},{8,0},{512,8},{520,512},{1,521},{9,1},{513,9},{521,513},{2... | collective-permute-start | bytes 1572872 | tf_op jit(solution)/shard_map/ppermute | solution.py:13
  25.7 27.4 %collective-permute-start.3 = (bf16[32,4,8,256]{3,2,1,0:T(8,128)(2,1)S(1)}, bf16[32,4,8,256]{3,2,1,0:T(8,128)(2,1)}, u32[]{:S(2)}, u32[]{:S(2)}) collective-permute-start(bf16[32,4,8,256]{3,2,1,0:T(8,128)(2,1)S(1)} %get-tuple-element.22), channel_id=1, source_target_pairs={{0,8},{8,512},{512,520},{520,0},{1,9},{9,513},{513,521},{521,1},{2... | collective-permute-start | bytes 1572872 | tf_op jit(solution)/shard_map/ppermute | solution.py:13
  29.0 24.1 %collective-permute-start.2 = (bf16[32,4,8,256]{3,2,1,0:T(8,128)(2,1)S(1)}, bf16[32,4,8,256]{3,2,1,0:T(8,128)(2,1)}, u32[]{:S(2)}, u32[]{:S(2)}) collective-permute-start(bf16[32,4,8,256]{3,2,1,0:T(8,128)(2,1)S(1)} %get-tuple-element.20), channel_id=1, source_target_pairs={{0,512},{8,520},{512,0},{520,8},{1,513},{9,521},{513,1},{521,9},{2... | collective-permute-start | bytes 1572872 | tf_op jit(solution)/shard_map/ppermute | solution.py:13
  32.5 35.7 %all-to-all-start = ((bf16[32,8,256]{2,1,0:T(8,128)(2,1)}), bf16[32,8,256]{2,1,0:T(8,128)(2,1)S(1)}, u32[]{:S(2)}, u32[]{:S(2)}) async-start(bf16[32,8,256]{2,1,0:T(8,128)(2,1)} %broadcast_in_dim.11), calls=%async_computation | async-start | bytes 262144 | tf_op jit(solution)/shard_map/all_to_all | solution.py:29
  54.9 8.4 %collective-permute-start.7 = (bf16[32,8,256]{2,1,0:T(8,128)(2,1)S(1)}, bf16[32,8,256]{2,1,0:T(8,128)(2,1)S(1)}, u32[]{:S(2)}, u32[]{:S(2)}) collective-permute-start(bf16[32,8,256]{2,1,0:T(8,128)(2,1)S(1)} %get-tuple-element.24), channel_id=1, source_target_pairs={{0,6},{2,0},{4,2},{6,4},{1,7},{3,1},{5,3},{7,5},{8,14},{10,8},{12,... | collective-permute-start | bytes 393224 | tf_op jit(solution)/shard_map/ppermute | solution.py:13
  57.9 7.2 %collective-permute-start.6 = (bf16[32,8,256]{2,1,0:T(8,128)(2,1)S(1)}, bf16[32,8,256]{2,1,0:T(8,128)(2,1)S(1)}, u32[]{:S(2)}, u32[]{:S(2)}) collective-permute-start(bf16[32,8,256]{2,1,0:T(8,128)(2,1)S(1)} %get-tuple-element.25), channel_id=1, source_target_pairs={{0,2},{2,4},{4,6},{6,0},{1,3},{3,5},{5,7},{7,1},{8,10},{10,12},{12... | collective-permute-start | bytes 393224 | tf_op jit(solution)/shard_map/ppermute | solution.py:13
  60.2 7.9 %collective-permute-start.5 = (bf16[32,8,256]{2,1,0:T(8,128)(2,1)S(1)}, bf16[32,8,256]{2,1,0:T(8,128)(2,1)S(1)}, u32[]{:S(2)}, u32[]{:S(2)}) collective-permute-start(bf16[32,8,256]{2,1,0:T(8,128)(2,1)S(1)} %get-tuple-element.23), channel_id=1, source_target_pairs={{0,4},{2,6},{4,0},{6,2},{1,5},{3,7},{5,1},{7,3},{8,12},{10,14},{12... | collective-permute-start | bytes 393224 | tf_op jit(solution)/shard_map/ppermute | solution.py:13
  69.1 10.4 %all-to-all-start.1 = ((bf16[4,256,256]{2,1,0:T(8,128)(2,1)}), bf16[4,256,256]{2,1,0:T(8,128)(2,1)S(1)}, u32[]{:S(2)}, u32[]{:S(2)}) async-start(bf16[4,256,256]{2,1,0:T(8,128)(2,1)} %broadcast_in_dim.25), calls=%async_computation.1 | async-start | bytes 1048576 | tf_op jit(solution)/shard_map/all_to_all | solution.py:81
  79.5 33.2 %collective-permute-start.10 = (bf16[4,256,256]{2,1,0:T(8,128)(2,1)S(1)}, bf16[4,256,256]{2,1,0:T(8,128)(2,1)S(1)}, u32[]{:S(2)}, u32[]{:S(2)}) collective-permute-start(bf16[4,256,256]{2,1,0:T(8,128)(2,1)S(1)} %all-to-all-done.1), channel_id=1, source_target_pairs={{0,520},{8,0},{512,8},{520,512},{1,521},{9,1},{513,9},{521,513},{2... | collective-permute-start | bytes 1572872 | tf_op jit(solution)/shard_map/ppermute | solution.py:13
  82.2 30.5 %collective-permute-start.9 = (bf16[4,256,256]{2,1,0:T(8,128)(2,1)S(1)}, bf16[4,256,256]{2,1,0:T(8,128)(2,1)S(1)}, u32[]{:S(2)}, u32[]{:S(2)}) collective-permute-start(bf16[4,256,256]{2,1,0:T(8,128)(2,1)S(1)} %all-to-all-done.1), channel_id=1, source_target_pairs={{0,512},{8,520},{512,0},{520,8},{1,513},{9,521},{513,1},{521,9},{2... | collective-permute-start | bytes 1572872 | tf_op jit(solution)/shard_map/ppermute | solution.py:13
  86.6 26.2 %collective-permute-start.8 = (bf16[4,256,256]{2,1,0:T(8,128)(2,1)S(1)}, bf16[4,256,256]{2,1,0:T(8,128)(2,1)S(1)}, u32[]{:S(2)}, u32[]{:S(2)}) collective-permute-start(bf16[4,256,256]{2,1,0:T(8,128)(2,1)S(1)} %all-to-all-done.1), channel_id=1, source_target_pairs={{0,8},{8,512},{512,520},{520,0},{1,9},{9,513},{513,521},{521,1},{2... | collective-permute-start | bytes 1572872 | tf_op jit(solution)/shard_map/ppermute | solution.py:13
  88.6 37.2 %all-to-all-start.2 = ((bf16[32,8,256]{2,1,0:T(8,128)(2,1)}), bf16[32,8,256]{2,1,0:T(8,128)(2,1)S(1)}, u32[]{:S(2)}, u32[]{:S(2)}) async-start(bf16[32,8,256]{2,1,0:T(8,128)(2,1)} %pad_maximum_fusion.3), calls=%async_computation.2 | async-start | bytes 262144 | tf_op jit(solution)/shard_map/all_to_all | solution.py:29
  113.5 2.2 %copy-start.1 = (bf16[512,4096]{1,0:T(8,128)(2,1)S(1)}, bf16[512,4096]{1,0:T(8,128)(2,1)}, u32[]{:S(2)}) copy-start(bf16[512,4096]{1,0:T(8,128)(2,1)} %copy-done) | copy-start | bytes 12582916
  116.9 8.8 %collective-permute-start.11 = (bf16[256,256]{1,0:T(8,128)(2,1)S(1)}, bf16[256,256]{1,0:T(8,128)(2,1)S(1)}, u32[]{:S(2)}, u32[]{:S(2)}) collective-permute-start(bf16[256,256]{1,0:T(8,128)(2,1)S(1)} %get-tuple-element.29), channel_id=1, source_target_pairs={{0,1},{1,0},{2,3},{3,2},{4,5},{5,4},{6,7},{7,6},{8,9},{9,8},{10,11... | collective-permute-start | bytes 393224 | tf_op jit(solution)/shard_map/ppermute | solution.py:94
  126.4 8.7 %all-to-all-start.3 = ((f32[8,8,256]{2,1,0:T(8,128)}), f32[8,8,256]{2,1,0:T(8,128)S(1)}, u32[]{:S(2)}, u32[]{:S(2)}) async-start(f32[8,8,256]{2,1,0:T(8,128)} %broadcast_in_dim.26), calls=%async_computation.3 | async-start | bytes 131072 | tf_op jit(solution)/shard_map/all_to_all | solution.py:99

commit v13 on v11

--- a/solution.py
+++ b/solution.py
@@ -80,10 +80,10 @@
     slab = jnp.broadcast_to(col.reshape(1, column, half), (4, column, half))
     slab = lax.all_to_all(slab, "y", split_axis=0, concat_axis=0, tiled=True)
     slab, plane = lax.optimization_barrier((slab, plane))
-    held = [around(slab, X, shift) for shift in (2, 1, 3)]
+    held = [around(slab, X, shift) for shift in (1, 3, 2)]
     moved = over_z(jnp.roll(plane, n_z // 2, axis=0), n_z // 2)
 
-    two, one, three = held
+    one, three, two = held
     stack = jnp.stack([slab, one, two, three])
     whole = jnp.stack([pick(stack, (x - k) % 4) for k in range(4)])
     whole = whole.reshape(2, 2, 4, n_z, rows, half)

time: 137 us -> 137 us (level)
  no operation moved by 1% of the time
where the time goes in v13:
time: 137 us; the launch traced here: 135 us
  starting transfers between devices  97.3 us (71%)
  waiting for transfers between devices  12 us (9%)
  blocking collectives  10 us (7%)
  local copies, waits for them, and re-layouts  7.69 us (6%)
  other arithmetic  4.62 us (3%)
  matrix products  2.55 us (2%)
    all_to_all x2, starting transfers between devices, over_z(): lax.all_to_all(value, 'z', split_axis=0, concat_axis=0, axis_index_groups...  43.3 us
    ppermute x9, starting transfers between devices, around(): return lax.ppermute(value, axes, [(i, (i + shift) % 4) for i in range(4)])  24.6 us
    ppermute x1, starting transfers between devices, body(): other_act = lax.ppermute(activations, 'c', SWAP)  16.1 us
    all_to_all x1, blocking collectives, body(): slab = lax.all_to_all(slab, 'y', split_axis=0, concat_axis=0, tiled=True)  10 us
    ppermute x1, starting transfers between devices, body(): got = lax.ppermute(proj[tok:], 'c', SWAP)  7.57 us
    ppermute x9, waiting for transfers between devices, around(): return lax.ppermute(value, axes, [(i, (i + shift) % 4) for i in range(4)])  6.53 us
    unnamed x10, local copies, waits for them, and re-layouts  4.67 us
    all_to_all x1, waiting for transfers between devices, body(): lax.all_to_all(pieces, ('y', 'c'), split_axis=0, concat_axis=0, tiled=True)  4.12 us
  transfers between devices with their start and end apart: 15, of which 7 were waited for; matrix products, arithmetic and copies ran while one was open for 7% of the time, Pallas kernels for 0%

profile of v13, /device:TPU:1, one launch (start us, length us, event | category | flops | bytes accessed | tf_op | source)
XLA Modules:
  0.0 135.4 jit_solution(13321269684857635353)
XLA Ops:
  0.6 16.1 %collective-permute-start = (bf16[256,4096]{1,0:T(8,128)(2,1)}, bf16[256,4096]{1,0:T(8,128)(2,1)S(1)}, u32[]{:S(2)}, u32[]{:S(2)}) collective-permute-start(bf16[256,4096]{1,0:T(8,128)(2,1)} %param.4), channel_id=1, source_target_pairs={{0,1},{1,0},{2,3},{3,2},{4,5},{5,4},{6,7},{7,6},{8,9},{9,8},{10,11... | collective-permute-start | bytes 6291464 | tf_op jit(solution)/shard_map/ppermute | solution.py:51
  16.7 1.9 %collective-permute-start.1 = (bf16[256,512]{1,0:T(8,128)(2,1)}, bf16[256,512]{1,0:T(8,128)(2,1)S(1)}, u32[]{:S(2)}, u32[]{:S(2)}) collective-permute-start(bf16[256,512]{1,0:T(8,128)(2,1)} %param.7), channel_id=1, source_target_pairs={{0,1},{1,0},{2,3},{3,2},{4,5},{5,4},{6,7},{7,6},{8,9},{9,8},{10,11... | collective-permute-start | bytes 786440 | tf_op jit(solution)/shard_map/ppermute | solution.py:52
  18.8 1.7 %constant_dynamic-update-slice_fusion.1 = bf16[512,4096]{1,0:T(8,128)(2,1)S(1)} fusion(bf16[256,4096]{1,0:T(8,128)(2,1)} %param.4), kind=kLoop, calls=%fused_computation.31 | loop fusion | bytes 4194304
  21.5 1.3 fusion
  22.8 1.0 dynamic-slice_bitcast_fusion.2
  23.8 1.9 %collective-permute-start.4 = (bf16[32,4,8,256]{3,2,1,0:T(8,128)(2,1)}, bf16[32,4,8,256]{3,2,1,0:T(8,128)(2,1)}, u32[]{:S(2)}, u32[]{:S(2)}) collective-permute-start(bf16[32,4,8,256]{3,2,1,0:T(8,128)(2,1)} %get-tuple-element.21), channel_id=1, source_target_pairs={{0,520},{8,0},{512,8},{520,512},{1,521},{9,1},{513,9},{521,513},{2... | collective-permute-start | bytes 1572872 | tf_op jit(solution)/shard_map/ppermute | solution.py:13
  25.7 3.4 %collective-permute-start.3 = (bf16[32,4,8,256]{3,2,1,0:T(8,128)(2,1)S(1)}, bf16[32,4,8,256]{3,2,1,0:T(8,128)(2,1)}, u32[]{:S(2)}, u32[]{:S(2)}) collective-permute-start(bf16[32,4,8,256]{3,2,1,0:T(8,128)(2,1)S(1)} %get-tuple-element.22), channel_id=1, source_target_pairs={{0,8},{8,512},{512,520},{520,0},{1,9},{9,513},{513,521},{521,1},{2... | collective-permute-start | bytes 1572872 | tf_op jit(solution)/shard_map/ppermute | solution.py:13
  29.0 1.9 %collective-permute-start.2 = (bf16[32,4,8,256]{3,2,1,0:T(8,128)(2,1)S(1)}, bf16[32,4,8,256]{3,2,1,0:T(8,128)(2,1)}, u32[]{:S(2)}, u32[]{:S(2)}) collective-permute-start(bf16[32,4,8,256]{3,2,1,0:T(8,128)(2,1)S(1)} %get-tuple-element.20), channel_id=1, source_target_pairs={{0,512},{8,520},{512,0},{520,8},{1,513},{9,521},{513,1},{521,9},{2... | collective-permute-start | bytes 1572872 | tf_op jit(solution)/shard_map/ppermute | solution.py:13
  31.1 0.8 fusion.9
  31.8 0.7 broadcast_in_dim.11
  32.5 18.8 %all-to-all-start = ((bf16[32,8,256]{2,1,0:T(8,128)(2,1)}), bf16[32,8,256]{2,1,0:T(8,128)(2,1)S(1)}, u32[]{:S(2)}, u32[]{:S(2)}) async-start(bf16[32,8,256]{2,1,0:T(8,128)(2,1)} %broadcast_in_dim.11), calls=%async_computation | async-start | bytes 262144 | tf_op jit(solution)/shard_map/all_to_all | solution.py:29
  51.4 1.7 %collective-permute-done.3 = bf16[32,4,8,256]{3,2,1,0:T(8,128)(2,1)} collective-permute-done((bf16[32,4,8,256]{3,2,1,0:T(8,128)(2,1)S(1)}, bf16[32,4,8,256]{3,2,1,0:T(8,128)(2,1)}, u32[]{:S(2)}, u32[]{:S(2)}) %collective-permute-start.3) | collective-permute-done | bytes 524320 | tf_op jit(solution)/shard_map/ppermute | solution.py:13
  53.1 1.7 %fusion.3 = bf16[32,4,8,256]{3,2,1,0:T(8,128)(2,1)S(1)} fusion(bf16[32,4,8,256]{3,2,1,0:T(8,128)(2,1)} %collective-permute-done.4, bf16[32,4,8,256]{3,2,1,0:T(8,128)(2,1)} %collective-permute-done.3, bf16[32,4,8,256]{3,2,1,0:T(8,128)(2,1)} %collective-permute-done.2, bf16[2,32,2,4,8,256]{5,4,3,2,1,0:T(8,128)(2,1)S(1)} %bitcast.43, s32[]{:T(128)S(6)} %select_n.150, ...), kind=kLoop, calls=%fused_computation.8 | loop fusion | flops 2097152 | bytes 2621448 | tf_op jit(solution)/shard_map/convert_element_type | solution.py:23
  54.9 2.9 %collective-permute-start.7 = (bf16[32,8,256]{2,1,0:T(8,128)(2,1)S(1)}, bf16[32,8,256]{2,1,0:T(8,128)(2,1)S(1)}, u32[]{:S(2)}, u32[]{:S(2)}) collective-permute-start(bf16[32,8,256]{2,1,0:T(8,128)(2,1)S(1)} %get-tuple-element.24), channel_id=1, source_target_pairs={{0,6},{2,0},{4,2},{6,4},{1,7},{3,1},{5,3},{7,5},{8,14},{10,8},{12,... | collective-permute-start | bytes 393224 | tf_op jit(solution)/shard_map/ppermute | solution.py:13
  57.9 2.3 %collective-permute-start.6 = (bf16[32,8,256]{2,1,0:T(8,128)(2,1)S(1)}, bf16[32,8,256]{2,1,0:T(8,128)(2,1)S(1)}, u32[]{:S(2)}, u32[]{:S(2)}) collective-permute-start(bf16[32,8,256]{2,1,0:T(8,128)(2,1)S(1)} %get-tuple-element.25), channel_id=1, source_target_pairs={{0,2},{2,4},{4,6},{6,0},{1,3},{3,5},{5,7},{7,1},{8,10},{10,12},{12... | collective-permute-start | bytes 393224 | tf_op jit(solution)/shard_map/ppermute | solution.py:13
  60.2 3.1 %collective-permute-start.5 = (bf16[32,8,256]{2,1,0:T(8,128)(2,1)S(1)}, bf16[32,8,256]{2,1,0:T(8,128)(2,1)S(1)}, u32[]{:S(2)}, u32[]{:S(2)}) collective-permute-start(bf16[32,8,256]{2,1,0:T(8,128)(2,1)S(1)} %get-tuple-element.23), channel_id=1, source_target_pairs={{0,4},{2,6},{4,0},{6,2},{1,5},{3,7},{5,1},{7,3},{8,12},{10,14},{12... | collective-permute-start | bytes 393224 | tf_op jit(solution)/shard_map/ppermute | solution.py:13
  63.3 1.7 %collective-permute-done.6 = bf16[32,8,256]{2,1,0:T(8,128)(2,1)S(1)} collective-permute-done((bf16[32,8,256]{2,1,0:T(8,128)(2,1)S(1)}, bf16[32,8,256]{2,1,0:T(8,128)(2,1)S(1)}, u32[]{:S(2)}, u32[]{:S(2)}) %collective-permute-start.6) | collective-permute-done | bytes 131104 | tf_op jit(solution)/shard_map/ppermute | solution.py:13
  65.1 3.1 %collective-permute-done.5 = bf16[32,8,256]{2,1,0:T(8,128)(2,1)S(1)} collective-permute-done((bf16[32,8,256]{2,1,0:T(8,128)(2,1)S(1)}, bf16[32,8,256]{2,1,0:T(8,128)(2,1)S(1)}, u32[]{:S(2)}, u32[]{:S(2)}) %collective-permute-start.5) | collective-permute-done | bytes 131104 | tf_op jit(solution)/shard_map/ppermute | solution.py:13
  68.3 10.0 %all_to_all.20 = bf16[4,256,256]{2,1,0:T(8,128)(2,1)S(1)} all-to-all(bf16[4,256,256]{2,1,0:T(8,128)(2,1)S(1)} %broadcast_in_dim.25), channel_id=1, replica_groups=mesh['xh'=2,'z'=32,'xl'=2,'y'=4,'c'=2] {'y'}, dimensions={0} | all-to-all | bytes 1048576 | tf_op jit(solution)/shard_map/all_to_all | solution.py:81
  78.3 2.7 %collective-permute-start.10 = (bf16[4,256,256]{2,1,0:T(8,128)(2,1)S(1)}, bf16[4,256,256]{2,1,0:T(8,128)(2,1)S(1)}, u32[]{:S(2)}, u32[]{:S(2)}) collective-permute-start(bf16[4,256,256]{2,1,0:T(8,128)(2,1)S(1)} %all_to_all.20), channel_id=1, source_target_pairs={{0,520},{8,0},{512,8},{520,512},{1,521},{9,1},{513,9},{521,513},{2... | collective-permute-start | bytes 1572872 | tf_op jit(solution)/shard_map/ppermute | solution.py:13
  81.0 4.5 %collective-permute-start.9 = (bf16[4,256,256]{2,1,0:T(8,128)(2,1)S(1)}, bf16[4,256,256]{2,1,0:T(8,128)(2,1)S(1)}, u32[]{:S(2)}, u32[]{:S(2)}) collective-permute-start(bf16[4,256,256]{2,1,0:T(8,128)(2,1)S(1)} %all_to_all.20), channel_id=1, source_target_pairs={{0,512},{8,520},{512,0},{520,8},{1,513},{9,521},{513,1},{521,9},{2... | collective-permute-start | bytes 1572872 | tf_op jit(solution)/shard_map/ppermute | solution.py:13
  85.5 1.9 %collective-permute-start.8 = (bf16[4,256,256]{2,1,0:T(8,128)(2,1)S(1)}, bf16[4,256,256]{2,1,0:T(8,128)(2,1)S(1)}, u32[]{:S(2)}, u32[]{:S(2)}) collective-permute-start(bf16[4,256,256]{2,1,0:T(8,128)(2,1)S(1)} %all_to_all.20), channel_id=1, source_target_pairs={{0,8},{8,512},{512,520},{520,0},{1,9},{9,513},{513,521},{521,1},{2... | collective-permute-start | bytes 1572872 | tf_op jit(solution)/shard_map/ppermute | solution.py:13
  87.5 0.7 pad_maximum_fusion.3
  88.2 24.5 %all-to-all-start.2 = ((bf16[32,8,256]{2,1,0:T(8,128)(2,1)}), bf16[32,8,256]{2,1,0:T(8,128)(2,1)S(1)}, u32[]{:S(2)}, u32[]{:S(2)}) async-start(bf16[32,8,256]{2,1,0:T(8,128)(2,1)} %pad_maximum_fusion.3), calls=%async_computation.2 | async-start | bytes 262144 | tf_op jit(solution)/shard_map/all_to_all | solution.py:29
  113.7 1.9 %copy-done.1 = bf16[512,4096]{1,0:T(8,128)(2,1)S(1)} copy-done((bf16[512,4096]{1,0:T(8,128)(2,1)S(1)}, bf16[512,4096]{1,0:T(8,128)(2,1)}, u32[]{:S(2)}) %copy-start.1) | copy-done | bytes 4194328
  115.6 1.2 convolution_convert_fusion
  116.9 7.6 %collective-permute-start.11 = (bf16[256,256]{1,0:T(8,128)(2,1)S(1)}, bf16[256,256]{1,0:T(8,128)(2,1)S(1)}, u32[]{:S(2)}, u32[]{:S(2)}) collective-permute-start(bf16[256,256]{1,0:T(8,128)(2,1)S(1)} %get-tuple-element.29), channel_id=1, source_target_pairs={{0,1},{1,0},{2,3},{3,2},{4,5},{5,4},{6,7},{7,6},{8,9},{9,8},{10,11... | collective-permute-start | bytes 393224 | tf_op jit(solution)/shard_map/ppermute | solution.py:93
  124.5 1.0 collective-permute-done.11
  125.5 0.6 broadcast_in_dim.26
  126.1 3.8 %all-to-all-start.3 = ((f32[8,8,256]{2,1,0:T(8,128)}), f32[8,8,256]{2,1,0:T(8,128)S(1)}, u32[]{:S(2)}, u32[]{:S(2)}) async-start(f32[8,8,256]{2,1,0:T(8,128)} %broadcast_in_dim.26), calls=%async_computation.3 | async-start | bytes 131072 | tf_op jit(solution)/shard_map/all_to_all | solution.py:98
  130.0 0.7 pad_maximum_fusion.2
  130.7 4.1 %all-to-all-done.3 = f32[8,8,256]{2,1,0:T(8,128)S(1)} async-done(((f32[8,8,256]{2,1,0:T(8,128)}), f32[8,8,256]{2,1,0:T(8,128)S(1)}, u32[]{:S(2)}, u32[]{:S(2)}) %all-to-all-start.3) | async-done | bytes 65568 | tf_op jit(solution)/shard_map/all_to_all | solution.py:98
  (34 shorter events, 3.0 us)
Async XLA Ops:
  0.6 20.0 %collective-permute-start = (bf16[256,4096]{1,0:T(8,128)(2,1)}, bf16[256,4096]{1,0:T(8,128)(2,1)S(1)}, u32[]{:S(2)}, u32[]{:S(2)}) collective-permute-start(bf16[256,4096]{1,0:T(8,128)(2,1)} %param.4), channel_id=1, source_target_pairs={{0,1},{1,0},{2,3},{3,2},{4,5},{5,4},{6,7},{7,6},{8,9},{9,8},{10,11... | collective-permute-start | bytes 6291464 | tf_op jit(solution)/shard_map/ppermute | solution.py:51
  16.7 4.3 %collective-permute-start.1 = (bf16[256,512]{1,0:T(8,128)(2,1)}, bf16[256,512]{1,0:T(8,128)(2,1)S(1)}, u32[]{:S(2)}, u32[]{:S(2)}) collective-permute-start(bf16[256,512]{1,0:T(8,128)(2,1)} %param.7), channel_id=1, source_target_pairs={{0,1},{1,0},{2,3},{3,2},{4,5},{5,4},{6,7},{7,6},{8,9},{9,8},{10,11... | collective-permute-start | bytes 786440 | tf_op jit(solution)/shard_map/ppermute | solution.py:52
  20.5 1.0 copy-start.3
  20.8 2.0 %copy-start = (bf16[512,4096]{1,0:T(8,128)(2,1)}, bf16[512,4096]{1,0:T(8,128)(2,1)S(1)}, u32[]{:S(2)}) copy-start(bf16[512,4096]{1,0:T(8,128)(2,1)S(1)} %constant_dynamic-update-slice_fusion) | copy-start | bytes 12582916
  22.8 8.2 %copy-start.2 = (bf16[32,4]{0,1:T(4,128)(2,1)S(1)}, bf16[32,4]{0,1:T(4,128)(2,1)}, u32[]{:S(2)}) copy-start(bf16[32,4]{0,1:T(4,128)(2,1)} %param.6) | copy-start | bytes 772
  23.8 27.6 %collective-permute-start.4 = (bf16[32,4,8,256]{3,2,1,0:T(8,128)(2,1)}, bf16[32,4,8,256]{3,2,1,0:T(8,128)(2,1)}, u32[]{:S(2)}, u32[]{:S(2)}) collective-permute-start(bf16[32,4,8,256]{3,2,1,0:T(8,128)(2,1)} %get-tuple-element.21), channel_id=1, source_target_pairs={{0,520},{8,0},{512,8},{520,512},{1,521},{9,1},{513,9},{521,513},{2... | collective-permute-start | bytes 1572872 | tf_op jit(solution)/shard_map/ppermute | solution.py:13
  25.7 27.4 %collective-permute-start.3 = (bf16[32,4,8,256]{3,2,1,0:T(8,128)(2,1)S(1)}, bf16[32,4,8,256]{3,2,1,0:T(8,128)(2,1)}, u32[]{:S(2)}, u32[]{:S(2)}) collective-permute-start(bf16[32,4,8,256]{3,2,1,0:T(8,128)(2,1)S(1)} %get-tuple-element.22), channel_id=1, source_target_pairs={{0,8},{8,512},{512,520},{520,0},{1,9},{9,513},{513,521},{521,1},{2... | collective-permute-start | bytes 1572872 | tf_op jit(solution)/shard_map/ppermute | solution.py:13
  29.0 24.1 %collective-permute-start.2 = (bf16[32,4,8,256]{3,2,1,0:T(8,128)(2,1)S(1)}, bf16[32,4,8,256]{3,2,1,0:T(8,128)(2,1)}, u32[]{:S(2)}, u32[]{:S(2)}) collective-permute-start(bf16[32,4,8,256]{3,2,1,0:T(8,128)(2,1)S(1)} %get-tuple-element.20), channel_id=1, source_target_pairs={{0,512},{8,520},{512,0},{520,8},{1,513},{9,521},{513,1},{521,9},{2... | collective-permute-start | bytes 1572872 | tf_op jit(solution)/shard_map/ppermute | solution.py:13
  32.5 35.7 %all-to-all-start = ((bf16[32,8,256]{2,1,0:T(8,128)(2,1)}), bf16[32,8,256]{2,1,0:T(8,128)(2,1)S(1)}, u32[]{:S(2)}, u32[]{:S(2)}) async-start(bf16[32,8,256]{2,1,0:T(8,128)(2,1)} %broadcast_in_dim.11), calls=%async_computation | async-start | bytes 262144 | tf_op jit(solution)/shard_map/all_to_all | solution.py:29
  54.9 8.4 %collective-permute-start.7 = (bf16[32,8,256]{2,1,0:T(8,128)(2,1)S(1)}, bf16[32,8,256]{2,1,0:T(8,128)(2,1)S(1)}, u32[]{:S(2)}, u32[]{:S(2)}) collective-permute-start(bf16[32,8,256]{2,1,0:T(8,128)(2,1)S(1)} %get-tuple-element.24), channel_id=1, source_target_pairs={{0,6},{2,0},{4,2},{6,4},{1,7},{3,1},{5,3},{7,5},{8,14},{10,8},{12,... | collective-permute-start | bytes 393224 | tf_op jit(solution)/shard_map/ppermute | solution.py:13
  57.9 7.2 %collective-permute-start.6 = (bf16[32,8,256]{2,1,0:T(8,128)(2,1)S(1)}, bf16[32,8,256]{2,1,0:T(8,128)(2,1)S(1)}, u32[]{:S(2)}, u32[]{:S(2)}) collective-permute-start(bf16[32,8,256]{2,1,0:T(8,128)(2,1)S(1)} %get-tuple-element.25), channel_id=1, source_target_pairs={{0,2},{2,4},{4,6},{6,0},{1,3},{3,5},{5,7},{7,1},{8,10},{10,12},{12... | collective-permute-start | bytes 393224 | tf_op jit(solution)/shard_map/ppermute | solution.py:13
  60.2 7.9 %collective-permute-start.5 = (bf16[32,8,256]{2,1,0:T(8,128)(2,1)S(1)}, bf16[32,8,256]{2,1,0:T(8,128)(2,1)S(1)}, u32[]{:S(2)}, u32[]{:S(2)}) collective-permute-start(bf16[32,8,256]{2,1,0:T(8,128)(2,1)S(1)} %get-tuple-element.23), channel_id=1, source_target_pairs={{0,4},{2,6},{4,0},{6,2},{1,5},{3,7},{5,1},{7,3},{8,12},{10,14},{12... | collective-permute-start | bytes 393224 | tf_op jit(solution)/shard_map/ppermute | solution.py:13
  78.3 34.3 %collective-permute-start.10 = (bf16[4,256,256]{2,1,0:T(8,128)(2,1)S(1)}, bf16[4,256,256]{2,1,0:T(8,128)(2,1)S(1)}, u32[]{:S(2)}, u32[]{:S(2)}) collective-permute-start(bf16[4,256,256]{2,1,0:T(8,128)(2,1)S(1)} %all_to_all.20), channel_id=1, source_target_pairs={{0,520},{8,0},{512,8},{520,512},{1,521},{9,1},{513,9},{521,513},{2... | collective-permute-start | bytes 1572872 | tf_op jit(solution)/shard_map/ppermute | solution.py:13
  81.0 31.6 %collective-permute-start.9 = (bf16[4,256,256]{2,1,0:T(8,128)(2,1)S(1)}, bf16[4,256,256]{2,1,0:T(8,128)(2,1)S(1)}, u32[]{:S(2)}, u32[]{:S(2)}) collective-permute-start(bf16[4,256,256]{2,1,0:T(8,128)(2,1)S(1)} %all_to_all.20), channel_id=1, source_target_pairs={{0,512},{8,520},{512,0},{520,8},{1,513},{9,521},{513,1},{521,9},{2... | collective-permute-start | bytes 1572872 | tf_op jit(solution)/shard_map/ppermute | solution.py:13
  85.5 27.2 %collective-permute-start.8 = (bf16[4,256,256]{2,1,0:T(8,128)(2,1)S(1)}, bf16[4,256,256]{2,1,0:T(8,128)(2,1)S(1)}, u32[]{:S(2)}, u32[]{:S(2)}) collective-permute-start(bf16[4,256,256]{2,1,0:T(8,128)(2,1)S(1)} %all_to_all.20), channel_id=1, source_target_pairs={{0,8},{8,512},{512,520},{520,0},{1,9},{9,513},{513,521},{521,1},{2... | collective-permute-start | bytes 1572872 | tf_op jit(solution)/shard_map/ppermute | solution.py:13
  88.2 37.3 %all-to-all-start.2 = ((bf16[32,8,256]{2,1,0:T(8,128)(2,1)}), bf16[32,8,256]{2,1,0:T(8,128)(2,1)S(1)}, u32[]{:S(2)}, u32[]{:S(2)}) async-start(bf16[32,8,256]{2,1,0:T(8,128)(2,1)} %pad_maximum_fusion.3), calls=%async_computation.2 | async-start | bytes 262144 | tf_op jit(solution)/shard_map/all_to_all | solution.py:29
  113.4 2.2 %copy-start.1 = (bf16[512,4096]{1,0:T(8,128)(2,1)S(1)}, bf16[512,4096]{1,0:T(8,128)(2,1)}, u32[]{:S(2)}) copy-start(bf16[512,4096]{1,0:T(8,128)(2,1)} %copy-done) | copy-start | bytes 12582916
  116.9 8.5 %collective-permute-start.11 = (bf16[256,256]{1,0:T(8,128)(2,1)S(1)}, bf16[256,256]{1,0:T(8,128)(2,1)S(1)}, u32[]{:S(2)}, u32[]{:S(2)}) collective-permute-start(bf16[256,256]{1,0:T(8,128)(2,1)S(1)} %get-tuple-element.29), channel_id=1, source_target_pairs={{0,1},{1,0},{2,3},{3,2},{4,5},{5,4},{6,7},{7,6},{8,9},{9,8},{10,11... | collective-permute-start | bytes 393224 | tf_op jit(solution)/shard_map/ppermute | solution.py:93
  126.1 8.7 %all-to-all-start.3 = ((f32[8,8,256]{2,1,0:T(8,128)}), f32[8,8,256]{2,1,0:T(8,128)S(1)}, u32[]{:S(2)}, u32[]{:S(2)}) async-start(f32[8,8,256]{2,1,0:T(8,128)} %broadcast_in_dim.26), calls=%async_computation.3 | async-start | bytes 131072 | tf_op jit(solution)/shard_map/all_to_all | solution.py:98
